TPU v7x, 512 devices: a whole 4x4x16 slice. The times are simulated.
512 devices in a mesh: row: 16 (over y, z_lo), col: 32 (over x, z_hi, core).
Axes of the slice: x: 4, y: 4, z: 16 (z_hi: 4, z_lo: 4; z = z_hi * 4 + z_lo), core: 2. Of those that a mesh axis runs over, the one named last changes fastest.
Arguments:
- gradient: float32 [5120, 25600], P('row', 'col'), may hold values from -48 to 48
- previous: float32 [5120, 2880], P('row', 'col'), may hold values from -1 to 1
- root: bfloat16 [5120, 2880], P('row', 'col'), may hold values from -2.1 to 2.1
Outputs:
- statistic: float32 [5120, 2880], P('row', 'col')
- preconditioned: float32 [5120, 25600], P('row', 'col')
All inputs are finite; a program needn't handle non-finite values.
Results may differ from a plain program's by a relative error of at most 0.005.
Values may be sent and summed in bfloat16 or wider, within the bound.
No kernel may reach another device: no remote copies, remote signals or barrier semaphores. Data moves between devices by JAX's collectives and lax.ppermute only.
A program may use at most 64 MiB of HBM per device.

v0:
```python
import jax
import jax.numpy as jnp
from jax import lax
from jax.sharding import Mesh
from jax.sharding import PartitionSpec as P

INTER = 25600
COL = ("col_0", "col_1", "col_2")


def passed_along(x, axis, by):
    count = lax.axis_size(axis)
    return lax.ppermute(x, axis, [(i, (i + by) % count) for i in range(count)])


def in_blocks(x, dim, count):
    shape = x.shape
    blocks = x.reshape(*shape[:dim], count, shape[dim] // count, *shape[dim + 1 :])
    return jnp.moveaxis(blocks, dim, 0)


def summed_rows(x, chips, core, dim):
    sizes = (lax.axis_size(chips), lax.axis_size(core))
    blocks = in_blocks(x, dim, sizes[0] * sizes[1])
    inside = blocks.shape[1:]
    blocks = blocks.reshape(*sizes, *inside).swapaxes(0, 1).reshape(-1, *inside)
    blocks = lax.psum_scatter(blocks, core, scatter_dimension=0, tiled=True)
    return lax.psum_scatter(blocks, chips, scatter_dimension=0, tiled=True)[0]


def contract_rows(left, right):
    return lax.dot_general(
        left, right, (((0,), (0,)), ((), ())), preferred_element_type=jnp.float32
    )


def contract_cols(left, right):
    return lax.dot_general(
        left, right, (((1,), (1,)), ((), ())), preferred_element_type=jnp.float32
    )


def local(gradient, previous, root):
    block_rows = gradient.shape[0]
    half_cycle = lax.axis_size("row") // 2
    own_rows = gradient.astype(jnp.bfloat16)
    full_band = lax.all_gather(root, COL, axis=1, tiled=True)

    def own_tile(offset):
        return full_band[:, offset * block_rows : (offset + 1) * block_rows]

    gram_tiles = []
    moving = own_rows
    applied = jnp.zeros(own_rows.shape, jnp.float32)
    for offset in range(half_cycle + 1):
        if offset > 0:
            moving = passed_along(moving, "row", 1)
        gram_tiles.append(contract_cols(own_rows, moving))
        applied = applied + jnp.dot(own_tile(offset), moving, preferred_element_type=jnp.float32)
    for offset in range(1, half_cycle):
        partial_term = contract_rows(own_tile(offset), own_rows)
        applied = applied + passed_along(partial_term.astype(jnp.bfloat16), "row", -offset).astype(
            partial_term.dtype
        )
    gram_band = jnp.concatenate(gram_tiles, axis=1)
    own_share = summed_rows(gram_band.astype(jnp.bfloat16), ("col_0", "col_1"), "col_2", 1).astype(
        jnp.float32
    )
    statistic = 0.9 * previous + 0.1 / INTER * own_share
    return (statistic, applied)


def solution(mesh):
    split = Mesh(
        mesh.devices.reshape(mesh.shape["row"], 4, 4, 2), ("row", "col_0", "col_1", "col_2")
    )
    in_specs = (P("row", COL), P("row", COL), P("row", COL))
    out_specs = (P("row", COL), P("row", COL))
    return jax.shard_map(local, mesh=split, in_specs=in_specs, out_specs=out_specs, check_vma=False)
```

profile of v0, /device:TPU:24, one launch (start us, length us, event | category | flops | bytes accessed | tf_op | source)
XLA Modules:
  0.0 396.9 jit_solution(1645381719371357516)
XLA Ops:
  8.0 1.3 convert_element_type.54
  9.4 3.8 collective-permute-start
  13.2 15.8 %collective-permute-done = bf16[320,800]{1,0:T(8,128)(2,1)S(1)} collective-permute-done((bf16[320,800]{1,0:T(8,128)(2,1)S(1)}, bf16[320,800]{1,0:T(8,128)(2,1)S(1)}, u32[]{:S(2)}, u32[]{:S(2)}) %collective-permute-start) | collective-permute-done | bytes 512032 | tf_op jit(solution)/shard_map/ppermute | solution.py:13
  29.1 1.9 collective-permute-start.1
  31.0 16.8 %collective-permute-done.1 = bf16[320,800]{1,0:T(8,128)(2,1)S(1)} collective-permute-done((bf16[320,800]{1,0:T(8,128)(2,1)S(1)}, bf16[320,800]{1,0:T(8,128)(2,1)S(1)}, u32[]{:S(2)}, u32[]{:S(2)}) %collective-permute-start.1) | collective-permute-done | bytes 512032 | tf_op jit(solution)/shard_map/ppermute | solution.py:13
  47.8 1.9 collective-permute-start.2
  49.7 17.2 %collective-permute-done.2 = bf16[320,800]{1,0:T(8,128)(2,1)S(1)} collective-permute-done((bf16[320,800]{1,0:T(8,128)(2,1)S(1)}, bf16[320,800]{1,0:T(8,128)(2,1)S(1)}, u32[]{:S(2)}, u32[]{:S(2)}) %collective-permute-start.2) | collective-permute-done | bytes 512032 | tf_op jit(solution)/shard_map/ppermute | solution.py:13
  66.9 1.9 collective-permute-start.3
  68.8 17.2 %collective-permute-done.3 = bf16[320,800]{1,0:T(8,128)(2,1)S(1)} collective-permute-done((bf16[320,800]{1,0:T(8,128)(2,1)S(1)}, bf16[320,800]{1,0:T(8,128)(2,1)S(1)}, u32[]{:S(2)}, u32[]{:S(2)}) %collective-permute-start.3) | collective-permute-done | bytes 512032 | tf_op jit(solution)/shard_map/ppermute | solution.py:13
  86.0 1.9 collective-permute-start.4
  87.9 0.5 convolution_convert_fusion.15
  88.4 0.5 convolution_convert_fusion.14
  88.9 13.5 %collective-permute-done.4 = bf16[320,800]{1,0:T(8,128)(2,1)S(1)} collective-permute-done((bf16[320,800]{1,0:T(8,128)(2,1)S(1)}, bf16[320,800]{1,0:T(8,128)(2,1)S(1)}, u32[]{:S(2)}, u32[]{:S(2)}) %collective-permute-start.4) | collective-permute-done | bytes 512032 | tf_op jit(solution)/shard_map/ppermute | solution.py:13
  102.4 1.9 collective-permute-start.5
  104.4 0.5 convolution_convert_fusion.13
  104.9 0.5 convolution_convert_fusion.12
  105.4 27.2 %collective-permute-done.5 = bf16[320,800]{1,0:T(8,128)(2,1)S(1)} collective-permute-done((bf16[320,800]{1,0:T(8,128)(2,1)S(1)}, bf16[320,800]{1,0:T(8,128)(2,1)S(1)}, u32[]{:S(2)}, u32[]{:S(2)}) %collective-permute-start.5) | collective-permute-done | bytes 512032 | tf_op jit(solution)/shard_map/ppermute | solution.py:13
  132.6 1.9 collective-permute-start.6
  134.5 0.5 convolution_convert_fusion.11
  135.0 0.5 convolution_convert_fusion.10
  135.5 16.1 %collective-permute-done.6 = bf16[320,800]{1,0:T(8,128)(2,1)S(1)} collective-permute-done((bf16[320,800]{1,0:T(8,128)(2,1)S(1)}, bf16[320,800]{1,0:T(8,128)(2,1)S(1)}, u32[]{:S(2)}, u32[]{:S(2)}) %collective-permute-start.6) | collective-permute-done | bytes 512032 | tf_op jit(solution)/shard_map/ppermute | solution.py:13
  151.6 1.9 collective-permute-start.7
  153.5 0.5 convolution_convert_fusion.9
  154.0 0.5 convolution_convert_fusion.8
  154.5 14.6 %collective-permute-done.7 = bf16[320,800]{1,0:T(8,128)(2,1)S(1)} collective-permute-done((bf16[320,800]{1,0:T(8,128)(2,1)S(1)}, bf16[320,800]{1,0:T(8,128)(2,1)S(1)}, u32[]{:S(2)}, u32[]{:S(2)}) %collective-permute-start.7) | collective-permute-done | bytes 512032 | tf_op jit(solution)/shard_map/ppermute | solution.py:13
  169.1 0.8 copy-done
  169.9 0.5 convolution_convert_fusion.7
  170.4 2.3 concatenate.4
  172.8 10.9 %convert_element_type.55 = bf16[320,32,90]{2,1,0:T(8,128)(2,1)S(1)} reshape(bf16[320,2880]{1,0:T(8,128)(2,1)} %concatenate.4) | data formatting | bytes 3686400 | tf_op jit(solution)/shard_map/convert_element_type | solution.py:66
  183.6 6.1 %copy.8 = bf16[2,16,320,90]{2,3,1,0:T(8,128)(2,1)} copy(bf16[2,16,320,90]{3,0,1,2:T(2,128)(2,1)S(1)} %bitcast.62) | data formatting | bytes 3686400 | tf_op jit(solution)/shard_map/transpose | solution.py:26
  189.7 0.0 reduce-scatter.5.cloned.1.call-start
  189.8 4.2 %reshape.20 = bf16[2880,320]{1,0:T(8,128)(2,1)} reshape(bf16[32,90,320]{2,1,0:T(8,128)(2,1)} %all-gather.3.cloned.1.call-done) | data formatting | bytes 3686400
  194.1 3.0 copy.10
  197.1 1.4 convolution_convert_fusion
  198.5 1.9 collective-permute-start.14
  200.4 1.3 convolution_convert_fusion.1
  201.7 1.9 collective-permute-start.13
  203.6 1.4 convolution_convert_fusion.2
  205.0 2.7 collective-permute-start.12
  207.8 1.3 convolution_convert_fusion.3
  209.1 7.8 %collective-permute-start.11 = (bf16[320,800]{1,0:T(8,128)(2,1)}, bf16[320,800]{1,0:T(8,128)(2,1)}, u32[]{:S(2)}, u32[]{:S(2)}) collective-permute-start(bf16[320,800]{1,0:T(8,128)(2,1)} %convolution_convert_fusion.3), channel_id=1, source_target_pairs={{0,384},{32,416},{64,448},{96,480},{128,0},{160,32},{192,64},{224,... | collective-permute-start | bytes 1536008 | tf_op jit(solution)/shard_map/ppermute | solution.py:13
  217.0 1.4 convolution_convert_fusion.4
  218.4 2.4 collective-permute-start.10
  220.8 0.5 fusion.8
  221.3 0.5 convolution_add_fusion.7
  221.8 0.5 copy-done.7
  222.4 0.5 convolution_add_fusion.6
  222.8 0.6 copy-done.14
  223.5 1.5 convolution_add_fusion.5
  225.0 1.3 reduce-scatter.3.cloned.1.call-done
  226.3 1.9 convolution_add_fusion.4
  228.2 0.5 convolution_convert_fusion.5
  228.7 0.6 convolution_convert_fusion.6
  229.3 0.5 convolution_add_fusion.3
  229.9 4.9 %collective-permute-start.9 = (bf16[320,800]{1,0:T(8,128)(2,1)S(1)}, bf16[320,800]{1,0:T(8,128)(2,1)S(1)}, u32[]{:S(2)}, u32[]{:S(2)}) collective-permute-start(bf16[320,800]{1,0:T(8,128)(2,1)S(1)} %convolution_convert_fusion.5), channel_id=1, source_target_pairs={{0,448},{32,480},{64,0},{96,32},{128,64},{160,96},{192,128},{224,1... | collective-permute-start | bytes 1536008 | tf_op jit(solution)/shard_map/ppermute | solution.py:13
  234.8 10.4 %collective-permute-done.13 = bf16[320,800]{1,0:T(8,128)(2,1)} collective-permute-done((bf16[320,800]{1,0:T(8,128)(2,1)}, bf16[320,800]{1,0:T(8,128)(2,1)}, u32[]{:S(2)}, u32[]{:S(2)}) %collective-permute-start.13) | collective-permute-done | bytes 512032 | tf_op jit(solution)/shard_map/ppermute | solution.py:13
  245.2 7.7 %collective-permute-start.8 = (bf16[320,800]{1,0:T(8,128)(2,1)S(1)}, bf16[320,800]{1,0:T(8,128)(2,1)S(1)}, u32[]{:S(2)}, u32[]{:S(2)}) collective-permute-start(bf16[320,800]{1,0:T(8,128)(2,1)S(1)} %convolution_convert_fusion.6), channel_id=1, source_target_pairs={{0,480},{32,0},{64,32},{96,64},{128,96},{160,128},{192,160},{224,1... | collective-permute-start | bytes 1536008 | tf_op jit(solution)/shard_map/ppermute | solution.py:13
  252.9 0.5 convolution_add_fusion.2
  253.4 0.5 convolution_add_fusion.1
  254.0 1.7 collective-permute-done.10
  255.7 42.4 %collective-permute-done.9 = bf16[320,800]{1,0:T(8,128)(2,1)S(1)} collective-permute-done((bf16[320,800]{1,0:T(8,128)(2,1)S(1)}, bf16[320,800]{1,0:T(8,128)(2,1)S(1)}, u32[]{:S(2)}, u32[]{:S(2)}) %collective-permute-start.9) | collective-permute-done | bytes 512032 | tf_op jit(solution)/shard_map/ppermute | solution.py:13
  298.1 3.4 fusion.6
  301.5 86.4 %reduce-scatter.5.cloned.1.call-done = bf16[1,320,90]{1,2,0:T(8,128)(2,1)} async-done(((bf16[16,320,90]{1,2,0:T(8,128)(2,1)}), bf16[1,320,90]{1,2,0:T(8,128)(2,1)}) %reduce-scatter.5.cloned.1.call-update) | async-done | bytes 57616 | tf_op jit(solution)/shard_map/reduce_scatter | solution.py:28
  387.9 1.6 bitcast_add_fusion
  (39 shorter events, 0.2 us)
Async XLA Ops:
  8.0 181.8 %all-gather.3.cloned.1.call-start = ((), (), s32[]{:S(2)}) async-start(), calls=%async_computation.4 | async-start | bytes 2433024 | tf_op jit(solution)/shard_map/all_gather | solution.py:47
  9.4 19.7 %collective-permute-start = (bf16[320,800]{1,0:T(8,128)(2,1)S(1)}, bf16[320,800]{1,0:T(8,128)(2,1)S(1)}, u32[]{:S(2)}, u32[]{:S(2)}) collective-permute-start(bf16[320,800]{1,0:T(8,128)(2,1)S(1)} %convert_element_type.54), channel_id=1, source_target_pairs={{0,32},{32,64},{64,96},{96,128},{128,160},{160,192},{192,224},{224... | collective-permute-start | bytes 1536008 | tf_op jit(solution)/shard_map/ppermute | solution.py:13
  29.0 59.9 %copy-start.2 = (bf16[320,800]{1,0:T(8,128)(2,1)}, bf16[320,800]{1,0:T(8,128)(2,1)S(1)}, u32[]{:S(2)}) copy-start(bf16[320,800]{1,0:T(8,128)(2,1)S(1)} %collective-permute-done) | copy-start | bytes 1536004
  29.1 18.7 %collective-permute-start.1 = (bf16[320,800]{1,0:T(8,128)(2,1)S(1)}, bf16[320,800]{1,0:T(8,128)(2,1)S(1)}, u32[]{:S(2)}, u32[]{:S(2)}) collective-permute-start(bf16[320,800]{1,0:T(8,128)(2,1)S(1)} %collective-permute-done), channel_id=1, source_target_pairs={{0,32},{32,64},{64,96},{96,128},{128,160},{160,192},{192,224},{224... | collective-permute-start | bytes 1536008 | tf_op jit(solution)/shard_map/ppermute | solution.py:13
  31.0 195.3 %reduce-scatter.3.cloned.1.call-start = ((), (), s32[]{:S(2)}) async-start(), calls=%async_computation.2 | async-start | bytes 3538944 | tf_op jit(solution)/shard_map/reduce_scatter | solution.py:27
  47.8 56.6 %copy-start.6 = (bf16[320,800]{1,0:T(8,128)(2,1)}, bf16[320,800]{1,0:T(8,128)(2,1)S(1)}, u32[]{:S(2)}) copy-start(bf16[320,800]{1,0:T(8,128)(2,1)S(1)} %collective-permute-done.1) | copy-start | bytes 1536004
  47.8 19.1 %collective-permute-start.2 = (bf16[320,800]{1,0:T(8,128)(2,1)S(1)}, bf16[320,800]{1,0:T(8,128)(2,1)S(1)}, u32[]{:S(2)}, u32[]{:S(2)}) collective-permute-start(bf16[320,800]{1,0:T(8,128)(2,1)S(1)} %collective-permute-done.1), channel_id=1, source_target_pairs={{0,32},{32,64},{64,96},{96,128},{128,160},{160,192},{192,224},{224... | collective-permute-start | bytes 1536008 | tf_op jit(solution)/shard_map/ppermute | solution.py:13
  66.9 38.0 %copy-start.13 = (bf16[320,800]{1,0:T(8,128)(2,1)}, bf16[320,800]{1,0:T(8,128)(2,1)S(1)}, u32[]{:S(2)}) copy-start(bf16[320,800]{1,0:T(8,128)(2,1)S(1)} %collective-permute-done.2) | copy-start | bytes 1536004
  66.9 19.1 %collective-permute-start.3 = (bf16[320,800]{1,0:T(8,128)(2,1)S(1)}, bf16[320,800]{1,0:T(8,128)(2,1)S(1)}, u32[]{:S(2)}, u32[]{:S(2)}) collective-permute-start(bf16[320,800]{1,0:T(8,128)(2,1)S(1)} %collective-permute-done.2), channel_id=1, source_target_pairs={{0,32},{32,64},{64,96},{96,128},{128,160},{160,192},{192,224},{224... | collective-permute-start | bytes 1536008 | tf_op jit(solution)/shard_map/ppermute | solution.py:13
  86.0 48.5 %copy-start.10 = (bf16[320,800]{1,0:T(8,128)(2,1)}, bf16[320,800]{1,0:T(8,128)(2,1)S(1)}, u32[]{:S(2)}) copy-start(bf16[320,800]{1,0:T(8,128)(2,1)S(1)} %collective-permute-done.3) | copy-start | bytes 1536004
  86.0 16.4 %collective-permute-start.4 = (bf16[320,800]{1,0:T(8,128)(2,1)S(1)}, bf16[320,800]{1,0:T(8,128)(2,1)S(1)}, u32[]{:S(2)}, u32[]{:S(2)}) collective-permute-start(bf16[320,800]{1,0:T(8,128)(2,1)S(1)} %collective-permute-done.3), channel_id=1, source_target_pairs={{0,32},{32,64},{64,96},{96,128},{128,160},{160,192},{192,224},{224... | collective-permute-start | bytes 1536008 | tf_op jit(solution)/shard_map/ppermute | solution.py:13
  102.4 32.6 %copy-start.11 = (bf16[320,800]{1,0:T(8,128)(2,1)}, bf16[320,800]{1,0:T(8,128)(2,1)S(1)}, u32[]{:S(2)}) copy-start(bf16[320,800]{1,0:T(8,128)(2,1)S(1)} %collective-permute-done.4) | copy-start | bytes 1536004
  102.4 30.1 %collective-permute-start.5 = (bf16[320,800]{1,0:T(8,128)(2,1)S(1)}, bf16[320,800]{1,0:T(8,128)(2,1)S(1)}, u32[]{:S(2)}, u32[]{:S(2)}) collective-permute-start(bf16[320,800]{1,0:T(8,128)(2,1)S(1)} %collective-permute-done.4), channel_id=1, source_target_pairs={{0,32},{32,64},{64,96},{96,128},{128,160},{160,192},{192,224},{224... | collective-permute-start | bytes 1536008 | tf_op jit(solution)/shard_map/ppermute | solution.py:13
  132.6 21.0 %copy-start.4 = (bf16[320,800]{1,0:T(8,128)(2,1)}, bf16[320,800]{1,0:T(8,128)(2,1)S(1)}, u32[]{:S(2)}) copy-start(bf16[320,800]{1,0:T(8,128)(2,1)S(1)} %collective-permute-done.5) | copy-start | bytes 1536004
  132.6 19.0 %collective-permute-start.6 = (bf16[320,800]{1,0:T(8,128)(2,1)S(1)}, bf16[320,800]{1,0:T(8,128)(2,1)S(1)}, u32[]{:S(2)}, u32[]{:S(2)}) collective-permute-start(bf16[320,800]{1,0:T(8,128)(2,1)S(1)} %collective-permute-done.5), channel_id=1, source_target_pairs={{0,32},{32,64},{64,96},{96,128},{128,160},{160,192},{192,224},{224... | collective-permute-start | bytes 1536008 | tf_op jit(solution)/shard_map/ppermute | solution.py:13
  151.6 2.9 copy-start.8
  151.6 17.5 %collective-permute-start.7 = (bf16[320,800]{1,0:T(8,128)(2,1)S(1)}, bf16[320,800]{1,0:T(8,128)(2,1)S(1)}, u32[]{:S(2)}, u32[]{:S(2)}) collective-permute-start(bf16[320,800]{1,0:T(8,128)(2,1)S(1)} %collective-permute-done.6), channel_id=1, source_target_pairs={{0,32},{32,64},{64,96},{96,128},{128,160},{160,192},{192,224},{224... | collective-permute-start | bytes 1536008 | tf_op jit(solution)/shard_map/ppermute | solution.py:13
  169.1 0.8 copy-start
  189.7 198.1 %reduce-scatter.5.cloned.1.call-start = ((), (), s32[]{:S(2)}) async-start(), calls=%async_computation.3 | async-start | bytes 1253376 | tf_op jit(solution)/shard_map/reduce_scatter | solution.py:28
  198.5 31.4 %collective-permute-start.14 = (bf16[320,800]{1,0:T(8,128)(2,1)}, bf16[320,800]{1,0:T(8,128)(2,1)S(1)}, u32[]{:S(2)}, u32[]{:S(2)}) collective-permute-start(bf16[320,800]{1,0:T(8,128)(2,1)} %convolution_convert_fusion), channel_id=1, source_target_pairs={{0,288},{32,320},{64,352},{96,384},{128,416},{160,448},{192,480},{... | collective-permute-start | bytes 1536008 | tf_op jit(solution)/shard_map/ppermute | solution.py:13
  201.7 43.5 %collective-permute-start.13 = (bf16[320,800]{1,0:T(8,128)(2,1)}, bf16[320,800]{1,0:T(8,128)(2,1)}, u32[]{:S(2)}, u32[]{:S(2)}) collective-permute-start(bf16[320,800]{1,0:T(8,128)(2,1)} %convolution_convert_fusion.1), channel_id=1, source_target_pairs={{0,320},{32,352},{64,384},{96,416},{128,448},{160,480},{192,0},{22... | collective-permute-start | bytes 1536008 | tf_op jit(solution)/shard_map/ppermute | solution.py:13
  205.0 48.9 %collective-permute-start.12 = (bf16[320,800]{1,0:T(8,128)(2,1)}, bf16[320,800]{1,0:T(8,128)(2,1)}, u32[]{:S(2)}, u32[]{:S(2)}) collective-permute-start(bf16[320,800]{1,0:T(8,128)(2,1)} %convolution_convert_fusion.2), channel_id=1, source_target_pairs={{0,352},{32,384},{64,416},{96,448},{128,480},{160,0},{192,32},{224... | collective-permute-start | bytes 1536008 | tf_op jit(solution)/shard_map/ppermute | solution.py:13
  209.1 44.9 %collective-permute-start.11 = (bf16[320,800]{1,0:T(8,128)(2,1)}, bf16[320,800]{1,0:T(8,128)(2,1)}, u32[]{:S(2)}, u32[]{:S(2)}) collective-permute-start(bf16[320,800]{1,0:T(8,128)(2,1)} %convolution_convert_fusion.3), channel_id=1, source_target_pairs={{0,384},{32,416},{64,448},{96,480},{128,0},{160,32},{192,64},{224,... | collective-permute-start | bytes 1536008 | tf_op jit(solution)/shard_map/ppermute | solution.py:13
  218.4 2.9 copy-start.3
  218.4 37.3 %collective-permute-start.10 = (bf16[320,800]{1,0:T(8,128)(2,1)}, bf16[320,800]{1,0:T(8,128)(2,1)}, u32[]{:S(2)}, u32[]{:S(2)}) collective-permute-start(bf16[320,800]{1,0:T(8,128)(2,1)} %convolution_convert_fusion.4), channel_id=1, source_target_pairs={{0,416},{32,448},{64,480},{96,0},{128,32},{160,64},{192,96},{224,1... | collective-permute-start | bytes 1536008 | tf_op jit(solution)/shard_map/ppermute | solution.py:13
  221.3 1.1 copy-start.7
  222.4 1.1 copy-start.14
  228.2 1.1 copy-start.12
  229.3 23.6 %copy-start.5 = (bf16[320,800]{1,0:T(8,128)(2,1)S(1)}, bf16[320,800]{1,0:T(8,128)(2,1)}, u32[]{:S(2)}) copy-start(bf16[320,800]{1,0:T(8,128)(2,1)} %copy-done.4) | copy-start | bytes 1536004
  229.9 23.5 %copy-start.9 = (bf16[320,800]{1,0:T(8,128)(2,1)S(1)}, bf16[320,800]{1,0:T(8,128)(2,1)}, u32[]{:S(2)}) copy-start(bf16[320,800]{1,0:T(8,128)(2,1)} %copy-done.8) | copy-start | bytes 1536004
  229.9 68.2 %collective-permute-start.9 = (bf16[320,800]{1,0:T(8,128)(2,1)S(1)}, bf16[320,800]{1,0:T(8,128)(2,1)S(1)}, u32[]{:S(2)}, u32[]{:S(2)}) collective-permute-start(bf16[320,800]{1,0:T(8,128)(2,1)S(1)} %convolution_convert_fusion.5), channel_id=1, source_target_pairs={{0,448},{32,480},{64,0},{96,32},{128,64},{160,96},{192,128},{224,1... | collective-permute-start | bytes 1536008 | tf_op jit(solution)/shard_map/ppermute | solution.py:13
  245.2 52.9 %collective-permute-start.8 = (bf16[320,800]{1,0:T(8,128)(2,1)S(1)}, bf16[320,800]{1,0:T(8,128)(2,1)S(1)}, u32[]{:S(2)}, u32[]{:S(2)}) collective-permute-start(bf16[320,800]{1,0:T(8,128)(2,1)S(1)} %convolution_convert_fusion.6), channel_id=1, source_target_pairs={{0,480},{32,0},{64,32},{96,64},{128,96},{160,128},{192,160},{224,1... | collective-permute-start | bytes 1536008 | tf_op jit(solution)/shard_map/ppermute | solution.py:13
  253.4 44.7 %copy-start.1 = (bf16[320,800]{1,0:T(8,128)(2,1)S(1)}, bf16[320,800]{1,0:T(8,128)(2,1)}, u32[]{:S(2)}) copy-start(bf16[320,800]{1,0:T(8,128)(2,1)} %copy-done) | copy-start | bytes 1536004
  254.0 133.9 %copy-start.15 = (f32[320,90]{0,1:T(8,128)S(1)}, f32[320,90]{0,1:T(8,128)}, u32[]{:S(2)}) copy-start(f32[320,90]{0,1:T(8,128)} %param.4) | copy-start | bytes 345604
Sparse Core Ops, SparseCore 0:
  31.1 98.2 all-gather.2
Sparse Core Ops, SparseCore 1:
  189.8 36.4 reduce-scatter.2
  230.8 157.1 reduce-scatter.4
where the time goes:
time: 398 us; the launch traced here: 397 us
  waiting for transfers between devices  281 us (71%)
  starting transfers between devices  46.7 us (12%)
  local copies, waits for them, and re-layouts  28.5 us (7%)
  matrix products  22.3 us (6%)
  between operations  15.9 us (4%)
    ppermute x15, waiting for transfers between devices, passed_along(): return lax.ppermute(x, axis, [(i, (i + by) % count) for i in range(count)])  193 us
    reduce_scatter x1, waiting for transfers between devices, summed_rows(): return lax.psum_scatter(blocks, chips, scatter_dimension=0, tiled=True)[0]  86.4 us
    ppermute x15, starting transfers between devices, passed_along(): return lax.ppermute(x, axis, [(i, (i + by) % count) for i in range(count)])  46.5 us
    convert_element_type x1, local copies, waits for them, and re-layouts, local(): gram_band.astype(jnp.bfloat16)  10.9 us
    dot_general x9, matrix products, local(): jnp.dot(own_tile(offset), moving, preferred_element_type=jnp.float32)  9.89 us
    unnamed x34, local copies, waits for them, and re-layouts  9.23 us
    dot_general x7, matrix products, contract_rows(): lax.dot_general(left, right, (((0,), (0,)), ((), ())), preferred_element_...  8 us
  transfers between devices with their start and end apart: 18, of which 13 were waited for; matrix products, arithmetic and copies ran while one was open for 12% of the time, Pallas kernels for 0%

commit v1 on v0

v1 whole, which is shorter than its diff:
```python
import jax
import jax.numpy as jnp
from jax import lax
from jax.sharding import Mesh
from jax.sharding import PartitionSpec as P

INTER = 25600
COL = ("x", "zh", "core")
ALL = ("row",) + COL
TILES = ((0, 0), (0, -1), (6, 4), (-1, -4), (4, 0), (4, -1), (6, 0), (6, -1), (4, -4))


def passed_along(x, axis, by):
    count = lax.axis_size(axis)
    return lax.ppermute(x, axis, [(i, (i + by) % count) for i in range(count)])


def shard_routes(sizes, shard, tile):
    nx, nzh, ncore = sizes
    routes = []
    for c in range(nx * nzh * ncore):
        first, last = c * shard // tile, (c * shard + shard - 1) // tile
        core, rest = divmod(c, nx * nzh)
        x, zh = divmod(rest, nzh)
        place = (x * nzh + zh) * ncore + core
        one, two = TILES[first][0], TILES[last][0]
        routes.append((c, place, one, two, last * tile - c * shard if one != two else shard))
    return routes


def dot(left, right, dims):
    return lax.dot_general(left, right, (dims, ((), ())), preferred_element_type=jnp.float32)


def local(gradient, previous, root):
    rows, shard = previous.shape
    n_row = lax.axis_size("row")
    nx, nzh, ncore = (lax.axis_size(a) for a in COL)
    n_col = nx * nzh * ncore
    routes = shard_routes((nx, nzh, ncore), shard, rows)
    core = lax.axis_index("core")
    col = lax.axis_index(COL)
    cut = jnp.asarray([r[4] for r in routes], jnp.int32)[col]
    held_c = (core * nx + lax.axis_index("x")) * nzh + lax.axis_index("zh")
    held_cut = jnp.asarray([r[4] for r in routes], jnp.int32)[held_c]
    place_in_shard = lax.broadcasted_iota(jnp.int32, (shard, rows), 0)

    g = {0: gradient.astype(jnp.bfloat16)}
    g[-1] = passed_along(g[0], "row", 1)
    g[-4] = passed_along(g[0], "row", 4)
    g[4] = passed_along(g[0], "row", -4)
    g[6] = passed_along(g[-1], "row", -7)

    mine = root.T
    to_use = [
        [((i + r[pick]) % n_row * n_col + r[0], i * n_col + r[1]) for i in range(n_row) for r in routes if pick == 2 or r[2] != r[3]]
        for pick in (2, 3)
    ]
    one = lax.ppermute(mine, ALL, to_use[0])
    two = lax.ppermute(mine, ALL, to_use[1])
    piece = jnp.where(place_in_shard < held_cut, one, two)
    piece = lax.all_to_all(jnp.broadcast_to(piece[None], (nzh,) + piece.shape), "zh", 0, 0, tiled=True)
    piece = lax.all_to_all(jnp.broadcast_to(piece[None], (nx,) + piece.shape), "x", 0, 0, tiled=True)
    other = passed_along(piece, "core", 1)
    root_t = jnp.concatenate(
        [jnp.where(core == 0, piece, other), jnp.where(core == 0, other, piece)], 0
    ).reshape(-1, rows)

    gram = jnp.concatenate(
        [dot(g[b], g[a], ((1,), (1,))).astype(jnp.bfloat16) for a, b in TILES], 0
    )
    half = gram.shape[0] // ncore
    keep = lax.dynamic_slice_in_dim(gram, core * half, half, 0)
    give = lax.dynamic_slice_in_dim(gram, (1 - core) * half, half, 0)
    total = keep.astype(jnp.float32) + passed_along(give, "core", 1).astype(jnp.float32)
    for axis, count in (("x", nx), ("zh", nzh)):
        parts = total.astype(jnp.bfloat16).reshape(count, -1, rows)
        total = lax.all_to_all(parts, axis, 0, 0, tiled=True).astype(jnp.float32).sum(0)
    total = total.astype(jnp.bfloat16)
    home = [[(b, a) for a, b in pairs] for pairs in to_use]
    one = lax.ppermute(total, ALL, home[0])
    two = lax.ppermute(total, ALL, home[1])
    share = jnp.where(place_in_shard < cut, one, two).astype(jnp.float32).T
    statistic = 0.9 * previous + 0.1 / INTER * share

    out = {}
    last = n_row // 2
    for k, (a, b) in enumerate(TILES):
        tile = root_t[k * rows : (k + 1) * rows]
        terms = [(a, dot(tile, g[b], ((0,), (0,))))]
        if 0 < k < last:
            terms.append((b, dot(tile, g[a], ((1,), (0,)))))
        for o, term in terms:
            out[o] = out[o] + term if o in out else term
    applied = out[0]
    for o in (4, -4):
        applied = applied + passed_along(out[o].astype(jnp.bfloat16), "row", o).astype(jnp.float32)
    chained = out[-1] + passed_along(out[6].astype(jnp.bfloat16), "row", 7).astype(jnp.float32)
    applied = applied + passed_along(chained.astype(jnp.bfloat16), "row", -1).astype(jnp.float32)
    return (statistic, applied)


def solution(mesh):
    split = Mesh(mesh.devices.reshape(mesh.shape["row"], 4, 4, 2), ALL)
    spec = P("row", COL)
    return jax.shard_map(
        local, mesh=split, in_specs=(spec,) * 3, out_specs=(spec,) * 2, check_vma=False
    )
```

time: 398 us -> 188 us (0.47)
  the two profiles are of different devices: /device:TPU:24 before, /device:TPU:35 now
where the time goes in v1:
time: 188 us; the launch traced here: 187 us
  starting transfers between devices  88.7 us (47%)
  waiting for transfers between devices  34.9 us (19%)
  matrix products  28.6 us (15%)
  local copies, waits for them, and re-layouts  20.6 us (11%)
  other arithmetic  12.6 us (7%)
    ppermute x10, starting transfers between devices, passed_along(): return lax.ppermute(x, axis, [(i, (i + by) % count) for i in range(count)])  29.6 us
    dot_general x25, matrix products, dot(): lax.dot_general(left, right, (dims, ((), ())), preferred_element_type=jnp...  28.6 us
    all_to_all x1, starting transfers between devices, local(): lax.all_to_all(jnp.broadcast_to(piece[None], (nx,) + piece.shape), 'x', 0...  16.4 us
    ppermute x1, starting transfers between devices, local(): one = lax.ppermute(mine, ALL, to_use[0])  15.6 us
    ppermute x1, waiting for transfers between devices, local(): one = lax.ppermute(total, ALL, home[0])  14.2 us
    all_to_all x2, starting transfers between devices, local(): lax.all_to_all(parts, axis, 0, 0, tiled=True).astype(jnp.float32).sum(0)  11.1 us
    ppermute x1, starting transfers between devices, local(): one = lax.ppermute(total, ALL, home[0])  9.99 us
    reshape x4, local copies, waits for them, and re-layouts, local(): parts = total.astype(jnp.bfloat16).reshape(count, -1, rows)  7.76 us
  transfers between devices with their start and end apart: 18, of which 5 were waited for; matrix products, arithmetic and copies ran while one was open for 32% of the time, Pallas kernels for 0%

profile of v1, /device:TPU:35, one launch (start us, length us, event | category | flops | bytes accessed | tf_op | source)
XLA Modules:
  0.0 186.6 jit_solution(2050316458161683505)
XLA Ops:
  0.6 15.6 %collective-permute-start.7 = (bf16[90,320]{1,0:T(8,128)(2,1)}, bf16[90,320]{1,0:T(8,128)(2,1)S(1)}, u32[]{:S(2)}, u32[]{:S(2)}) collective-permute-start(bf16[90,320]{1,0:T(8,128)(2,1)} %bitcast.49), channel_id=1, source_target_pairs={{0,0},{1,2},{2,4},{3,6},{4,8},{5,10},{6,12},{7,14},{200,16},{201,1... | collective-permute-start | bytes 172808 | tf_op jit(solution)/shard_map/ppermute | solution.py:59
  16.3 0.7 collective-permute-start.8
  17.0 1.3 convert_element_type.70
  18.3 2.3 %collective-permute-start.3 = (bf16[320,800]{1,0:T(8,128)(2,1)S(1)}, bf16[320,800]{1,0:T(8,128)(2,1)S(1)}, u32[]{:S(2)}, u32[]{:S(2)}) collective-permute-start(bf16[320,800]{1,0:T(8,128)(2,1)S(1)} %convert_element_type.70), channel_id=1, source_target_pairs={{0,128},{32,160},{64,192},{96,224},{128,256},{160,288},{192,320},{... | collective-permute-start | bytes 1536008 | tf_op jit(solution)/shard_map/ppermute | solution.py:15
  20.6 1.9 %collective-permute-start = (bf16[320,800]{1,0:T(8,128)(2,1)S(1)}, bf16[320,800]{1,0:T(8,128)(2,1)S(1)}, u32[]{:S(2)}, u32[]{:S(2)}) collective-permute-start(bf16[320,800]{1,0:T(8,128)(2,1)S(1)} %convert_element_type.70), channel_id=1, source_target_pairs={{0,32},{32,64},{64,96},{96,128},{128,160},{160,192},{192,224},{224... | collective-permute-start | bytes 1536008 | tf_op jit(solution)/shard_map/ppermute | solution.py:15
  22.5 4.2 %collective-permute-start.1 = (bf16[320,800]{1,0:T(8,128)(2,1)S(1)}, bf16[320,800]{1,0:T(8,128)(2,1)S(1)}, u32[]{:S(2)}, u32[]{:S(2)}) collective-permute-start(bf16[320,800]{1,0:T(8,128)(2,1)S(1)} %convert_element_type.70), channel_id=1, source_target_pairs={{0,384},{32,416},{64,448},{96,480},{128,0},{160,32},{192,64},{224,... | collective-permute-start | bytes 1536008 | tf_op jit(solution)/shard_map/ppermute | solution.py:15
  26.7 0.7 fusion.33
  27.9 0.7 iota_compare_fusion
  28.7 0.7 broadcast_in_dim.4
  29.4 4.7 %all-to-all-start.2 = ((bf16[4,90,320]{2,1,0:T(8,128)(2,1)}), bf16[4,90,320]{2,1,0:T(8,128)(2,1)S(1)}, u32[]{:S(2)}, u32[]{:S(2)}) async-start(bf16[4,90,320]{2,1,0:T(8,128)(2,1)} %broadcast_in_dim.4), calls=%async_computation.2 | async-start | bytes 589824 | tf_op jit(solution)/shard_map/all_to_all | solution.py:62
  34.2 3.8 %collective-permute-start.2 = (bf16[320,800]{1,0:T(8,128)(2,1)S(1)}, bf16[320,800]{1,0:T(8,128)(2,1)S(1)}, u32[]{:S(2)}, u32[]{:S(2)}) collective-permute-start(bf16[320,800]{1,0:T(8,128)(2,1)S(1)} %collective-permute-done), channel_id=1, source_target_pairs={{0,288},{32,320},{64,352},{96,384},{128,416},{160,448},{192,480},{... | collective-permute-start | bytes 1536008 | tf_op jit(solution)/shard_map/ppermute | solution.py:15
  38.0 1.2 convolution_convert_fusion.4
  39.2 1.2 convolution_convert_fusion.6
  40.4 1.2 convolution_convert_fusion.1
  41.6 1.2 convolution_convert_fusion.8
  42.8 1.2 convolution_convert_fusion.5
  44.0 6.5 %all-to-all-done.2 = bf16[4,90,320]{2,1,0:T(8,128)(2,1)S(1)} async-done(((bf16[4,90,320]{2,1,0:T(8,128)(2,1)}), bf16[4,90,320]{2,1,0:T(8,128)(2,1)S(1)}, u32[]{:S(2)}, u32[]{:S(2)}) %all-to-all-start.2) | async-done | bytes 230432 | tf_op jit(solution)/shard_map/all_to_all | solution.py:62
  50.6 1.3 broadcast_in_dim.5
  51.9 16.4 %all-to-all-start.3 = ((bf16[4,4,90,320]{3,1,2,0:T(4,128)(2,1)}), bf16[4,4,90,320]{3,1,2,0:T(4,128)(2,1)}, u32[]{:S(2)}, u32[]{:S(2)}) async-start(bf16[4,4,90,320]{3,1,2,0:T(4,128)(2,1)} %broadcast_in_dim.5), calls=%async_computation.3 | async-start | bytes 2211840 | tf_op jit(solution)/shard_map/all_to_all | solution.py:63
  68.2 1.2 convolution_convert_fusion.2
  69.4 1.2 convolution_convert_fusion.7
  70.6 1.2 convolution_convert_fusion.3
  71.8 2.8 %concatenate.6 = bf16[2880,320]{0,1:T(8,128)(2,1)S(1)} concatenate(bf16[320,320]{0,1:T(8,128)(2,1)S(1)} %convolution_convert_fusion.9, bf16[320,320]{0,1:T(8,128)(2,1)} %convolution_convert_fusion.8, bf16[320,320]{0,1:T(8,128)(2,1)} %convolution_convert_fusion.7, bf16[320,320]{0,1:T(8,128)(2,1)} %convolution_convert_fusion.6, bf16[320,320]{0,1:T(8,128)(2,1)} %convolution_convert_fusion.5, ...), dimensions={0} | concatenate | bytes 3686400 | tf_op jit(solution)/shard_map/concatenate | solution.py:69
  74.6 1.4 constant_dynamic-slice_fusion
  76.0 1.9 %collective-permute-start.4 = (bf16[1440,320]{0,1:T(8,128)(2,1)}, bf16[1440,320]{0,1:T(8,128)(2,1)}, u32[]{:S(2)}, u32[]{:S(2)}) collective-permute-start(bf16[1440,320]{0,1:T(8,128)(2,1)} %constant_dynamic-slice_fusion), channel_id=1, source_target_pairs={{0,1},{1,0},{2,3},{3,2},{4,5},{5,4},{6,7},{7,6},{8,9},{9,8},{10,11... | collective-permute-start | bytes 2764808 | tf_op jit(solution)/shard_map/ppermute | solution.py:15
  77.9 3.9 %all-to-all-done.3 = bf16[4,4,90,320]{3,1,2,0:T(4,128)(2,1)} async-done(((bf16[4,4,90,320]{3,1,2,0:T(4,128)(2,1)}), bf16[4,4,90,320]{3,1,2,0:T(4,128)(2,1)}, u32[]{:S(2)}, u32[]{:S(2)}) %all-to-all-start.3) | async-done | bytes 921632 | tf_op jit(solution)/shard_map/all_to_all | solution.py:63
  81.8 1.9 %collective-permute-start.9 = (bf16[4,4,90,320]{3,1,2,0:T(4,128)(2,1)}, bf16[4,4,90,320]{3,1,2,0:T(4,128)(2,1)}, u32[]{:S(2)}, u32[]{:S(2)}) collective-permute-start(bf16[4,4,90,320]{3,1,2,0:T(4,128)(2,1)} %all-to-all-done.3), channel_id=1, source_target_pairs={{0,1},{1,0},{2,3},{3,2},{4,5},{5,4},{6,7},{7,6},{8,9},{9,8},{10,11... | collective-permute-start | bytes 2764808 | tf_op jit(solution)/shard_map/ppermute | solution.py:15
  83.7 0.7 iota_compare_fusion.1
  84.4 2.7 %add_convert_fusion = bf16[1440,320]{0,1:T(8,128)(2,1)} fusion(bf16[1440,320]{0,1:T(8,128)(2,1)} %collective-permute-done.4, bf16[2880,320]{0,1:T(8,128)(2,1)S(1)} %concatenate.6, s32[]{:T(128)S(6)} %select_n.32), kind=kLoop, calls=%fused_computation.1 | loop fusion | flops 1843200 | bytes 2764804 | tf_op jit(solution)/shard_map/convert_element_type | solution.py:77
  87.1 2.7 %reshape.15 = bf16[4,360,320]{1,0,2:T(4,128)(2,1)S(1)} reshape(bf16[1440,320]{0,1:T(8,128)(2,1)} %add_convert_fusion) | data formatting | bytes 1843200 | tf_op jit(solution)/shard_map/reshape | solution.py:77
  89.8 1.1 copy.11
  90.9 5.4 %all-to-all-start = ((bf16[4,360,320]{1,2,0:T(8,128)(2,1)}), bf16[4,360,320]{1,2,0:T(8,128)(2,1)}, u32[]{:S(2)}, u32[]{:S(2)}) async-start(bf16[4,360,320]{1,2,0:T(8,128)(2,1)} %copy.11), calls=%async_computation | async-start | bytes 1966080 | tf_op jit(solution)/shard_map/all_to_all | solution.py:78
  96.3 1.8 broadcast_select_fusion.1
  98.0 1.5 pad_maximum_fusion
  99.6 1.8 copy.15
  101.4 2.9 %reshape.17 = bf16[2880,320]{1,0:T(8,128)(2,1)S(1)} reshape(bf16[8,4,90,320]{3,2,1,0:T(8,128)(2,1)} %copy.15) | data formatting | bytes 3686400 | tf_op jit(solution)/shard_map/reshape | solution.py:67
  104.3 0.5 fusion.27
  105.8 0.6 copy-done.8
  106.4 0.5 fusion.10
  107.4 0.5 copy-done.1
  108.0 1.3 fusion.9
  109.3 2.0 %collective-permute-start.10 = (bf16[320,800]{1,0:T(8,128)(2,1)}, bf16[320,800]{1,0:T(8,128)(2,1)}, u32[]{:S(2)}, u32[]{:S(2)}) collective-permute-start(bf16[320,800]{1,0:T(8,128)(2,1)} %fusion.9), channel_id=1, source_target_pairs={{0,128},{32,160},{64,192},{96,224},{128,256},{160,288},{192,320},{... | collective-permute-start | bytes 1536008 | tf_op jit(solution)/shard_map/ppermute | solution.py:15
  111.9 1.3 fusion.8
  113.2 4.7 %collective-permute-start.12 = (bf16[320,800]{1,0:T(8,128)(2,1)}, bf16[320,800]{1,0:T(8,128)(2,1)}, u32[]{:S(2)}, u32[]{:S(2)}) collective-permute-start(bf16[320,800]{1,0:T(8,128)(2,1)} %fusion.8), channel_id=1, source_target_pairs={{0,224},{32,256},{64,288},{96,320},{128,352},{160,384},{192,416},{... | collective-permute-start | bytes 1536008 | tf_op jit(solution)/shard_map/ppermute | solution.py:15
  117.9 1.3 convolution_convert_fusion
  119.2 4.8 %collective-permute-start.11 = (bf16[320,800]{1,0:T(8,128)(2,1)}, bf16[320,800]{1,0:T(8,128)(2,1)}, u32[]{:S(2)}, u32[]{:S(2)}) collective-permute-start(bf16[320,800]{1,0:T(8,128)(2,1)} %convolution_convert_fusion), channel_id=1, source_target_pairs={{0,384},{32,416},{64,448},{96,480},{128,0},{160,32},{192,64},{224,... | collective-permute-start | bytes 1536008 | tf_op jit(solution)/shard_map/ppermute | solution.py:15
  124.0 0.5 convolution_add_fusion.3
  124.5 1.5 fusion.12
  126.0 1.5 convolution_add_fusion.2
  127.5 2.1 %reduce_sum.24 = bf16[360,320]{0,1:T(8,128)(2,1)} reduce(bf16[4,360,320]{1,2,0:T(8,128)(2,1)} %all-to-all-done, bf16[]{:T(256)} %constant.34.clone.1), dimensions={0}, to_apply=%region_0.1 | reduce | flops 345600 | bytes 1152002 | tf_op jit(solution)/shard_map/reduce_sum | solution.py:78
  129.7 1.9 %reshape.18 = bf16[4,90,320]{1,0,2:T(4,128)(2,1)} reshape(bf16[360,320]{0,1:T(8,128)(2,1)} %reduce_sum.24) | data formatting | bytes 460800 | tf_op jit(solution)/shard_map/reshape | solution.py:77
  131.6 2.0 %copy.16 = bf16[4,90,320]{2,1,0:T(8,128)(2,1)} copy(bf16[4,90,320]{1,0,2:T(4,128)(2,1)} %reshape.18) | data formatting | bytes 460800 | tf_op jit(solution)/shard_map/reshape | solution.py:77
  133.6 5.7 %all-to-all-start.1 = ((bf16[4,90,320]{2,1,0:T(8,128)(2,1)}), bf16[4,90,320]{2,1,0:T(8,128)(2,1)}, u32[]{:S(2)}, u32[]{:S(2)}) async-start(bf16[4,90,320]{2,1,0:T(8,128)(2,1)} %copy.16), calls=%async_computation.1 | async-start | bytes 589824 | tf_op jit(solution)/shard_map/all_to_all | solution.py:78
  139.4 2.8 %fusion.7 = bf16[320,800]{1,0:T(8,128)(2,1)} fusion(f32[320,800]{1,0:T(8,128)} %convolution_add_fusion.2, bf16[320,800]{1,0:T(8,128)(2,1)S(1)} %copy-done.2, bf16[320,800]{1,0:T(8,128)(2,1)} %collective-permute-done.12, bf16[2880,320]{1,0:T(8,128)(2,1)S(1)} %reshape.17), kind=kOutput, calls=%fused_computation.17 | convolution fusion | flops 164864000 | bytes 2867200 | tf_op jit(solution)/shard_map/dot_general | solution.py:32
  142.2 2.0 %collective-permute-start.13 = (bf16[320,800]{1,0:T(8,128)(2,1)}, bf16[320,800]{1,0:T(8,128)(2,1)}, u32[]{:S(2)}, u32[]{:S(2)}) collective-permute-start(bf16[320,800]{1,0:T(8,128)(2,1)} %fusion.7), channel_id=1, source_target_pairs={{0,480},{32,0},{64,32},{96,64},{128,96},{160,128},{192,160},{224,1... | collective-permute-start | bytes 1536008 | tf_op jit(solution)/shard_map/ppermute | solution.py:15
  144.8 1.5 convolution_add_fusion.6
  146.2 7.0 %all-to-all-done.1 = bf16[4,90,320]{2,1,0:T(8,128)(2,1)} async-done(((bf16[4,90,320]{2,1,0:T(8,128)(2,1)}), bf16[4,90,320]{2,1,0:T(8,128)(2,1)}, u32[]{:S(2)}, u32[]{:S(2)}) %all-to-all-start.1) | async-done | bytes 230432 | tf_op jit(solution)/shard_map/all_to_all | solution.py:78
  153.2 1.0 reduce_sum.25
  154.3 10.0 %collective-permute-start.5 = (bf16[90,320]{1,0:T(8,128)(2,1)S(1)}, bf16[90,320]{1,0:T(8,128)(2,1)S(1)}, u32[]{:S(2)}, u32[]{:S(2)}) collective-permute-start(bf16[90,320]{1,0:T(8,128)(2,1)S(1)} %reduce_sum.25), channel_id=1, source_target_pairs={{0,0},{2,1},{4,2},{6,3},{8,4},{10,5},{12,6},{14,7},{16,200},{18,20... | collective-permute-start | bytes 172808 | tf_op jit(solution)/shard_map/ppermute | solution.py:81
  164.3 0.7 collective-permute-start.6
  164.9 3.3 %collective-permute-done.13 = bf16[320,800]{1,0:T(8,128)(2,1)} collective-permute-done((bf16[320,800]{1,0:T(8,128)(2,1)}, bf16[320,800]{1,0:T(8,128)(2,1)}, u32[]{:S(2)}, u32[]{:S(2)}) %collective-permute-start.13) | collective-permute-done | bytes 512032 | tf_op jit(solution)/shard_map/ppermute | solution.py:15
  168.3 3.3 %fusion.6 = f32[320,800]{1,0:T(8,128)} fusion(f32[320,800]{1,0:T(8,128)} %convolution_add_fusion.6, bf16[320,800]{1,0:T(8,128)(2,1)S(1)} %copy-done.2, bf16[320,800]{1,0:T(8,128)(2,1)} %collective-permute-done.13, bf16[320,800]{1,0:T(8,128)(2,1)} %collective-permute-done.11, bf16[320,800]{1,0:T(8,128)(2,1)} %collective-permute-done.10, ...), kind=kOutput, calls=%fused_computation.14 | convolution fusion | flops 165632000 | bytes 4403200 | tf_op jit(solution)/shard_map/dot_general | solution.py:32
  171.6 14.2 %collective-permute-done.5 = bf16[90,320]{1,0:T(8,128)(2,1)S(1)} collective-permute-done((bf16[90,320]{1,0:T(8,128)(2,1)S(1)}, bf16[90,320]{1,0:T(8,128)(2,1)S(1)}, u32[]{:S(2)}, u32[]{:S(2)}) %collective-permute-start.5) | collective-permute-done | bytes 57632 | tf_op jit(solution)/shard_map/ppermute | solution.py:81
  185.8 0.8 bitcast_add_fusion
  (41 shorter events, 3.3 us)
Async XLA Ops:
  0.6 26.1 %copy-start.10 = (s32[32]{0:T(128)S(1)}, s32[32]{0:T(128)}, u32[]{:S(2)}) copy-start(s32[32]{0:T(128)} %constant.37.clone) | copy-start | bytes 388
  0.6 27.9 %collective-permute-start.7 = (bf16[90,320]{1,0:T(8,128)(2,1)}, bf16[90,320]{1,0:T(8,128)(2,1)S(1)}, u32[]{:S(2)}, u32[]{:S(2)}) collective-permute-start(bf16[90,320]{1,0:T(8,128)(2,1)} %bitcast.49), channel_id=1, source_target_pairs={{0,0},{1,2},{2,4},{3,6},{4,8},{5,10},{6,12},{7,14},{200,16},{201,1... | collective-permute-start | bytes 172808 | tf_op jit(solution)/shard_map/ppermute | solution.py:59
  16.3 12.3 %collective-permute-start.8 = (bf16[90,320]{1,0:T(8,128)(2,1)}, bf16[90,320]{1,0:T(8,128)(2,1)S(1)}, u32[]{:S(2)}, u32[]{:S(2)}) collective-permute-start(bf16[90,320]{1,0:T(8,128)(2,1)} %bitcast.50), channel_id=1, source_target_pairs={{199,14},{490,20},{142,28},{213,11},{156,25},{231,46},{10,52},{174... | collective-permute-start | bytes 172808 | tf_op jit(solution)/shard_map/ppermute | solution.py:60
  18.3 20.9 %collective-permute-start.3 = (bf16[320,800]{1,0:T(8,128)(2,1)S(1)}, bf16[320,800]{1,0:T(8,128)(2,1)S(1)}, u32[]{:S(2)}, u32[]{:S(2)}) collective-permute-start(bf16[320,800]{1,0:T(8,128)(2,1)S(1)} %convert_element_type.70), channel_id=1, source_target_pairs={{0,128},{32,160},{64,192},{96,224},{128,256},{160,288},{192,320},{... | collective-permute-start | bytes 1536008 | tf_op jit(solution)/shard_map/ppermute | solution.py:15
  20.6 13.6 %collective-permute-start = (bf16[320,800]{1,0:T(8,128)(2,1)S(1)}, bf16[320,800]{1,0:T(8,128)(2,1)S(1)}, u32[]{:S(2)}, u32[]{:S(2)}) collective-permute-start(bf16[320,800]{1,0:T(8,128)(2,1)S(1)} %convert_element_type.70), channel_id=1, source_target_pairs={{0,32},{32,64},{64,96},{96,128},{128,160},{160,192},{192,224},{224... | collective-permute-start | bytes 1536008 | tf_op jit(solution)/shard_map/ppermute | solution.py:15
  22.5 15.4 %collective-permute-start.1 = (bf16[320,800]{1,0:T(8,128)(2,1)S(1)}, bf16[320,800]{1,0:T(8,128)(2,1)S(1)}, u32[]{:S(2)}, u32[]{:S(2)}) collective-permute-start(bf16[320,800]{1,0:T(8,128)(2,1)S(1)} %convert_element_type.70), channel_id=1, source_target_pairs={{0,384},{32,416},{64,448},{96,480},{128,0},{160,32},{192,64},{224,... | collective-permute-start | bytes 1536008 | tf_op jit(solution)/shard_map/ppermute | solution.py:15
  29.4 21.0 %all-to-all-start.2 = ((bf16[4,90,320]{2,1,0:T(8,128)(2,1)}), bf16[4,90,320]{2,1,0:T(8,128)(2,1)S(1)}, u32[]{:S(2)}, u32[]{:S(2)}) async-start(bf16[4,90,320]{2,1,0:T(8,128)(2,1)} %broadcast_in_dim.4), calls=%async_computation.2 | async-start | bytes 589824 | tf_op jit(solution)/shard_map/all_to_all | solution.py:62
  34.2 34.1 %collective-permute-start.2 = (bf16[320,800]{1,0:T(8,128)(2,1)S(1)}, bf16[320,800]{1,0:T(8,128)(2,1)S(1)}, u32[]{:S(2)}, u32[]{:S(2)}) collective-permute-start(bf16[320,800]{1,0:T(8,128)(2,1)S(1)} %collective-permute-done), channel_id=1, source_target_pairs={{0,288},{32,320},{64,352},{96,384},{128,416},{160,448},{192,480},{... | collective-permute-start | bytes 1536008 | tf_op jit(solution)/shard_map/ppermute | solution.py:15
  38.0 31.4 %copy-start.3 = (bf16[320,800]{1,0:T(8,128)(2,1)}, bf16[320,800]{1,0:T(8,128)(2,1)S(1)}, u32[]{:S(2)}) copy-start(bf16[320,800]{1,0:T(8,128)(2,1)S(1)} %collective-permute-done.1) | copy-start | bytes 1536004
  39.2 2.4 %copy-start.7 = (bf16[320,800]{1,0:T(8,128)(2,1)}, bf16[320,800]{1,0:T(8,128)(2,1)S(1)}, u32[]{:S(2)}) copy-start(bf16[320,800]{1,0:T(8,128)(2,1)S(1)} %collective-permute-done.3) | copy-start | bytes 1536004
  51.9 29.9 %all-to-all-start.3 = ((bf16[4,4,90,320]{3,1,2,0:T(4,128)(2,1)}), bf16[4,4,90,320]{3,1,2,0:T(4,128)(2,1)}, u32[]{:S(2)}, u32[]{:S(2)}) async-start(bf16[4,4,90,320]{3,1,2,0:T(4,128)(2,1)} %broadcast_in_dim.5), calls=%async_computation.3 | async-start | bytes 2211840 | tf_op jit(solution)/shard_map/all_to_all | solution.py:63
  68.2 2.4 %copy-start = (bf16[320,800]{1,0:T(8,128)(2,1)}, bf16[320,800]{1,0:T(8,128)(2,1)S(1)}, u32[]{:S(2)}) copy-start(bf16[320,800]{1,0:T(8,128)(2,1)S(1)} %collective-permute-done.2) | copy-start | bytes 1536004
  76.0 8.4 %collective-permute-start.4 = (bf16[1440,320]{0,1:T(8,128)(2,1)}, bf16[1440,320]{0,1:T(8,128)(2,1)}, u32[]{:S(2)}, u32[]{:S(2)}) collective-permute-start(bf16[1440,320]{0,1:T(8,128)(2,1)} %constant_dynamic-slice_fusion), channel_id=1, source_target_pairs={{0,1},{1,0},{2,3},{3,2},{4,5},{5,4},{6,7},{7,6},{8,9},{9,8},{10,11... | collective-permute-start | bytes 2764808 | tf_op jit(solution)/shard_map/ppermute | solution.py:15
  81.8 14.5 %collective-permute-start.9 = (bf16[4,4,90,320]{3,1,2,0:T(4,128)(2,1)}, bf16[4,4,90,320]{3,1,2,0:T(4,128)(2,1)}, u32[]{:S(2)}, u32[]{:S(2)}) collective-permute-start(bf16[4,4,90,320]{3,1,2,0:T(4,128)(2,1)} %all-to-all-done.3), channel_id=1, source_target_pairs={{0,1},{1,0},{2,3},{3,2},{4,5},{5,4},{6,7},{7,6},{8,9},{9,8},{10,11... | collective-permute-start | bytes 2764808 | tf_op jit(solution)/shard_map/ppermute | solution.py:15
  90.9 36.6 %all-to-all-start = ((bf16[4,360,320]{1,2,0:T(8,128)(2,1)}), bf16[4,360,320]{1,2,0:T(8,128)(2,1)}, u32[]{:S(2)}, u32[]{:S(2)}) async-start(bf16[4,360,320]{1,2,0:T(8,128)(2,1)} %copy.11), calls=%async_computation | async-start | bytes 1966080 | tf_op jit(solution)/shard_map/all_to_all | solution.py:78
  105.3 1.1 copy-start.8
  106.9 1.1 copy-start.1
  109.3 2.6 %copy-start.4 = (bf16[320,800]{1,0:T(8,128)(2,1)S(1)}, bf16[320,800]{1,0:T(8,128)(2,1)}, u32[]{:S(2)}) copy-start(bf16[320,800]{1,0:T(8,128)(2,1)} %copy-done.3) | copy-start | bytes 1536004
  109.3 55.6 %collective-permute-start.10 = (bf16[320,800]{1,0:T(8,128)(2,1)}, bf16[320,800]{1,0:T(8,128)(2,1)}, u32[]{:S(2)}, u32[]{:S(2)}) collective-permute-start(bf16[320,800]{1,0:T(8,128)(2,1)} %fusion.9), channel_id=1, source_target_pairs={{0,128},{32,160},{64,192},{96,224},{128,256},{160,288},{192,320},{... | collective-permute-start | bytes 1536008 | tf_op jit(solution)/shard_map/ppermute | solution.py:15
  113.2 26.2 %collective-permute-start.12 = (bf16[320,800]{1,0:T(8,128)(2,1)}, bf16[320,800]{1,0:T(8,128)(2,1)}, u32[]{:S(2)}, u32[]{:S(2)}) collective-permute-start(bf16[320,800]{1,0:T(8,128)(2,1)} %fusion.8), channel_id=1, source_target_pairs={{0,224},{32,256},{64,288},{96,320},{128,352},{160,384},{192,416},{... | collective-permute-start | bytes 1536008 | tf_op jit(solution)/shard_map/ppermute | solution.py:15
  119.2 45.8 %collective-permute-start.11 = (bf16[320,800]{1,0:T(8,128)(2,1)}, bf16[320,800]{1,0:T(8,128)(2,1)}, u32[]{:S(2)}, u32[]{:S(2)}) collective-permute-start(bf16[320,800]{1,0:T(8,128)(2,1)} %convolution_convert_fusion), channel_id=1, source_target_pairs={{0,384},{32,416},{64,448},{96,480},{128,0},{160,32},{192,64},{224,... | collective-permute-start | bytes 1536008 | tf_op jit(solution)/shard_map/ppermute | solution.py:15
  129.7 9.7 %copy-start.2 = (bf16[320,800]{1,0:T(8,128)(2,1)S(1)}, bf16[320,800]{1,0:T(8,128)(2,1)}, u32[]{:S(2)}) copy-start(bf16[320,800]{1,0:T(8,128)(2,1)} %copy-done) | copy-start | bytes 1536004
  133.6 19.6 %all-to-all-start.1 = ((bf16[4,90,320]{2,1,0:T(8,128)(2,1)}), bf16[4,90,320]{2,1,0:T(8,128)(2,1)}, u32[]{:S(2)}, u32[]{:S(2)}) async-start(bf16[4,90,320]{2,1,0:T(8,128)(2,1)} %copy.16), calls=%async_computation.1 | async-start | bytes 589824 | tf_op jit(solution)/shard_map/all_to_all | solution.py:78
  139.4 4.9 %copy-start.6 = (f32[320,800]{1,0:T(8,128)S(1)}, f32[320,800]{1,0:T(8,128)}, u32[]{:S(2)}) copy-start(f32[320,800]{1,0:T(8,128)} %fusion.12) | copy-start | bytes 3072004
  142.2 2.6 %copy-start.5 = (bf16[320,800]{1,0:T(8,128)(2,1)S(1)}, bf16[320,800]{1,0:T(8,128)(2,1)}, u32[]{:S(2)}) copy-start(bf16[320,800]{1,0:T(8,128)(2,1)} %copy-done.3) | copy-start | bytes 1536004
  142.2 26.1 %collective-permute-start.13 = (bf16[320,800]{1,0:T(8,128)(2,1)}, bf16[320,800]{1,0:T(8,128)(2,1)}, u32[]{:S(2)}, u32[]{:S(2)}) collective-permute-start(bf16[320,800]{1,0:T(8,128)(2,1)} %fusion.7), channel_id=1, source_target_pairs={{0,480},{32,0},{64,32},{96,64},{128,96},{160,128},{192,160},{224,1... | collective-permute-start | bytes 1536008 | tf_op jit(solution)/shard_map/ppermute | solution.py:15
  154.2 31.6 %copy-start.9 = (f32[320,90]{0,1:T(8,128)S(1)}, f32[320,90]{0,1:T(8,128)}, u32[]{:S(2)}) copy-start(f32[320,90]{0,1:T(8,128)} %param.6) | copy-start | bytes 345604
  154.3 31.5 %collective-permute-start.5 = (bf16[90,320]{1,0:T(8,128)(2,1)S(1)}, bf16[90,320]{1,0:T(8,128)(2,1)S(1)}, u32[]{:S(2)}, u32[]{:S(2)}) collective-permute-start(bf16[90,320]{1,0:T(8,128)(2,1)S(1)} %reduce_sum.25), channel_id=1, source_target_pairs={{0,0},{2,1},{4,2},{6,3},{8,4},{10,5},{12,6},{14,7},{16,200},{18,20... | collective-permute-start | bytes 172808 | tf_op jit(solution)/shard_map/ppermute | solution.py:81
  164.3 21.5 %collective-permute-start.6 = (bf16[90,320]{1,0:T(8,128)(2,1)S(1)}, bf16[90,320]{1,0:T(8,128)(2,1)S(1)}, u32[]{:S(2)}, u32[]{:S(2)}) collective-permute-start(bf16[90,320]{1,0:T(8,128)(2,1)S(1)} %reduce_sum.25), channel_id=1, source_target_pairs={{14,199},{20,490},{28,142},{11,213},{25,156},{46,231},{52,10},{60,... | collective-permute-start | bytes 172808 | tf_op jit(solution)/shard_map/ppermute | solution.py:82

commit v2 on v1

v2 whole, which is shorter than its diff:
```python
import functools

import jax
import jax.numpy as jnp
from jax import lax
from jax.experimental import pallas as pl
from jax.experimental.pallas import tpu as pltpu
from jax.sharding import Mesh
from jax.sharding import PartitionSpec as P

INTER = 25600
COL = ("x", "zh", "core")
ALL = ("row",) + COL
TILES = ((0, 0), (0, -1), (6, 4), (-1, -4), (4, 0), (4, -1), (6, 0), (6, -1), (4, -4))
LATE = tuple(k for k, t in enumerate(TILES) if 6 in t)
EARLY = tuple(k for k, t in enumerate(TILES) if 6 not in t)


def passed_along(x, axis, by):
    count = lax.axis_size(axis)
    return lax.ppermute(x, axis, [(i, (i + by) % count) for i in range(count)])


def shard_routes(sizes, shard, tile):
    nx, nzh, ncore = sizes
    routes = []
    for c in range(nx * nzh * ncore):
        first, last = c * shard // tile, (c * shard + shard - 1) // tile
        core, rest = divmod(c, nx * nzh)
        x, zh = divmod(rest, nzh)
        place = (x * nzh + zh) * ncore + core
        one, two = TILES[first][0], TILES[last][0]
        routes.append((c, place, one, two, last * tile - c * shard if one != two else shard))
    return routes


def dot(left, right, dims):
    return lax.dot_general(left, right, (dims, ((), ())), preferred_element_type=jnp.float32)


def call(kernel, outs, args, scratch=(), flops=0):
    moved = sum(a.size * a.dtype.itemsize for a in args)
    return pl.pallas_call(
        kernel,
        out_shape=[jax.ShapeDtypeStruct(s, d) for s, d in outs],
        in_specs=[pl.BlockSpec(memory_space=pltpu.VMEM)] * len(args),
        out_specs=[pl.BlockSpec(memory_space=pltpu.VMEM)] * len(outs),
        scratch_shapes=list(scratch),
        cost_estimate=pl.CostEstimate(flops=flops, bytes_accessed=moved, transcendentals=0),
        compiler_params=pltpu.CompilerParams(vmem_limit_bytes=48 * 2**20),
    )(*args)


def early_gram(g0, gm1, gm4, g4, out):
    held = {0: g0, -1: gm1, -4: gm4, 4: g4}
    for n, k in enumerate(EARLY):
        a, b = TILES[k]
        out[n] = dot(held[b][...], held[a][...], ((1,), (1,))).astype(out.dtype)


def late_gram(g0, gm1, g4, g6, early, keep, give):
    held = {0: g0, -1: gm1, 4: g4, 6: g6}
    core = lax.axis_index("core")
    rows = early.shape[1]
    half = keep.shape[0]

    def put(low, high):
        for k, (a, b) in enumerate(TILES):
            if k in LATE:
                tile = dot(held[b][...], held[a][...], ((1,), (1,)))
            else:
                tile = early[EARLY.index(k)]
            start = k * rows
            if start + rows <= half:
                low[start : start + rows] = tile.astype(low.dtype)
            elif start >= half:
                high[start - half : start - half + rows] = tile.astype(high.dtype)
            else:
                cut = half - start
                low[start:half] = tile[:cut].astype(low.dtype)
                high[: rows - cut] = tile[cut:].astype(high.dtype)

    @pl.when(core == 0)
    def _():
        put(keep, give)

    @pl.when(core == 1)
    def _():
        put(give, keep)


def core_sum(keep, came, *rest):
    outs, total = rest[:-1], rest[-1]
    count = len(outs)
    part = total.shape[0] // count
    me = lax.axis_index("x")
    total[...] = keep[...] + came[...].astype(jnp.float32)
    for s, out in enumerate(outs):
        start = pl.multiple_of(lax.rem(me + s, count) * part, 8)
        out[...] = total[pl.ds(start, part)].astype(out.dtype)


def x_sum(*rest):
    count = (len(rest) - 1) // 2
    ins, outs, total = rest[:count], rest[count:-1], rest[-1]
    part = outs[0].shape[0]
    me = lax.axis_index("zh")
    value = sum(i[...].astype(jnp.float32) for i in ins)
    for q in range(count):
        total[q, :part] = value[q * part : (q + 1) * part]
    for s, out in enumerate(outs):
        out[...] = total[lax.rem(me + s, count), :part].astype(out.dtype)


def assemble(mine, other, g0, gm1, g4, tiles, out6, flat):
    nx, nzh, shard, rows = mine.shape
    x, zh, core = lax.axis_index("x"), lax.axis_index("zh"), lax.axis_index("core")

    def put(parts):
        for b, part in enumerate(parts):
            for p in range(nx):
                for q in range(nzh):
                    c = (b * nx + p) * nzh + q
                    piece = part[lax.rem(p - x + nx, nx), lax.rem(q - zh + nzh, nzh)]
                    flat[c * shard : (c + 1) * shard] = piece.astype(jnp.float32)

    @pl.when(core == 0)
    def _():
        put((mine, other))

    @pl.when(core == 1)
    def _():
        put((other, mine))

    for k in range(len(TILES)):
        tiles[k] = flat[k * rows : (k + 1) * rows].astype(tiles.dtype)
    out6[...] = summed_terms(tiles, {0: g0, -1: gm1, 4: g4}, 6).astype(out6.dtype)


def summed_terms(tiles, held, o):
    total = None
    for k, (a, b) in enumerate(TILES):
        if a == o:
            term = dot(tiles[k], held[b][...], ((0,), (0,)))
            total = term if total is None else total + term
        if b == o and 0 < k < len(TILES) - 1:
            term = dot(tiles[k], held[a][...], ((1,), (0,)))
            total = term if total is None else total + term
    return total


def products(which, tiles, g0, gm1, gm4, g4, g6, *outs):
    held = {0: g0, -1: gm1, -4: gm4, 4: g4, 6: g6}
    for o, out in zip(which, outs):
        out[...] = summed_terms(tiles, held, o).astype(out.dtype)


def local(gradient, previous, root):
    rows, shard = previous.shape
    n_row = lax.axis_size("row")
    nx, nzh, ncore = (lax.axis_size(a) for a in COL)
    n_col = nx * nzh * ncore
    routes = shard_routes((nx, nzh, ncore), shard, rows)
    cuts = jnp.asarray([r[4] for r in routes], jnp.int32)
    cut = cuts[lax.axis_index(COL)]
    held_cut = cuts[lax.axis_index(("core", "x", "zh"))]
    place_in_shard = lax.broadcasted_iota(jnp.int32, (shard, rows), 0)
    bf16, f32 = jnp.bfloat16, jnp.float32
    product = 2 * rows * rows * gradient.shape[1]

    g0 = gradient.astype(bf16)
    gm1 = passed_along(g0, "row", 1)
    gm4 = passed_along(g0, "row", 4)
    g4 = passed_along(g0, "row", -4)
    g6 = passed_along(gm1, "row", -7)

    to_use = [
        [
            ((i + r[pick]) % n_row * n_col + r[0], i * n_col + r[1])
            for i in range(n_row)
            for r in routes
            if pick == 2 or r[2] != r[3]
        ]
        for pick in (2, 3)
    ]
    mine = root.T
    one = lax.ppermute(mine, ALL, to_use[0])
    two = lax.ppermute(mine, ALL, to_use[1])
    piece = jnp.where(place_in_shard < held_cut, one, two)
    piece = jnp.stack([piece] + [passed_along(piece, "zh", -s) for s in range(1, nzh)])
    piece = jnp.stack([piece] + [passed_along(piece, "x", -s) for s in range(1, nx)])
    other = passed_along(piece, "core", 1)

    (early,) = call(
        early_gram, [((len(EARLY), rows, rows), bf16)], (g0, gm1, gm4, g4), flops=len(EARLY) * product
    )
    half = len(TILES) * rows // ncore
    keep, give = call(
        late_gram,
        [((half, rows), f32), ((half, rows), bf16)],
        (g0, gm1, g4, g6, early),
        flops=len(LATE) * product,
    )
    came = passed_along(give, "core", 1)
    part = half // nx
    sent = call(core_sum, [((part, rows), bf16)] * nx, (keep, came), [pltpu.VMEM((half, rows), f32)])
    got = [sent[0]] + [passed_along(sent[s], "x", s) for s in range(1, nx)]
    padded = -(-shard // 8) * 8
    sent = call(x_sum, [((shard, rows), bf16)] * nzh, got, [pltpu.VMEM((nzh, padded, rows), f32)])
    got = [sent[0]] + [passed_along(sent[s], "zh", s) for s in range(1, nzh)]
    total = sum(a.astype(f32) for a in got).astype(bf16)
    home = [[(b, a) for a, b in pairs] for pairs in to_use]
    one = lax.ppermute(total, ALL, home[0])
    two = lax.ppermute(total, ALL, home[1])
    share = jnp.where(place_in_shard < cut, one, two).astype(f32).T
    statistic = 0.9 * previous + 0.1 / INTER * share

    shape = g0.shape
    tiles, out6 = call(
        assemble,
        [((len(TILES), rows, rows), bf16), (shape, bf16)],
        (piece, other, g0, gm1, g4),
        [pltpu.VMEM((len(TILES) * rows, rows), f32)],
        flops=3 * product,
    )
    operands = (tiles, g0, gm1, gm4, g4, g6)
    came6 = passed_along(out6, "row", 7)
    out4, outm4 = call(
        functools.partial(products, (4, -4)), [(shape, bf16)] * 2, operands, flops=5 * product
    )
    came4, camem4 = passed_along(out4, "row", 4), passed_along(outm4, "row", -4)
    outm1, out0 = call(
        functools.partial(products, (-1, 0)), [(shape, f32)] * 2, operands, flops=8 * product
    )
    chained = passed_along((outm1 + came6.astype(f32)).astype(bf16), "row", -1)
    applied = out0 + came4.astype(f32) + camem4.astype(f32) + chained.astype(f32)
    return (statistic, applied)


def solution(mesh):
    split = Mesh(mesh.devices.reshape(mesh.shape["row"], 4, 4, 2), ALL)
    spec = P("row", COL)
    return jax.shard_map(
        local, mesh=split, in_specs=(spec,) * 3, out_specs=(spec,) * 2, check_vma=False
    )
```

time: 188 us -> 206 us (1.096)
  the two profiles are of different devices: /device:TPU:35 before, /device:TPU:165 now
where the time goes in v2:
time: 206 us; the launch traced here: 205 us
  starting transfers between devices  106 us (51%)
  waiting for transfers between devices  65.8 us (32%)
  Pallas kernels  14.8 us (7%)
  local copies, waits for them, and re-layouts  12.1 us (6%)
  other arithmetic  5.13 us (2%)
    ppermute x22, starting transfers between devices, passed_along(): return lax.ppermute(x, axis, [(i, (i + by) % count) for i in range(count)])  90.6 us
    ppermute x22, waiting for transfers between devices, passed_along(): return lax.ppermute(x, axis, [(i, (i + by) % count) for i in range(count)])  50.6 us
    ppermute x1, waiting for transfers between devices, local(): one = lax.ppermute(total, ALL, home[0])  15.2 us
    pallas_call x7, Pallas kernels, call(): pl.pallas_call(kernel, out_shape=[jax.ShapeDtypeStruct(s, d) for s, d in...  14.8 us
    ppermute x1, starting transfers between devices, local(): one = lax.ppermute(mine, ALL, to_use[0])  12.1 us
  transfers between devices with their start and end apart: 26, of which 6 were waited for; matrix products, arithmetic and copies ran while one was open for 6% of the time, Pallas kernels for 7%

profile of v2, /device:TPU:165, one launch (start us, length us, event | category | flops | bytes accessed | tf_op | source)
XLA Modules:
  0.0 204.9 jit_solution(17324244506264029884)
XLA Ops:
  0.6 0.0 copy-start.7
  0.6 12.1 %collective-permute-start.13 = (bf16[90,320]{1,0:T(8,128)(2,1)}, bf16[90,320]{1,0:T(8,128)(2,1)S(1)}, u32[]{:S(2)}, u32[]{:S(2)}) collective-permute-start(bf16[90,320]{1,0:T(8,128)(2,1)} %bitcast.21), channel_id=1, source_target_pairs={{0,0},{1,2},{2,4},{3,6},{4,8},{5,10},{6,12},{7,14},{200,16},{201,1... | collective-permute-start | bytes 172808 | tf_op jit(solution)/shard_map/ppermute | solution.py:187
  12.8 0.7 collective-permute-start.14
  13.5 1.3 convert_element_type.36.g0
  14.8 2.6 %collective-permute-start = (bf16[320,800]{1,0:T(8,128)(2,1)S(1)}, bf16[320,800]{1,0:T(8,128)(2,1)S(1)}, u32[]{:S(2)}, u32[]{:S(2)}) collective-permute-start(bf16[320,800]{1,0:T(8,128)(2,1)S(1)} %convert_element_type.36.g0), channel_id=1, source_target_pairs={{0,32},{32,64},{64,96},{96,128},{128,160},{160,192},{192,224},{224... | collective-permute-start | bytes 1536008 | tf_op jit(solution)/shard_map/ppermute | solution.py:21
  17.5 0.6 fusion.1
  18.0 0.6 iota_compare_fusion
  18.7 0.0 collective-permute-done.14
  18.7 0.1 broadcast_select_fusion
  18.8 19.3 %collective-permute-start.17 = (bf16[90,320]{1,0:T(8,128)(2,1)S(1)}, bf16[90,320]{1,0:T(8,128)(2,1)S(1)}, u32[]{:S(2)}, u32[]{:S(2)}) collective-permute-start(bf16[90,320]{1,0:T(8,128)(2,1)S(1)} %broadcast_select_fusion), channel_id=1, source_target_pairs={{0,2},{2,4},{4,6},{6,0},{1,3},{3,5},{5,7},{7,1},{8,10},{10,12},{12... | collective-permute-start | bytes 172808 | tf_op jit(solution)/shard_map/ppermute | solution.py:21
  38.1 1.9 collective-permute-start.16
  40.0 7.0 %collective-permute-start.15 = (bf16[90,320]{1,0:T(8,128)(2,1)S(1)}, bf16[90,320]{1,0:T(8,128)(2,1)S(1)}, u32[]{:S(2)}, u32[]{:S(2)}) collective-permute-start(bf16[90,320]{1,0:T(8,128)(2,1)S(1)} %broadcast_select_fusion), channel_id=1, source_target_pairs={{0,6},{2,0},{4,2},{6,4},{1,7},{3,1},{5,3},{7,5},{8,14},{10,8},{12,... | collective-permute-start | bytes 172808 | tf_op jit(solution)/shard_map/ppermute | solution.py:21
  47.0 0.0 collective-permute-done.17
  47.1 6.2 %collective-permute-done.16 = bf16[90,320]{1,0:T(8,128)(2,1)S(1)} collective-permute-done((bf16[90,320]{1,0:T(8,128)(2,1)S(1)}, bf16[90,320]{1,0:T(8,128)(2,1)S(1)}, u32[]{:S(2)}, u32[]{:S(2)}) %collective-permute-start.16) | collective-permute-done | bytes 57632 | tf_op jit(solution)/shard_map/ppermute | solution.py:21
  53.2 0.0 collective-permute-done.15
  53.2 0.1 fusion
  53.3 1.9 collective-permute-start.20
  55.3 1.9 collective-permute-start.19
  57.2 3.4 %collective-permute-start.18 = (bf16[4,90,320]{2,1,0:T(8,128)(2,1)S(1)}, bf16[4,90,320]{2,1,0:T(8,128)(2,1)S(1)}, u32[]{:S(2)}, u32[]{:S(2)}) collective-permute-start(bf16[4,90,320]{2,1,0:T(8,128)(2,1)S(1)} %get-tuple-element.35), channel_id=1, source_target_pairs={{0,24},{8,0},{16,8},{24,16},{1,25},{9,1},{17,9},{25,17},{2,26},{10... | collective-permute-start | bytes 691208 | tf_op jit(solution)/shard_map/ppermute | solution.py:21
  60.6 2.2 %collective-permute-start.1 = (bf16[320,800]{1,0:T(8,128)(2,1)S(1)}, bf16[320,800]{1,0:T(8,128)(2,1)S(1)}, u32[]{:S(2)}, u32[]{:S(2)}) collective-permute-start(bf16[320,800]{1,0:T(8,128)(2,1)S(1)} %convert_element_type.36.g0), channel_id=1, source_target_pairs={{0,384},{32,416},{64,448},{96,480},{128,0},{160,32},{192,64},{224,... | collective-permute-start | bytes 1536008 | tf_op jit(solution)/shard_map/ppermute | solution.py:21
  62.8 4.6 %collective-permute-done.20 = bf16[4,90,320]{2,1,0:T(8,128)(2,1)S(1)} collective-permute-done((bf16[4,90,320]{2,1,0:T(8,128)(2,1)S(1)}, bf16[4,90,320]{2,1,0:T(8,128)(2,1)S(1)}, u32[]{:S(2)}, u32[]{:S(2)}) %collective-permute-start.20) | collective-permute-done | bytes 230432 | tf_op jit(solution)/shard_map/ppermute | solution.py:21
  67.4 1.9 collective-permute-start.3
  69.3 0.0 collective-permute-done.gm1
  69.3 4.2 %collective-permute-start.2 = (bf16[320,800]{1,0:T(8,128)(2,1)S(1)}, bf16[320,800]{1,0:T(8,128)(2,1)S(1)}, u32[]{:S(2)}, u32[]{:S(2)}) collective-permute-start(bf16[320,800]{1,0:T(8,128)(2,1)S(1)} %collective-permute-done.gm1), channel_id=1, source_target_pairs={{0,288},{32,320},{64,352},{96,384},{128,416},{160,448},{192,480},{... | collective-permute-start | bytes 1536008 | tf_op jit(solution)/shard_map/ppermute | solution.py:21
  73.6 0.0 collective-permute-done.18
  73.6 0.3 pad_maximum_fusion.mine
  73.9 1.6 copy.8
  75.4 3.7 %collective-permute-start.21 = (bf16[4,4,90,320]{3,1,2,0:T(4,128)(2,1)}, bf16[4,4,90,320]{3,1,2,0:T(4,128)(2,1)}, u32[]{:S(2)}, u32[]{:S(2)}) collective-permute-start(bf16[4,4,90,320]{3,1,2,0:T(4,128)(2,1)} %copy.8), channel_id=1, source_target_pairs={{0,1},{1,0},{2,3},{3,2},{4,5},{5,4},{6,7},{7,6},{8,9},{9,8},{10,11... | collective-permute-start | bytes 2764808 | tf_op jit(solution)/shard_map/ppermute | solution.py:21
  79.1 9.0 %collective-permute-done.1.g4 = bf16[320,800]{1,0:T(8,128)(2,1)S(1)} collective-permute-done((bf16[320,800]{1,0:T(8,128)(2,1)S(1)}, bf16[320,800]{1,0:T(8,128)(2,1)S(1)}, u32[]{:S(2)}, u32[]{:S(2)}) %collective-permute-start.1) | collective-permute-done | bytes 512032 | tf_op jit(solution)/shard_map/ppermute | solution.py:21
  88.2 6.0 %collective-permute-done.3.gm4 = bf16[320,800]{1,0:T(8,128)(2,1)S(1)} collective-permute-done((bf16[320,800]{1,0:T(8,128)(2,1)S(1)}, bf16[320,800]{1,0:T(8,128)(2,1)S(1)}, u32[]{:S(2)}, u32[]{:S(2)}) %collective-permute-start.3) | collective-permute-done | bytes 512032 | tf_op jit(solution)/shard_map/ppermute | solution.py:21
  94.1 2.1 %shard_map.59.early = bf16[6,320,320]{2,1,0:T(8,128)(2,1)S(1)} custom-call(bf16[320,800]{1,0:T(8,128)(2,1)S(1)} %convert_element_type.36.g0, bf16[320,800]{1,0:T(8,128)(2,1)S(1)} %collective-permute-done.gm1, bf16[320,800]{1,0:T(8,128)(2,1)S(1)} %collective-permute-done.3.gm4, bf16[320,800]{1,0:T(8,128)(2,1)S(1)} %collective-permute-done.1.g4), custom_call_target="tpu_custom_call" | custom-call | flops 983040000 | bytes 2048000 | tf_op jit(solution)/shard_map/pallas_call | solution.py:43
  96.3 0.0 collective-permute-done.2.g6
  96.3 2.6 %shard_map.60 = (f32[1440,320]{1,0:T(8,128)}, bf16[1440,320]{1,0:T(8,128)(2,1)S(1)}) custom-call(bf16[320,800]{1,0:T(8,128)(2,1)S(1)} %convert_element_type.36.g0, bf16[320,800]{1,0:T(8,128)(2,1)S(1)} %collective-permute-done.gm1, bf16[320,800]{1,0:T(8,128)(2,1)S(1)} %collective-permute-done.1.g4, bf16[320,800]{1,0:T(8,128)(2,1)S(1)} %collective-permute-done.2.g6, ...), custom_call_target="tpu_custom_call" | custom-call | flops 491520000 | bytes 3276800 | tf_op jit(solution)/shard_map/pallas_call | solution.py:43
  98.9 1.0 copy-done.5
  99.8 2.3 %copy.6 = bf16[1440,320]{0,1:T(8,128)(2,1)} copy(bf16[1440,320]{1,0:T(8,128)(2,1)} %copy-done.5) | data formatting | bytes 1843200 | tf_op jit(solution)/shard_map/pallas_call | solution.py:43
  102.2 1.9 collective-permute-start.4
  104.1 1.4 copy.9.other
  105.5 3.2 %shard_map.63 = (bf16[9,320,320]{2,1,0:T(8,128)(2,1)}, bf16[320,800]{1,0:T(8,128)(2,1)}) custom-call(bf16[4,4,90,320]{3,2,1,0:T(8,128)(2,1)S(1)} %pad_maximum_fusion.mine, bf16[4,4,90,320]{3,2,1,0:T(8,128)(2,1)S(1)} %copy.9.other, bf16[320,800]{1,0:T(8,128)(2,1)S(1)} %convert_element_type.36.g0, bf16[320,800]{1,0:T(8,128)(2,1)S(1)} %collective-permute-done.gm1, ...), custom_call_target="tpu_custom_call" | custom-call | flops 491520000 | bytes 3379200 | tf_op jit(solution)/shard_map/pallas_call | solution.py:43
  108.7 1.9 collective-permute-start.24
  110.6 2.3 %copy.7.came = bf16[1440,320]{1,0:T(8,128)(2,1)} copy(bf16[1440,320]{0,1:T(8,128)(2,1)} %collective-permute-done.4) | data formatting | bytes 1843200 | tf_op jit(solution)/shard_map/ppermute | solution.py:21
  113.0 1.2 copy-done.3
  114.2 1.6 copy-done.4
  115.8 0.5 shard_map.61
  116.3 3.5 %collective-permute-start.5 = (bf16[360,320]{1,0:T(8,128)(2,1)S(1)}, bf16[360,320]{1,0:T(8,128)(2,1)S(1)}, u32[]{:S(2)}, u32[]{:S(2)}) collective-permute-start(bf16[360,320]{1,0:T(8,128)(2,1)S(1)} %get-tuple-element.21), channel_id=1, source_target_pairs={{0,8},{8,16},{16,24},{24,0},{1,9},{9,17},{17,25},{25,1},{2,10},{10... | collective-permute-start | bytes 691208 | tf_op jit(solution)/shard_map/ppermute | solution.py:21
  119.8 4.4 %collective-permute-start.6 = (bf16[360,320]{1,0:T(8,128)(2,1)S(1)}, bf16[360,320]{1,0:T(8,128)(2,1)S(1)}, u32[]{:S(2)}, u32[]{:S(2)}) collective-permute-start(bf16[360,320]{1,0:T(8,128)(2,1)S(1)} %get-tuple-element.22), channel_id=1, source_target_pairs={{0,16},{8,24},{16,0},{24,8},{1,17},{9,25},{17,1},{25,9},{2,18},{10... | collective-permute-start | bytes 691208 | tf_op jit(solution)/shard_map/ppermute | solution.py:21
  124.2 2.5 %collective-permute-start.7 = (bf16[360,320]{1,0:T(8,128)(2,1)S(1)}, bf16[360,320]{1,0:T(8,128)(2,1)S(1)}, u32[]{:S(2)}, u32[]{:S(2)}) collective-permute-start(bf16[360,320]{1,0:T(8,128)(2,1)S(1)} %get-tuple-element.23), channel_id=1, source_target_pairs={{0,24},{8,0},{16,8},{24,16},{1,25},{9,1},{17,9},{25,17},{2,26},{10... | collective-permute-start | bytes 691208 | tf_op jit(solution)/shard_map/ppermute | solution.py:21
  126.7 1.8 shard_map.65
  128.5 2.2 %collective-permute-start.23 = (bf16[320,800]{1,0:T(8,128)(2,1)S(1)}, bf16[320,800]{1,0:T(8,128)(2,1)S(1)}, u32[]{:S(2)}, u32[]{:S(2)}) collective-permute-start(bf16[320,800]{1,0:T(8,128)(2,1)S(1)} %get-tuple-element.31), channel_id=1, source_target_pairs={{0,384},{32,416},{64,448},{96,480},{128,0},{160,32},{192,64},{224,... | collective-permute-start | bytes 1536008 | tf_op jit(solution)/shard_map/ppermute | solution.py:21
  130.7 4.4 %shard_map.64 = (f32[320,800]{1,0:T(8,128)S(1)}, f32[320,800]{1,0:T(8,128)S(1)}) custom-call(bf16[9,320,320]{2,1,0:T(8,128)(2,1)} %get-tuple-element.28.tiles, bf16[320,800]{1,0:T(8,128)(2,1)S(1)} %convert_element_type.36.g0, bf16[320,800]{1,0:T(8,128)(2,1)S(1)} %collective-permute-done.gm1, bf16[320,800]{1,0:T(8,128)(2,1)S(1)} %collective-permute-done.3.gm4, ...), custom_call_target="tpu_custom_call" | custom-call | flops 1310720000 | bytes 4403200 | tf_op jit(solution)/shard_map/pallas_call | solution.py:43
  135.1 3.9 %collective-permute-start.22 = (bf16[320,800]{1,0:T(8,128)(2,1)S(1)}, bf16[320,800]{1,0:T(8,128)(2,1)S(1)}, u32[]{:S(2)}, u32[]{:S(2)}) collective-permute-start(bf16[320,800]{1,0:T(8,128)(2,1)S(1)} %get-tuple-element.30), channel_id=1, source_target_pairs={{0,128},{32,160},{64,192},{96,224},{128,256},{160,288},{192,320},{... | collective-permute-start | bytes 1536008 | tf_op jit(solution)/shard_map/ppermute | solution.py:21
  139.0 0.3 shard_map.62
  139.3 4.4 %collective-permute-start.10 = (bf16[90,320]{1,0:T(8,128)(2,1)S(1)}, bf16[90,320]{1,0:T(8,128)(2,1)S(1)}, u32[]{:S(2)}, u32[]{:S(2)}) collective-permute-start(bf16[90,320]{1,0:T(8,128)(2,1)S(1)} %get-tuple-element.27), channel_id=1, source_target_pairs={{0,6},{2,0},{4,2},{6,4},{1,7},{3,1},{5,3},{7,5},{8,14},{10,8},{12,... | collective-permute-start | bytes 172808 | tf_op jit(solution)/shard_map/ppermute | solution.py:21
  143.7 8.9 %collective-permute-start.9 = (bf16[90,320]{1,0:T(8,128)(2,1)S(1)}, bf16[90,320]{1,0:T(8,128)(2,1)S(1)}, u32[]{:S(2)}, u32[]{:S(2)}) collective-permute-start(bf16[90,320]{1,0:T(8,128)(2,1)S(1)} %get-tuple-element.26), channel_id=1, source_target_pairs={{0,4},{2,6},{4,0},{6,2},{1,5},{3,7},{5,1},{7,3},{8,12},{10,14},{12... | collective-permute-start | bytes 172808 | tf_op jit(solution)/shard_map/ppermute | solution.py:21
  152.6 2.0 collective-permute-start.8
  154.6 0.0 copy-start.6
  154.6 0.1 add_convert_fusion
  154.7 5.1 %collective-permute-start.25 = (bf16[320,800]{1,0:T(8,128)(2,1)S(1)}, bf16[320,800]{1,0:T(8,128)(2,1)S(1)}, u32[]{:S(2)}, u32[]{:S(2)}) collective-permute-start(bf16[320,800]{1,0:T(8,128)(2,1)S(1)} %add_convert_fusion), channel_id=1, source_target_pairs={{0,480},{32,0},{64,32},{96,64},{128,96},{160,128},{192,160},{224,1... | collective-permute-start | bytes 1536008 | tf_op jit(solution)/shard_map/ppermute | solution.py:21
  159.8 24.7 %collective-permute-done.8 = bf16[90,320]{1,0:T(8,128)(2,1)S(1)} collective-permute-done((bf16[90,320]{1,0:T(8,128)(2,1)S(1)}, bf16[90,320]{1,0:T(8,128)(2,1)S(1)}, u32[]{:S(2)}, u32[]{:S(2)}) %collective-permute-start.8) | collective-permute-done | bytes 57632 | tf_op jit(solution)/shard_map/ppermute | solution.py:21
  184.5 1.9 collective-permute-start.11
  186.5 0.7 collective-permute-start.12
  187.1 0.6 iota_compare_fusion.1
  187.7 15.2 %collective-permute-done.11 = bf16[90,320]{1,0:T(8,128)(2,1)S(1)} collective-permute-done((bf16[90,320]{1,0:T(8,128)(2,1)S(1)}, bf16[90,320]{1,0:T(8,128)(2,1)S(1)}, u32[]{:S(2)}, u32[]{:S(2)}) %collective-permute-start.11) | collective-permute-done | bytes 57632 | tf_op jit(solution)/shard_map/ppermute | solution.py:213
  202.9 0.8 bitcast_add_fusion
  203.6 1.2 convert_add_fusion
  (26 shorter events, 0.1 us)
Async XLA Ops:
  0.6 16.8 %copy-start.7 = (s32[32]{0:T(128)S(1)}, s32[32]{0:T(128)}, u32[]{:S(2)}) copy-start(s32[32]{0:T(128)} %constant.29.clone) | copy-start | bytes 388
  0.6 18.1 %collective-permute-start.13 = (bf16[90,320]{1,0:T(8,128)(2,1)}, bf16[90,320]{1,0:T(8,128)(2,1)S(1)}, u32[]{:S(2)}, u32[]{:S(2)}) collective-permute-start(bf16[90,320]{1,0:T(8,128)(2,1)} %bitcast.21), channel_id=1, source_target_pairs={{0,0},{1,2},{2,4},{3,6},{4,8},{5,10},{6,12},{7,14},{200,16},{201,1... | collective-permute-start | bytes 172808 | tf_op jit(solution)/shard_map/ppermute | solution.py:187
  12.8 5.9 %collective-permute-start.14 = (bf16[90,320]{1,0:T(8,128)(2,1)}, bf16[90,320]{1,0:T(8,128)(2,1)S(1)}, u32[]{:S(2)}, u32[]{:S(2)}) collective-permute-start(bf16[90,320]{1,0:T(8,128)(2,1)} %bitcast.22), channel_id=1, source_target_pairs={{199,14},{490,20},{142,28},{213,11},{156,25},{231,46},{10,52},{174... | collective-permute-start | bytes 172808 | tf_op jit(solution)/shard_map/ppermute | solution.py:188
  14.8 54.6 %collective-permute-start = (bf16[320,800]{1,0:T(8,128)(2,1)S(1)}, bf16[320,800]{1,0:T(8,128)(2,1)S(1)}, u32[]{:S(2)}, u32[]{:S(2)}) collective-permute-start(bf16[320,800]{1,0:T(8,128)(2,1)S(1)} %convert_element_type.36.g0), channel_id=1, source_target_pairs={{0,32},{32,64},{64,96},{96,128},{128,160},{160,192},{192,224},{224... | collective-permute-start | bytes 1536008 | tf_op jit(solution)/shard_map/ppermute | solution.py:21
  18.8 28.2 %collective-permute-start.17 = (bf16[90,320]{1,0:T(8,128)(2,1)S(1)}, bf16[90,320]{1,0:T(8,128)(2,1)S(1)}, u32[]{:S(2)}, u32[]{:S(2)}) collective-permute-start(bf16[90,320]{1,0:T(8,128)(2,1)S(1)} %broadcast_select_fusion), channel_id=1, source_target_pairs={{0,2},{2,4},{4,6},{6,0},{1,3},{3,5},{5,7},{7,1},{8,10},{10,12},{12... | collective-permute-start | bytes 172808 | tf_op jit(solution)/shard_map/ppermute | solution.py:21
  38.1 15.1 %collective-permute-start.16 = (bf16[90,320]{1,0:T(8,128)(2,1)S(1)}, bf16[90,320]{1,0:T(8,128)(2,1)S(1)}, u32[]{:S(2)}, u32[]{:S(2)}) collective-permute-start(bf16[90,320]{1,0:T(8,128)(2,1)S(1)} %broadcast_select_fusion), channel_id=1, source_target_pairs={{0,4},{2,6},{4,0},{6,2},{1,5},{3,7},{5,1},{7,3},{8,12},{10,14},{12... | collective-permute-start | bytes 172808 | tf_op jit(solution)/shard_map/ppermute | solution.py:21
  40.0 13.2 %collective-permute-start.15 = (bf16[90,320]{1,0:T(8,128)(2,1)S(1)}, bf16[90,320]{1,0:T(8,128)(2,1)S(1)}, u32[]{:S(2)}, u32[]{:S(2)}) collective-permute-start(bf16[90,320]{1,0:T(8,128)(2,1)S(1)} %broadcast_select_fusion), channel_id=1, source_target_pairs={{0,6},{2,0},{4,2},{6,4},{1,7},{3,1},{5,3},{7,5},{8,14},{10,8},{12,... | collective-permute-start | bytes 172808 | tf_op jit(solution)/shard_map/ppermute | solution.py:21
  53.3 14.1 %collective-permute-start.20 = (bf16[4,90,320]{2,1,0:T(8,128)(2,1)S(1)}, bf16[4,90,320]{2,1,0:T(8,128)(2,1)S(1)}, u32[]{:S(2)}, u32[]{:S(2)}) collective-permute-start(bf16[4,90,320]{2,1,0:T(8,128)(2,1)S(1)} %get-tuple-element.35), channel_id=1, source_target_pairs={{0,8},{8,16},{16,24},{24,0},{1,9},{9,17},{17,25},{25,1},{2,10},{10... | collective-permute-start | bytes 691208 | tf_op jit(solution)/shard_map/ppermute | solution.py:21
  55.3 18.3 %collective-permute-start.19 = (bf16[4,90,320]{2,1,0:T(8,128)(2,1)S(1)}, bf16[4,90,320]{2,1,0:T(8,128)(2,1)S(1)}, u32[]{:S(2)}, u32[]{:S(2)}) collective-permute-start(bf16[4,90,320]{2,1,0:T(8,128)(2,1)S(1)} %get-tuple-element.35), channel_id=1, source_target_pairs={{0,16},{8,24},{16,0},{24,8},{1,17},{9,25},{17,1},{25,9},{2,18},{10... | collective-permute-start | bytes 691208 | tf_op jit(solution)/shard_map/ppermute | solution.py:21
  57.2 16.4 %collective-permute-start.18 = (bf16[4,90,320]{2,1,0:T(8,128)(2,1)S(1)}, bf16[4,90,320]{2,1,0:T(8,128)(2,1)S(1)}, u32[]{:S(2)}, u32[]{:S(2)}) collective-permute-start(bf16[4,90,320]{2,1,0:T(8,128)(2,1)S(1)} %get-tuple-element.35), channel_id=1, source_target_pairs={{0,24},{8,0},{16,8},{24,16},{1,25},{9,1},{17,9},{25,17},{2,26},{10... | collective-permute-start | bytes 691208 | tf_op jit(solution)/shard_map/ppermute | solution.py:21
  60.6 27.6 %collective-permute-start.1 = (bf16[320,800]{1,0:T(8,128)(2,1)S(1)}, bf16[320,800]{1,0:T(8,128)(2,1)S(1)}, u32[]{:S(2)}, u32[]{:S(2)}) collective-permute-start(bf16[320,800]{1,0:T(8,128)(2,1)S(1)} %convert_element_type.36.g0), channel_id=1, source_target_pairs={{0,384},{32,416},{64,448},{96,480},{128,0},{160,32},{192,64},{224,... | collective-permute-start | bytes 1536008 | tf_op jit(solution)/shard_map/ppermute | solution.py:21
  67.4 26.7 %collective-permute-start.3 = (bf16[320,800]{1,0:T(8,128)(2,1)S(1)}, bf16[320,800]{1,0:T(8,128)(2,1)S(1)}, u32[]{:S(2)}, u32[]{:S(2)}) collective-permute-start(bf16[320,800]{1,0:T(8,128)(2,1)S(1)} %convert_element_type.36.g0), channel_id=1, source_target_pairs={{0,128},{32,160},{64,192},{96,224},{128,256},{160,288},{192,320},{... | collective-permute-start | bytes 1536008 | tf_op jit(solution)/shard_map/ppermute | solution.py:21
  69.3 26.9 %collective-permute-start.2 = (bf16[320,800]{1,0:T(8,128)(2,1)S(1)}, bf16[320,800]{1,0:T(8,128)(2,1)S(1)}, u32[]{:S(2)}, u32[]{:S(2)}) collective-permute-start(bf16[320,800]{1,0:T(8,128)(2,1)S(1)} %collective-permute-done.gm1), channel_id=1, source_target_pairs={{0,288},{32,320},{64,352},{96,384},{128,416},{160,448},{192,480},{... | collective-permute-start | bytes 1536008 | tf_op jit(solution)/shard_map/ppermute | solution.py:21
  75.4 28.7 %collective-permute-start.21 = (bf16[4,4,90,320]{3,1,2,0:T(4,128)(2,1)}, bf16[4,4,90,320]{3,1,2,0:T(4,128)(2,1)}, u32[]{:S(2)}, u32[]{:S(2)}) collective-permute-start(bf16[4,4,90,320]{3,1,2,0:T(4,128)(2,1)} %copy.8), channel_id=1, source_target_pairs={{0,1},{1,0},{2,3},{3,2},{4,5},{5,4},{6,7},{7,6},{8,9},{9,8},{10,11... | collective-permute-start | bytes 2764808 | tf_op jit(solution)/shard_map/ppermute | solution.py:21
  96.3 2.6 %copy-start.1 = (bf16[320,800]{1,0:T(8,128)(2,1)}, bf16[320,800]{1,0:T(8,128)(2,1)S(1)}, u32[]{:S(2)}) copy-start(bf16[320,800]{1,0:T(8,128)(2,1)S(1)} %collective-permute-done.2.g6) | copy-start | bytes 1536004
  98.9 1.0 copy-start.5
  102.2 8.5 %collective-permute-start.4 = (bf16[1440,320]{0,1:T(8,128)(2,1)}, bf16[1440,320]{0,1:T(8,128)(2,1)}, u32[]{:S(2)}, u32[]{:S(2)}) collective-permute-start(bf16[1440,320]{0,1:T(8,128)(2,1)} %copy.6), channel_id=1, source_target_pairs={{0,1},{1,0},{2,3},{3,2},{4,5},{5,4},{6,7},{7,6},{8,9},{9,8},{10,11... | collective-permute-start | bytes 2764808 | tf_op jit(solution)/shard_map/ppermute | solution.py:21
  108.7 43.9 %collective-permute-start.24 = (bf16[320,800]{1,0:T(8,128)(2,1)}, bf16[320,800]{1,0:T(8,128)(2,1)S(1)}, u32[]{:S(2)}, u32[]{:S(2)}) collective-permute-start(bf16[320,800]{1,0:T(8,128)(2,1)} %get-tuple-element.33), channel_id=1, source_target_pairs={{0,224},{32,256},{64,288},{96,320},{128,352},{160,384},{192,416},{... | collective-permute-start | bytes 1536008 | tf_op jit(solution)/shard_map/ppermute | solution.py:21
  113.0 1.2 copy-start.3
  114.2 1.6 copy-start.4
  115.8 10.8 %copy-start = (bf16[9,320,320]{2,1,0:T(8,128)(2,1)S(1)}, bf16[9,320,320]{2,1,0:T(8,128)(2,1)}, u32[]{:S(2)}) copy-start(bf16[9,320,320]{2,1,0:T(8,128)(2,1)} %get-tuple-element.28.tiles) | copy-start | bytes 5529604
  115.8 10.8 %copy-start.2 = (bf16[320,800]{1,0:T(8,128)(2,1)S(1)}, bf16[320,800]{1,0:T(8,128)(2,1)}, u32[]{:S(2)}) copy-start(bf16[320,800]{1,0:T(8,128)(2,1)} %copy-done.1) | copy-start | bytes 1536004
  116.3 18.8 %collective-permute-start.5 = (bf16[360,320]{1,0:T(8,128)(2,1)S(1)}, bf16[360,320]{1,0:T(8,128)(2,1)S(1)}, u32[]{:S(2)}, u32[]{:S(2)}) collective-permute-start(bf16[360,320]{1,0:T(8,128)(2,1)S(1)} %get-tuple-element.21), channel_id=1, source_target_pairs={{0,8},{8,16},{16,24},{24,0},{1,9},{9,17},{17,25},{25,1},{2,10},{10... | collective-permute-start | bytes 691208 | tf_op jit(solution)/shard_map/ppermute | solution.py:21
  119.8 19.2 %collective-permute-start.6 = (bf16[360,320]{1,0:T(8,128)(2,1)S(1)}, bf16[360,320]{1,0:T(8,128)(2,1)S(1)}, u32[]{:S(2)}, u32[]{:S(2)}) collective-permute-start(bf16[360,320]{1,0:T(8,128)(2,1)S(1)} %get-tuple-element.22), channel_id=1, source_target_pairs={{0,16},{8,24},{16,0},{24,8},{1,17},{9,25},{17,1},{25,9},{2,18},{10... | collective-permute-start | bytes 691208 | tf_op jit(solution)/shard_map/ppermute | solution.py:21
  124.2 14.8 %collective-permute-start.7 = (bf16[360,320]{1,0:T(8,128)(2,1)S(1)}, bf16[360,320]{1,0:T(8,128)(2,1)S(1)}, u32[]{:S(2)}, u32[]{:S(2)}) collective-permute-start(bf16[360,320]{1,0:T(8,128)(2,1)S(1)} %get-tuple-element.23), channel_id=1, source_target_pairs={{0,24},{8,0},{16,8},{24,16},{1,25},{9,1},{17,9},{25,17},{2,26},{10... | collective-permute-start | bytes 691208 | tf_op jit(solution)/shard_map/ppermute | solution.py:21
  128.5 75.1 %collective-permute-start.23 = (bf16[320,800]{1,0:T(8,128)(2,1)S(1)}, bf16[320,800]{1,0:T(8,128)(2,1)S(1)}, u32[]{:S(2)}, u32[]{:S(2)}) collective-permute-start(bf16[320,800]{1,0:T(8,128)(2,1)S(1)} %get-tuple-element.31), channel_id=1, source_target_pairs={{0,384},{32,416},{64,448},{96,480},{128,0},{160,32},{192,64},{224,... | collective-permute-start | bytes 1536008 | tf_op jit(solution)/shard_map/ppermute | solution.py:21
  135.1 68.5 %collective-permute-start.22 = (bf16[320,800]{1,0:T(8,128)(2,1)S(1)}, bf16[320,800]{1,0:T(8,128)(2,1)S(1)}, u32[]{:S(2)}, u32[]{:S(2)}) collective-permute-start(bf16[320,800]{1,0:T(8,128)(2,1)S(1)} %get-tuple-element.30), channel_id=1, source_target_pairs={{0,128},{32,160},{64,192},{96,224},{128,256},{160,288},{192,320},{... | collective-permute-start | bytes 1536008 | tf_op jit(solution)/shard_map/ppermute | solution.py:21
  139.3 15.4 %collective-permute-start.10 = (bf16[90,320]{1,0:T(8,128)(2,1)S(1)}, bf16[90,320]{1,0:T(8,128)(2,1)S(1)}, u32[]{:S(2)}, u32[]{:S(2)}) collective-permute-start(bf16[90,320]{1,0:T(8,128)(2,1)S(1)} %get-tuple-element.27), channel_id=1, source_target_pairs={{0,6},{2,0},{4,2},{6,4},{1,7},{3,1},{5,3},{7,5},{8,14},{10,8},{12,... | collective-permute-start | bytes 172808 | tf_op jit(solution)/shard_map/ppermute | solution.py:21
  143.7 16.1 %collective-permute-start.9 = (bf16[90,320]{1,0:T(8,128)(2,1)S(1)}, bf16[90,320]{1,0:T(8,128)(2,1)S(1)}, u32[]{:S(2)}, u32[]{:S(2)}) collective-permute-start(bf16[90,320]{1,0:T(8,128)(2,1)S(1)} %get-tuple-element.26), channel_id=1, source_target_pairs={{0,4},{2,6},{4,0},{6,2},{1,5},{3,7},{5,1},{7,3},{8,12},{10,14},{12... | collective-permute-start | bytes 172808 | tf_op jit(solution)/shard_map/ppermute | solution.py:21
  152.6 31.9 %collective-permute-start.8 = (bf16[90,320]{1,0:T(8,128)(2,1)S(1)}, bf16[90,320]{1,0:T(8,128)(2,1)S(1)}, u32[]{:S(2)}, u32[]{:S(2)}) collective-permute-start(bf16[90,320]{1,0:T(8,128)(2,1)S(1)} %get-tuple-element.25), channel_id=1, source_target_pairs={{0,2},{2,4},{4,6},{6,0},{1,3},{3,5},{5,7},{7,1},{8,10},{10,12},{12... | collective-permute-start | bytes 172808 | tf_op jit(solution)/shard_map/ppermute | solution.py:21
  154.6 48.3 %copy-start.6 = (f32[320,90]{0,1:T(8,128)S(1)}, f32[320,90]{0,1:T(8,128)}, u32[]{:S(2)}) copy-start(f32[320,90]{0,1:T(8,128)} %param.5) | copy-start | bytes 345604
  154.7 48.9 %collective-permute-start.25 = (bf16[320,800]{1,0:T(8,128)(2,1)S(1)}, bf16[320,800]{1,0:T(8,128)(2,1)S(1)}, u32[]{:S(2)}, u32[]{:S(2)}) collective-permute-start(bf16[320,800]{1,0:T(8,128)(2,1)S(1)} %add_convert_fusion), channel_id=1, source_target_pairs={{0,480},{32,0},{64,32},{96,64},{128,96},{160,128},{192,160},{224,1... | collective-permute-start | bytes 1536008 | tf_op jit(solution)/shard_map/ppermute | solution.py:21
  184.5 18.3 %collective-permute-start.11 = (bf16[90,320]{1,0:T(8,128)(2,1)S(1)}, bf16[90,320]{1,0:T(8,128)(2,1)S(1)}, u32[]{:S(2)}, u32[]{:S(2)}) collective-permute-start(bf16[90,320]{1,0:T(8,128)(2,1)S(1)} %add_convert_fusion.1), channel_id=1, source_target_pairs={{0,0},{2,1},{4,2},{6,3},{8,4},{10,5},{12,6},{14,7},{16,200},{18,20... | collective-permute-start | bytes 172808 | tf_op jit(solution)/shard_map/ppermute | solution.py:213
  186.5 16.4 %collective-permute-start.12 = (bf16[90,320]{1,0:T(8,128)(2,1)S(1)}, bf16[90,320]{1,0:T(8,128)(2,1)S(1)}, u32[]{:S(2)}, u32[]{:S(2)}) collective-permute-start(bf16[90,320]{1,0:T(8,128)(2,1)S(1)} %add_convert_fusion.1), channel_id=1, source_target_pairs={{14,199},{20,490},{28,142},{11,213},{25,156},{46,231},{52,10},{60,... | collective-permute-start | bytes 172808 | tf_op jit(solution)/shard_map/ppermute | solution.py:214

commit v3 on v2

v3 whole, which is shorter than its diff:
```python
import functools

import jax
import jax.numpy as jnp
from jax import lax
from jax.experimental import pallas as pl
from jax.experimental.pallas import tpu as pltpu
from jax.sharding import Mesh
from jax.sharding import PartitionSpec as P

INTER = 25600
COL = ("x", "zh", "core")
ALL = ("row",) + COL
TILES = ((0, 0), (0, -1), (6, 4), (-1, -4), (4, 0), (4, -1), (6, 0), (6, -1), (4, -4))
LATE = tuple(k for k, t in enumerate(TILES) if 6 in t)
HIDES = 10**10
EARLY = tuple(k for k, t in enumerate(TILES) if 6 not in t)


def passed_along(x, axis, by):
    count = lax.axis_size(axis)
    return lax.ppermute(x, axis, [(i, (i + by) % count) for i in range(count)])


def shard_routes(sizes, shard, tile):
    nx, nzh, ncore = sizes
    routes = []
    for c in range(nx * nzh * ncore):
        first, last = c * shard // tile, (c * shard + shard - 1) // tile
        core, rest = divmod(c, nx * nzh)
        x, zh = divmod(rest, nzh)
        place = (x * nzh + zh) * ncore + core
        one, two = TILES[first][0], TILES[last][0]
        routes.append((c, place, one, two, last * tile - c * shard if one != two else shard))
    return routes


def dot(left, right, dims):
    return lax.dot_general(left, right, (dims, ((), ())), preferred_element_type=jnp.float32)


def call(kernel, outs, args, scratch=(), flops=0):
    moved = sum(a.size * a.dtype.itemsize for a in args)
    return pl.pallas_call(
        kernel,
        out_shape=[jax.ShapeDtypeStruct(s, d) for s, d in outs],
        in_specs=[pl.BlockSpec(memory_space=pltpu.VMEM)] * len(args),
        out_specs=[pl.BlockSpec(memory_space=pltpu.VMEM)] * len(outs),
        scratch_shapes=list(scratch),
        cost_estimate=pl.CostEstimate(flops=flops, bytes_accessed=moved, transcendentals=0),
        compiler_params=pltpu.CompilerParams(vmem_limit_bytes=24 * 2**20),
    )(*args)


def early_gram(g0, gm1, gm4, g4, out):
    held = {0: g0, -1: gm1, -4: gm4, 4: g4}
    for n, k in enumerate(EARLY):
        a, b = TILES[k]
        out[n] = dot(held[b][...], held[a][...], ((1,), (1,))).astype(out.dtype)


def late_gram(g0, gm1, g4, g6, early, keep, give, flat):
    held = {0: g0, -1: gm1, 4: g4, 6: g6}
    core = lax.axis_index("core")
    rows = early.shape[1]
    count, full, _ = keep.shape
    shard = len(TILES) * rows // (2 * count)
    for k, (a, b) in enumerate(TILES):
        if k in LATE:
            tile = dot(held[b][...], held[a][...], ((1,), (1,)))
        else:
            tile = early[EARLY.index(k)].astype(jnp.float32)
        flat[k * rows : (k + 1) * rows, :rows] = tile

    def put(outs):
        for q in range(count):
            for b, out in enumerate(outs):
                start = (2 * q + b) * shard
                out[q] = flat[start : start + full].astype(out.dtype)

    @pl.when(core == 0)
    def _():
        put((keep, give))

    @pl.when(core == 1)
    def _():
        put((give, keep))


def partner(zh, core, turn):
    first = (core + turn) % 2 == 0
    near, far = zh + 1 - 2 * (zh % 2), 3 - zh
    if isinstance(core, int):
        return near if first else far
    return jnp.where(first, near, far)


def x_sum(came, keep, send):
    zh, core = lax.axis_index("zh"), lax.axis_index("core")
    for out, who in ((keep, zh), (send, partner(zh, core, 0))):
        for n, q in enumerate((who, partner(who, core, 1))):
            total = sum(came[p, q].astype(jnp.float32) for p in range(came.shape[0]))
            out[n] = total.astype(out.dtype)


def assemble(mine, other, g0, gm1, gm4, g4, g6, tiles, out6, outm1, flat):
    nx, nzh = mine.shape[:2]
    rows = tiles.shape[1]
    shard = flat.shape[0] // (2 * nx * nzh)
    core = lax.axis_index("core")

    def put(parts):
        for x in range(nx):
            for zh in range(nzh):
                for b, part in enumerate(parts):
                    start = ((x * nzh + zh) * 2 + b) * shard
                    flat[start : start + shard] = part[x, zh].astype(jnp.float32)[:shard, :rows]

    @pl.when(core == 0)
    def _():
        put((mine, other))

    @pl.when(core == 1)
    def _():
        put((other, mine))

    for k in range(len(TILES)):
        tiles[k] = flat[k * rows : (k + 1) * rows].astype(tiles.dtype)
    held = {0: g0, -1: gm1, -4: gm4, 4: g4, 6: g6}
    out6[...] = summed_terms(tiles, held, 6).astype(out6.dtype)
    outm1[...] = summed_terms(tiles, held, -1).astype(outm1.dtype)


def summed_terms(tiles, held, o):
    total = None
    for k, (a, b) in enumerate(TILES):
        if a == o:
            term = dot(tiles[k], held[b][...], ((0,), (0,)))
            total = term if total is None else total + term
        if b == o and 0 < k < len(TILES) - 1:
            term = dot(tiles[k], held[a][...], ((1,), (0,)))
            total = term if total is None else total + term
    return total


def products(which, tiles, g0, gm1, gm4, g4, g6, *outs):
    held = {0: g0, -1: gm1, -4: gm4, 4: g4, 6: g6}
    for o, out in zip(which, outs):
        out[...] = summed_terms(tiles, held, o).astype(out.dtype)


def local(gradient, previous, root):
    rows, shard = previous.shape
    n_row = lax.axis_size("row")
    nx, nzh, ncore = (lax.axis_size(a) for a in COL)
    n_col = nx * nzh * ncore
    routes = shard_routes((nx, nzh, ncore), shard, rows)
    cuts = jnp.asarray([r[4] for r in routes], jnp.int32)
    cut = cuts[lax.axis_index(COL)]
    place_in_shard = lax.broadcasted_iota(jnp.int32, (shard, rows), 0)
    bf16, f32 = jnp.bfloat16, jnp.float32
    product = 2 * rows * rows * gradient.shape[1]

    def pairs(pick, place):
        return [
            ((i + r[pick]) % n_row * n_col + r[0], i * n_col + r[place])
            for i in range(n_row)
            for r in routes
            if pick == 2 or r[2] != r[3]
        ]

    mine = root.T
    one = lax.ppermute(mine, ALL, pairs(2, 0))
    two = lax.ppermute(mine, ALL, pairs(3, 0))
    one, two, gradient = lax.optimization_barrier((one, two, gradient))
    piece = jnp.where(place_in_shard < cut, one, two)
    full, lanes = -(-shard // 16) * 16, -(-rows // 128) * 128
    piece = jnp.pad(piece, ((0, full - shard), (0, lanes - rows)))
    turns = [
        [(zh * ncore + c, partner(zh, c, turn) * ncore + c) for zh in range(nzh) for c in range(ncore)]
        for turn in (0, 1)
    ]

    def traded(x, turn):
        return lax.ppermute(x, ("zh", "core"), turns[turn])

    piece = lax.all_to_all(jnp.broadcast_to(piece[None], (nzh,) + piece.shape), "zh", 0, 0, tiled=True)
    piece = lax.all_to_all(jnp.broadcast_to(piece[None], (nx,) + piece.shape), "x", 0, 0, tiled=True)
    pieces = (piece, passed_along(piece, "core", 1))

    g0 = gradient.astype(bf16)
    gm1 = passed_along(g0, "row", 1)
    gm4 = passed_along(g0, "row", 4)
    g4 = passed_along(g0, "row", -4)
    g6 = passed_along(g0, "row", -6)

    g0 = gradient.astype(bf16)
    gm1 = passed_along(g0, "row", 1)
    gm4 = passed_along(g0, "row", 4)
    g4 = passed_along(g0, "row", -4)
    g6 = passed_along(g0, "row", -6)
    blocks = (g0, gm1, gm4, g4, g6)
    chunks = (nx * nzh, full, lanes)
    (early,) = call(early_gram, [((len(EARLY), rows, rows), bf16)], (g0, gm1, gm4, g4), flops=HIDES)
    keep, give = call(
        late_gram,
        [(chunks, bf16)] * 2,
        (g0, gm1, g4, g6, early),
        [pltpu.VMEM((len(TILES) * rows + 8, lanes), f32)],
        flops=HIDES,
    )
    came = passed_along(give, "core", 1)

    shape = g0.shape
    tiles, out6, outm1 = call(
        assemble,
        [((len(TILES), rows, rows), bf16), (shape, bf16), (shape, f32)],
        (*pieces, *blocks),
        [pltpu.VMEM((len(TILES) * rows, rows), f32)],
        flops=7 * product,
    )
    came, tiles, out6 = lax.optimization_barrier((came, tiles, out6))
    chained = (outm1 + passed_along(out6, "row", 7).astype(f32)).astype(bf16)
    camem1 = passed_along(chained, "row", -1)
    out4, outm4 = call(
        functools.partial(products, (4, -4)), [(shape, bf16)] * 2, (tiles, *blocks), flops=5 * product
    )
    came4, camem4 = passed_along(out4, "row", 4), passed_along(outm4, "row", -4)
    (out0,) = call(functools.partial(products, (0,)), [(shape, f32)], (tiles, *blocks), flops=4 * product)

    sent = (keep.astype(f32) + came.astype(f32)).astype(bf16).reshape(nx, nzh, full, lanes)
    got = lax.all_to_all(sent, "x", 0, 0, tiled=True)
    mine, sent = call(x_sum, [((2, full, lanes), bf16)] * 2, (got,))
    mine = (mine.astype(f32) + traded(sent, 0).astype(f32)).astype(bf16)
    total = (mine[0].astype(f32) + traded(mine[1], 1).astype(f32)).astype(bf16)
    total, camem1, came4, camem4 = lax.optimization_barrier((total, camem1, came4, camem4))
    one, two = (lax.ppermute(total, ALL, [(b, a) for a, b in pairs(pick, 0)]) for pick in (2, 3))
    one, two = one[:shard, :rows], two[:shard, :rows]
    share = jnp.where(place_in_shard < cut, one, two).astype(f32).T
    statistic = 0.9 * previous + 0.1 / INTER * share
    applied = out0 + came4.astype(f32) + camem4.astype(f32) + camem1.astype(f32)
    return (statistic, applied)


def solution(mesh):
    split = Mesh(mesh.devices.reshape(mesh.shape["row"], 4, 4, 2), ALL)
    spec = P("row", COL)
    return jax.shard_map(
        local, mesh=split, in_specs=(spec,) * 3, out_specs=(spec,) * 2, check_vma=False
    )
```

time: 206 us -> 164 us (0.80)
  the two profiles are of different devices: /device:TPU:165 before, /device:TPU:10 now
where the time goes in v3:
time: 164 us; the launch traced here: 163 us
  starting transfers between devices  90.1 us (55%)
  waiting for transfers between devices  40.7 us (25%)
  Pallas kernels  13.6 us (8%)
  local copies, waits for them, and re-layouts  11 us (7%)
  other arithmetic  6.92 us (4%)
    ppermute x10, starting transfers between devices, passed_along(): return lax.ppermute(x, axis, [(i, (i + by) % count) for i in range(count)])  38.5 us
    ppermute x2, starting transfers between devices, traded(): return lax.ppermute(x, ('zh', 'core'), turns[turn])  14.5 us
    all_to_all x1, starting transfers between devices, local(): lax.all_to_all(jnp.broadcast_to(piece[None], (nzh,) + piece.shape), 'zh',...  14.2 us
    pallas_call x6, Pallas kernels, call(): pl.pallas_call(kernel, out_shape=[jax.ShapeDtypeStruct(s, d) for s, d in...  13.6 us
    ppermute x10, waiting for transfers between devices, passed_along(): return lax.ppermute(x, axis, [(i, (i + by) % count) for i in range(count)])  11.5 us
    ppermute x2, waiting for transfers between devices, traded(): return lax.ppermute(x, ('zh', 'core'), turns[turn])  9.02 us
    unnamed x38, local copies, waits for them, and re-layouts  7.84 us
    all_to_all x1, starting transfers between devices, local(): got = lax.all_to_all(sent, 'x', 0, 0, tiled=True)  7.16 us
  transfers between devices with their start and end apart: 19, of which 9 were waited for; matrix products, arithmetic and copies ran while one was open for 4% of the time, Pallas kernels for 8%

profile of v3, /device:TPU:10, one launch (start us, length us, event | category | flops | bytes accessed | tf_op | source)
XLA Modules:
  0.0 163.3 jit_solution(10636873845650271909)
XLA Ops:
  0.6 7.0 %collective-permute-start = (bf16[90,320]{1,0:T(8,128)(2,1)}, bf16[90,320]{1,0:T(8,128)(2,1)S(1)}, u32[]{:S(2)}, u32[]{:S(2)}) collective-permute-start(bf16[90,320]{1,0:T(8,128)(2,1)} %bitcast.13), channel_id=1, source_target_pairs={{0,0},{1,1},{2,2},{3,3},{4,4},{5,5},{6,6},{7,7},{200,8},{201,9},{2... | collective-permute-start | bytes 172808 | tf_op jit(solution)/shard_map/ppermute | solution.py:173
  7.7 0.7 collective-permute-start.1
  8.4 1.2 dynamic_slice.3
  9.6 0.6 iota_compare_fusion
  10.3 0.8 collective-permute-done
  11.1 0.0 collective-permute-done.1
  11.1 0.1 broadcast_select_fusion
  11.2 0.7 broadcast_in_dim.4
  11.9 14.2 %all-to-all-start = ((bf16[4,96,384]{2,1,0:T(8,128)(2,1)}), bf16[4,96,384]{2,1,0:T(8,128)(2,1)S(1)}, u32[]{:S(2)}, u32[]{:S(2)}) async-start(bf16[4,96,384]{2,1,0:T(8,128)(2,1)} %broadcast_in_dim.4), calls=%async_computation | async-start | bytes 589824 | tf_op jit(solution)/shard_map/all_to_all | solution.py:187
  26.2 0.1 convert_element_type.53.g0
  26.2 1.9 %collective-permute-start.2 = (bf16[320,800]{1,0:T(8,128)(2,1)S(1)}, bf16[320,800]{1,0:T(8,128)(2,1)S(1)}, u32[]{:S(2)}, u32[]{:S(2)}) collective-permute-start(bf16[320,800]{1,0:T(8,128)(2,1)S(1)} %convert_element_type.53.g0), channel_id=1, source_target_pairs={{0,32},{32,64},{64,96},{96,128},{128,160},{160,192},{192,224},{224... | collective-permute-start | bytes 1536008 | tf_op jit(solution)/shard_map/ppermute | solution.py:22
  28.2 4.5 %collective-permute-start.3 = (bf16[320,800]{1,0:T(8,128)(2,1)S(1)}, bf16[320,800]{1,0:T(8,128)(2,1)S(1)}, u32[]{:S(2)}, u32[]{:S(2)}) collective-permute-start(bf16[320,800]{1,0:T(8,128)(2,1)S(1)} %convert_element_type.53.g0), channel_id=1, source_target_pairs={{0,384},{32,416},{64,448},{96,480},{128,0},{160,32},{192,64},{224,... | collective-permute-start | bytes 1536008 | tf_op jit(solution)/shard_map/ppermute | solution.py:22
  32.6 1.9 %collective-permute-start.5 = (bf16[320,800]{1,0:T(8,128)(2,1)S(1)}, bf16[320,800]{1,0:T(8,128)(2,1)S(1)}, u32[]{:S(2)}, u32[]{:S(2)}) collective-permute-start(bf16[320,800]{1,0:T(8,128)(2,1)S(1)} %convert_element_type.53.g0), channel_id=1, source_target_pairs={{0,128},{32,160},{64,192},{96,224},{128,256},{160,288},{192,320},{... | collective-permute-start | bytes 1536008 | tf_op jit(solution)/shard_map/ppermute | solution.py:22
  34.6 5.5 %collective-permute-start.4 = (bf16[320,800]{1,0:T(8,128)(2,1)S(1)}, bf16[320,800]{1,0:T(8,128)(2,1)S(1)}, u32[]{:S(2)}, u32[]{:S(2)}) collective-permute-start(bf16[320,800]{1,0:T(8,128)(2,1)S(1)} %convert_element_type.53.g0), channel_id=1, source_target_pairs={{0,320},{32,352},{64,384},{96,416},{128,448},{160,480},{192,0},{22... | collective-permute-start | bytes 1536008 | tf_op jit(solution)/shard_map/ppermute | solution.py:22
  40.1 6.4 %all-to-all-done = bf16[4,96,384]{2,1,0:T(8,128)(2,1)S(1)} async-done(((bf16[4,96,384]{2,1,0:T(8,128)(2,1)}), bf16[4,96,384]{2,1,0:T(8,128)(2,1)S(1)}, u32[]{:S(2)}, u32[]{:S(2)}) %all-to-all-start) | async-done | bytes 294944 | tf_op jit(solution)/shard_map/all_to_all | solution.py:187
  46.4 1.1 broadcast_in_dim.5
  47.6 5.3 %all-to-all-start.1 = ((bf16[4,4,96,384]{3,2,1,0:T(8,128)(2,1)}), bf16[4,4,96,384]{3,2,1,0:T(8,128)(2,1)}, u32[]{:S(2)}, u32[]{:S(2)}) async-start(bf16[4,4,96,384]{3,2,1,0:T(8,128)(2,1)} %broadcast_in_dim.5), calls=%async_computation.1 | async-start | bytes 2359296 | tf_op jit(solution)/shard_map/all_to_all | solution.py:188
  52.8 0.1 collective-permute-done.2.gm1
  52.9 0.0 collective-permute-done.3.g4
  52.9 5.4 %collective-permute-done.5.gm4 = bf16[320,800]{1,0:T(8,128)(2,1)S(1)} collective-permute-done((bf16[320,800]{1,0:T(8,128)(2,1)S(1)}, bf16[320,800]{1,0:T(8,128)(2,1)S(1)}, u32[]{:S(2)}, u32[]{:S(2)}) %collective-permute-start.5) | collective-permute-done | bytes 512032 | tf_op jit(solution)/shard_map/ppermute | solution.py:22
  58.4 2.1 %shard_map.59.early = bf16[6,320,320]{2,1,0:T(8,128)(2,1)S(1)} custom-call(bf16[320,800]{1,0:T(8,128)(2,1)S(1)} %convert_element_type.53.g0, bf16[320,800]{1,0:T(8,128)(2,1)S(1)} %collective-permute-done.2.gm1, bf16[320,800]{1,0:T(8,128)(2,1)S(1)} %collective-permute-done.5.gm4, bf16[320,800]{1,0:T(8,128)(2,1)S(1)} %collective-permute-done.3.g4), custom_call_target="tpu_custom_call" | custom-call | flops 10000000000 | bytes 2048000 | tf_op jit(solution)/shard_map/pallas_call | solution.py:44
  60.5 0.0 copy-done.4
  60.5 1.1 copy-done.15
  61.6 6.8 %all-to-all-done.1.mine = bf16[4,4,96,384]{3,2,1,0:T(8,128)(2,1)} async-done(((bf16[4,4,96,384]{3,2,1,0:T(8,128)(2,1)}), bf16[4,4,96,384]{3,2,1,0:T(8,128)(2,1)}, u32[]{:S(2)}, u32[]{:S(2)}) %all-to-all-start.1) | async-done | bytes 1179680 | tf_op jit(solution)/shard_map/all_to_all | solution.py:188
  68.4 3.0 %collective-permute-start.7 = (bf16[4,4,96,384]{3,2,1,0:T(8,128)(2,1)}, bf16[4,4,96,384]{3,2,1,0:T(8,128)(2,1)S(1)}, u32[]{:S(2)}, u32[]{:S(2)}) collective-permute-start(bf16[4,4,96,384]{3,2,1,0:T(8,128)(2,1)} %all-to-all-done.1.mine), channel_id=1, source_target_pairs={{0,1},{1,0},{2,3},{3,2},{4,5},{5,4},{6,7},{7,6},{8,9},{9,8},{10,11... | collective-permute-start | bytes 3538952 | tf_op jit(solution)/shard_map/ppermute | solution.py:22
  71.4 5.9 %collective-permute-done.4.g6 = bf16[320,800]{1,0:T(8,128)(2,1)S(1)} collective-permute-done((bf16[320,800]{1,0:T(8,128)(2,1)S(1)}, bf16[320,800]{1,0:T(8,128)(2,1)S(1)}, u32[]{:S(2)}, u32[]{:S(2)}) %collective-permute-start.4) | collective-permute-done | bytes 512032 | tf_op jit(solution)/shard_map/ppermute | solution.py:22
  77.4 1.4 copy-done.16
  78.8 1.6 shard_map.60
  80.4 1.9 %collective-permute-start.6 = (bf16[16,96,384]{2,1,0:T(8,128)(2,1)S(1)}, bf16[16,96,384]{2,1,0:T(8,128)(2,1)S(1)}, u32[]{:S(2)}, u32[]{:S(2)}) collective-permute-start(bf16[16,96,384]{2,1,0:T(8,128)(2,1)S(1)} %get-tuple-element.23), channel_id=1, source_target_pairs={{0,1},{1,0},{2,3},{3,2},{4,5},{5,4},{6,7},{7,6},{8,9},{9,8},{10,11... | collective-permute-start | bytes 3538952 | tf_op jit(solution)/shard_map/ppermute | solution.py:22
  82.3 0.0 collective-permute-done.7.other
  82.4 1.1 copy-done.1
  83.4 1.1 copy-done.9
  84.5 4.2 %shard_map.61 = (bf16[9,320,320]{2,1,0:T(8,128)(2,1)S(1)}, bf16[320,800]{1,0:T(8,128)(2,1)S(1)}, f32[320,800]{1,0:T(8,128)S(1)}) custom-call(bf16[4,4,96,384]{3,2,1,0:T(8,128)(2,1)} %all-to-all-done.1.mine, bf16[4,4,96,384]{3,2,1,0:T(8,128)(2,1)S(1)} %collective-permute-done.7.other, bf16[320,800]{1,0:T(8,128)(2,1)S(1)} %convert_element_type.53.g0, ...), custom_call_target="tpu_custom_call" | custom-call | flops 1146880000 | bytes 4919296 | tf_op jit(solution)/shard_map/pallas_call | solution.py:44
  88.7 0.0 copy-start.12
  88.7 0.0 collective-permute-done.6
  88.7 1.5 add_convert_fusion
  90.2 7.2 %all-to-all-start.2 = ((bf16[4,4,96,384]{3,2,1,0:T(8,128)(2,1)}), bf16[4,4,96,384]{3,2,1,0:T(8,128)(2,1)}, u32[]{:S(2)}, u32[]{:S(2)}) async-start(bf16[4,4,96,384]{3,2,1,0:T(8,128)(2,1)} %bitcast.12), calls=%async_computation.2 | async-start | bytes 2359296 | tf_op jit(solution)/shard_map/all_to_all | solution.py:232
  97.4 2.0 %collective-permute-start.10 = (bf16[320,800]{1,0:T(8,128)(2,1)}, bf16[320,800]{1,0:T(8,128)(2,1)}, u32[]{:S(2)}, u32[]{:S(2)}) collective-permute-start(bf16[320,800]{1,0:T(8,128)(2,1)} %copy-done.14), channel_id=1, source_target_pairs={{0,224},{32,256},{64,288},{96,320},{128,352},{160,384},{192,416},{... | collective-permute-start | bytes 1536008 | tf_op jit(solution)/shard_map/ppermute | solution.py:22
  99.5 1.1 copy-done.2
  100.5 1.1 copy-done.6
  101.6 1.1 copy-done.10
  102.6 2.7 %shard_map.63 = (bf16[320,800]{1,0:T(8,128)(2,1)}, bf16[320,800]{1,0:T(8,128)(2,1)}) custom-call(bf16[9,320,320]{2,1,0:T(8,128)(2,1)S(1)} %get-tuple-element.33.tiles, bf16[320,800]{1,0:T(8,128)(2,1)S(1)} %convert_element_type.53.g0, bf16[320,800]{1,0:T(8,128)(2,1)S(1)} %collective-permute-done.2.gm1, bf16[320,800]{1,0:T(8,128)(2,1)S(1)} %copy-done.6, ...), custom_call_target="tpu_custom_call" | custom-call | flops 819200000 | bytes 4403200 | tf_op jit(solution)/shard_map/pallas_call | solution.py:44
  105.3 3.4 %collective-permute-start.12 = (bf16[320,800]{1,0:T(8,128)(2,1)}, bf16[320,800]{1,0:T(8,128)(2,1)}, u32[]{:S(2)}, u32[]{:S(2)}) collective-permute-start(bf16[320,800]{1,0:T(8,128)(2,1)} %get-tuple-element.34), channel_id=1, source_target_pairs={{0,128},{32,160},{64,192},{96,224},{128,256},{160,288},{192,320},{... | collective-permute-start | bytes 1536008 | tf_op jit(solution)/shard_map/ppermute | solution.py:22
  108.7 2.7 %collective-permute-start.13 = (bf16[320,800]{1,0:T(8,128)(2,1)}, bf16[320,800]{1,0:T(8,128)(2,1)}, u32[]{:S(2)}, u32[]{:S(2)}) collective-permute-start(bf16[320,800]{1,0:T(8,128)(2,1)} %get-tuple-element.35), channel_id=1, source_target_pairs={{0,384},{32,416},{64,448},{96,480},{128,0},{160,32},{192,64},{224,... | collective-permute-start | bytes 1536008 | tf_op jit(solution)/shard_map/ppermute | solution.py:22
  111.4 1.7 %all-to-all-done.2.came = bf16[4,4,96,384]{3,2,1,0:T(8,128)(2,1)} async-done(((bf16[4,4,96,384]{3,2,1,0:T(8,128)(2,1)}), bf16[4,4,96,384]{3,2,1,0:T(8,128)(2,1)}, u32[]{:S(2)}, u32[]{:S(2)}) %all-to-all-start.2) | async-done | bytes 1179680 | tf_op jit(solution)/shard_map/all_to_all | solution.py:232
  113.1 1.5 shard_map.62
  114.6 7.4 %collective-permute-start.8 = (bf16[2,96,384]{2,1,0:T(8,128)(2,1)S(1)}, bf16[2,96,384]{2,1,0:T(8,128)(2,1)S(1)}, u32[]{:S(2)}, u32[]{:S(2)}) collective-permute-start(bf16[2,96,384]{2,1,0:T(8,128)(2,1)S(1)} %get-tuple-element.30), channel_id=1, source_target_pairs={{0,2},{1,7},{2,0},{3,5},{4,6},{5,3},{6,4},{7,1},{8,10},{9,15},{10,... | collective-permute-start | bytes 442376 | tf_op jit(solution)/shard_map/ppermute | solution.py:185
  122.0 0.0 collective-permute-done.10
  122.1 1.3 add_convert_fusion.1
  123.4 11.7 %collective-permute-start.11 = (bf16[320,800]{1,0:T(8,128)(2,1)S(1)}, bf16[320,800]{1,0:T(8,128)(2,1)S(1)}, u32[]{:S(2)}, u32[]{:S(2)}) collective-permute-start(bf16[320,800]{1,0:T(8,128)(2,1)S(1)} %add_convert_fusion.1), channel_id=1, source_target_pairs={{0,480},{32,0},{64,32},{96,64},{128,96},{160,128},{192,160},{224,1... | collective-permute-start | bytes 1536008 | tf_op jit(solution)/shard_map/ppermute | solution.py:22
  135.1 0.0 collective-permute-done.8
  135.2 7.0 %collective-permute-start.9 = (bf16[96,384]{1,0:T(8,128)(2,1)S(1)}, bf16[96,384]{1,0:T(8,128)(2,1)S(1)}, u32[]{:S(2)}, u32[]{:S(2)}) collective-permute-start(bf16[96,384]{1,0:T(8,128)(2,1)S(1)} %slice_bitcast_fusion), channel_id=1, source_target_pairs={{0,6},{1,3},{2,4},{3,1},{4,2},{5,7},{6,0},{7,5},{8,14},{9,11},{10,... | collective-permute-start | bytes 221192 | tf_op jit(solution)/shard_map/ppermute | solution.py:185
  142.3 1.5 shard_map.64
  143.7 9.0 %collective-permute-done.9 = bf16[96,384]{1,0:T(8,128)(2,1)S(1)} collective-permute-done((bf16[96,384]{1,0:T(8,128)(2,1)S(1)}, bf16[96,384]{1,0:T(8,128)(2,1)S(1)}, u32[]{:S(2)}, u32[]{:S(2)}) %collective-permute-start.9) | collective-permute-done | bytes 73760 | tf_op jit(solution)/shard_map/ppermute | solution.py:185
  152.8 0.0 copy-start.18
  152.8 0.0 collective-permute-done.12
  152.8 0.0 collective-permute-done.13
  152.8 0.0 collective-permute-done.11
  152.8 2.1 %collective-permute-start.14 = (bf16[96,384]{1,0:T(8,128)(2,1)S(1)}, bf16[96,384]{1,0:T(8,128)(2,1)S(1)}, u32[]{:S(2)}, u32[]{:S(2)}) collective-permute-start(bf16[96,384]{1,0:T(8,128)(2,1)S(1)} %fusion), channel_id=1, source_target_pairs={{0,0},{1,1},{2,2},{3,3},{4,4},{5,5},{6,6},{7,7},{8,200},{9,201},{1... | collective-permute-start | bytes 221192 | tf_op jit(solution)/shard_map/ppermute | solution.py:237
  154.9 0.7 collective-permute-start.15
  155.6 2.5 %convert_add_fusion = f32[320,800]{1,0:T(8,128)} fusion(bf16[320,800]{1,0:T(8,128)(2,1)S(1)} %collective-permute-done.11, bf16[320,800]{1,0:T(8,128)(2,1)} %collective-permute-done.13, f32[320,800]{1,0:T(8,128)S(1)} %shard_map.64, bf16[320,800]{1,0:T(8,128)(2,1)} %collective-permute-done.12), kind=kLoop, calls=%fused_computation.1 | loop fusion | flops 1536000 | bytes 3584000 | tf_op jit(solution)/shard_map/add | solution.py:241
  158.0 4.5 %collective-permute-done.14 = bf16[96,384]{1,0:T(8,128)(2,1)S(1)} collective-permute-done((bf16[96,384]{1,0:T(8,128)(2,1)S(1)}, bf16[96,384]{1,0:T(8,128)(2,1)S(1)}, u32[]{:S(2)}, u32[]{:S(2)}) %collective-permute-start.14) | collective-permute-done | bytes 73760 | tf_op jit(solution)/shard_map/ppermute | solution.py:237
  162.5 0.0 collective-permute-done.15
  162.5 0.8 bitcast_add_fusion
  (32 shorter events, 0.1 us)
Async XLA Ops:
  0.6 25.5 %copy-start.17 = (f32[320,800]{1,0:T(8,128)S(1)}, f32[320,800]{1,0:T(8,128)}, u32[]{:S(2)}) copy-start(f32[320,800]{1,0:T(8,128)} %param.4) | copy-start | bytes 3072004
  0.6 10.4 %collective-permute-start = (bf16[90,320]{1,0:T(8,128)(2,1)}, bf16[90,320]{1,0:T(8,128)(2,1)S(1)}, u32[]{:S(2)}, u32[]{:S(2)}) collective-permute-start(bf16[90,320]{1,0:T(8,128)(2,1)} %bitcast.13), channel_id=1, source_target_pairs={{0,0},{1,1},{2,2},{3,3},{4,4},{5,5},{6,6},{7,7},{200,8},{201,9},{2... | collective-permute-start | bytes 172808 | tf_op jit(solution)/shard_map/ppermute | solution.py:173
  7.7 3.4 %collective-permute-start.1 = (bf16[90,320]{1,0:T(8,128)(2,1)}, bf16[90,320]{1,0:T(8,128)(2,1)S(1)}, u32[]{:S(2)}, u32[]{:S(2)}) collective-permute-start(bf16[90,320]{1,0:T(8,128)(2,1)} %bitcast.14), channel_id=1, source_target_pairs={{199,7},{490,10},{142,14},{213,21},{156,28},{231,39},{10,42},{174,... | collective-permute-start | bytes 172808 | tf_op jit(solution)/shard_map/ppermute | solution.py:174
  11.9 34.5 %all-to-all-start = ((bf16[4,96,384]{2,1,0:T(8,128)(2,1)}), bf16[4,96,384]{2,1,0:T(8,128)(2,1)S(1)}, u32[]{:S(2)}, u32[]{:S(2)}) async-start(bf16[4,96,384]{2,1,0:T(8,128)(2,1)} %broadcast_in_dim.4), calls=%async_computation | async-start | bytes 589824 | tf_op jit(solution)/shard_map/all_to_all | solution.py:187
  26.2 26.7 %collective-permute-start.2 = (bf16[320,800]{1,0:T(8,128)(2,1)S(1)}, bf16[320,800]{1,0:T(8,128)(2,1)S(1)}, u32[]{:S(2)}, u32[]{:S(2)}) collective-permute-start(bf16[320,800]{1,0:T(8,128)(2,1)S(1)} %convert_element_type.53.g0), channel_id=1, source_target_pairs={{0,32},{32,64},{64,96},{96,128},{128,160},{160,192},{192,224},{224... | collective-permute-start | bytes 1536008 | tf_op jit(solution)/shard_map/ppermute | solution.py:22
  28.2 24.8 %collective-permute-start.3 = (bf16[320,800]{1,0:T(8,128)(2,1)S(1)}, bf16[320,800]{1,0:T(8,128)(2,1)S(1)}, u32[]{:S(2)}, u32[]{:S(2)}) collective-permute-start(bf16[320,800]{1,0:T(8,128)(2,1)S(1)} %convert_element_type.53.g0), channel_id=1, source_target_pairs={{0,384},{32,416},{64,448},{96,480},{128,0},{160,32},{192,64},{224,... | collective-permute-start | bytes 1536008 | tf_op jit(solution)/shard_map/ppermute | solution.py:22
  32.6 25.7 %collective-permute-start.5 = (bf16[320,800]{1,0:T(8,128)(2,1)S(1)}, bf16[320,800]{1,0:T(8,128)(2,1)S(1)}, u32[]{:S(2)}, u32[]{:S(2)}) collective-permute-start(bf16[320,800]{1,0:T(8,128)(2,1)S(1)} %convert_element_type.53.g0), channel_id=1, source_target_pairs={{0,128},{32,160},{64,192},{96,224},{128,256},{160,288},{192,320},{... | collective-permute-start | bytes 1536008 | tf_op jit(solution)/shard_map/ppermute | solution.py:22
  34.6 42.8 %collective-permute-start.4 = (bf16[320,800]{1,0:T(8,128)(2,1)S(1)}, bf16[320,800]{1,0:T(8,128)(2,1)S(1)}, u32[]{:S(2)}, u32[]{:S(2)}) collective-permute-start(bf16[320,800]{1,0:T(8,128)(2,1)S(1)} %convert_element_type.53.g0), channel_id=1, source_target_pairs={{0,320},{32,352},{64,384},{96,416},{128,448},{160,480},{192,0},{22... | collective-permute-start | bytes 1536008 | tf_op jit(solution)/shard_map/ppermute | solution.py:22
  47.6 20.9 %all-to-all-start.1 = ((bf16[4,4,96,384]{3,2,1,0:T(8,128)(2,1)}), bf16[4,4,96,384]{3,2,1,0:T(8,128)(2,1)}, u32[]{:S(2)}, u32[]{:S(2)}) async-start(bf16[4,4,96,384]{3,2,1,0:T(8,128)(2,1)} %broadcast_in_dim.5), calls=%async_computation.1 | async-start | bytes 2359296 | tf_op jit(solution)/shard_map/all_to_all | solution.py:188
  52.9 24.4 %copy-start = (bf16[320,800]{1,0:T(8,128)(2,1)}, bf16[320,800]{1,0:T(8,128)(2,1)S(1)}, u32[]{:S(2)}) copy-start(bf16[320,800]{1,0:T(8,128)(2,1)S(1)} %collective-permute-done.3.g4) | copy-start | bytes 1536004
  58.4 2.1 %copy-start.4 = (bf16[320,800]{1,0:T(8,128)(2,1)}, bf16[320,800]{1,0:T(8,128)(2,1)S(1)}, u32[]{:S(2)}) copy-start(bf16[320,800]{1,0:T(8,128)(2,1)S(1)} %collective-permute-done.5.gm4) | copy-start | bytes 1536004
  60.5 1.1 copy-start.15
  68.4 13.9 %copy-start.5 = (bf16[320,800]{1,0:T(8,128)(2,1)S(1)}, bf16[320,800]{1,0:T(8,128)(2,1)}, u32[]{:S(2)}) copy-start(bf16[320,800]{1,0:T(8,128)(2,1)} %copy-done.4) | copy-start | bytes 1536004
  68.4 13.9 %collective-permute-start.7 = (bf16[4,4,96,384]{3,2,1,0:T(8,128)(2,1)}, bf16[4,4,96,384]{3,2,1,0:T(8,128)(2,1)S(1)}, u32[]{:S(2)}, u32[]{:S(2)}) collective-permute-start(bf16[4,4,96,384]{3,2,1,0:T(8,128)(2,1)} %all-to-all-done.1.mine), channel_id=1, source_target_pairs={{0,1},{1,0},{2,3},{3,2},{4,5},{5,4},{6,7},{7,6},{8,9},{9,8},{10,11... | collective-permute-start | bytes 3538952 | tf_op jit(solution)/shard_map/ppermute | solution.py:22
  77.4 1.4 copy-start.16
  78.8 1.6 %copy-start.8 = (bf16[320,800]{1,0:T(8,128)(2,1)}, bf16[320,800]{1,0:T(8,128)(2,1)S(1)}, u32[]{:S(2)}) copy-start(bf16[320,800]{1,0:T(8,128)(2,1)S(1)} %collective-permute-done.4.g6) | copy-start | bytes 1536004
  80.4 8.3 %collective-permute-start.6 = (bf16[16,96,384]{2,1,0:T(8,128)(2,1)S(1)}, bf16[16,96,384]{2,1,0:T(8,128)(2,1)S(1)}, u32[]{:S(2)}, u32[]{:S(2)}) collective-permute-start(bf16[16,96,384]{2,1,0:T(8,128)(2,1)S(1)} %get-tuple-element.23), channel_id=1, source_target_pairs={{0,1},{1,0},{2,3},{3,2},{4,5},{5,4},{6,7},{7,6},{8,9},{9,8},{10,11... | collective-permute-start | bytes 3538952 | tf_op jit(solution)/shard_map/ppermute | solution.py:22
  82.4 1.1 copy-start.1
  83.4 1.1 copy-start.9
  88.7 1.6 copy-start.12
  88.7 1.6 copy-start.14
  90.2 22.8 %all-to-all-start.2 = ((bf16[4,4,96,384]{3,2,1,0:T(8,128)(2,1)}), bf16[4,4,96,384]{3,2,1,0:T(8,128)(2,1)}, u32[]{:S(2)}, u32[]{:S(2)}) async-start(bf16[4,4,96,384]{3,2,1,0:T(8,128)(2,1)} %bitcast.12), calls=%async_computation.2 | async-start | bytes 2359296 | tf_op jit(solution)/shard_map/all_to_all | solution.py:232
  97.4 24.6 %collective-permute-start.10 = (bf16[320,800]{1,0:T(8,128)(2,1)}, bf16[320,800]{1,0:T(8,128)(2,1)}, u32[]{:S(2)}, u32[]{:S(2)}) collective-permute-start(bf16[320,800]{1,0:T(8,128)(2,1)} %copy-done.14), channel_id=1, source_target_pairs={{0,224},{32,256},{64,288},{96,320},{128,352},{160,384},{192,416},{... | collective-permute-start | bytes 1536008 | tf_op jit(solution)/shard_map/ppermute | solution.py:22
  99.5 1.1 copy-start.2
  100.5 1.1 copy-start.6
  101.6 1.1 copy-start.10
  105.3 47.5 %collective-permute-start.12 = (bf16[320,800]{1,0:T(8,128)(2,1)}, bf16[320,800]{1,0:T(8,128)(2,1)}, u32[]{:S(2)}, u32[]{:S(2)}) collective-permute-start(bf16[320,800]{1,0:T(8,128)(2,1)} %get-tuple-element.34), channel_id=1, source_target_pairs={{0,128},{32,160},{64,192},{96,224},{128,256},{160,288},{192,320},{... | collective-permute-start | bytes 1536008 | tf_op jit(solution)/shard_map/ppermute | solution.py:22
  108.7 44.1 %collective-permute-start.13 = (bf16[320,800]{1,0:T(8,128)(2,1)}, bf16[320,800]{1,0:T(8,128)(2,1)}, u32[]{:S(2)}, u32[]{:S(2)}) collective-permute-start(bf16[320,800]{1,0:T(8,128)(2,1)} %get-tuple-element.35), channel_id=1, source_target_pairs={{0,384},{32,416},{64,448},{96,480},{128,0},{160,32},{192,64},{224,... | collective-permute-start | bytes 1536008 | tf_op jit(solution)/shard_map/ppermute | solution.py:22
  113.1 9.0 %copy-start.13 = (f32[320,800]{1,0:T(8,128)S(1)}, f32[320,800]{1,0:T(8,128)}, u32[]{:S(2)}) copy-start(f32[320,800]{1,0:T(8,128)} %copy-done.12) | copy-start | bytes 3072004
  114.6 20.5 %collective-permute-start.8 = (bf16[2,96,384]{2,1,0:T(8,128)(2,1)S(1)}, bf16[2,96,384]{2,1,0:T(8,128)(2,1)S(1)}, u32[]{:S(2)}, u32[]{:S(2)}) collective-permute-start(bf16[2,96,384]{2,1,0:T(8,128)(2,1)S(1)} %get-tuple-element.30), channel_id=1, source_target_pairs={{0,2},{1,7},{2,0},{3,5},{4,6},{5,3},{6,4},{7,1},{8,10},{9,15},{10,... | collective-permute-start | bytes 442376 | tf_op jit(solution)/shard_map/ppermute | solution.py:185
  122.0 20.2 %copy-start.3 = (bf16[320,800]{1,0:T(8,128)(2,1)S(1)}, bf16[320,800]{1,0:T(8,128)(2,1)}, u32[]{:S(2)}) copy-start(bf16[320,800]{1,0:T(8,128)(2,1)} %copy-done) | copy-start | bytes 1536004
  122.1 20.2 %copy-start.7 = (bf16[320,800]{1,0:T(8,128)(2,1)S(1)}, bf16[320,800]{1,0:T(8,128)(2,1)}, u32[]{:S(2)}) copy-start(bf16[320,800]{1,0:T(8,128)(2,1)} %copy-done.4) | copy-start | bytes 1536004
  122.1 20.2 %copy-start.11 = (bf16[320,800]{1,0:T(8,128)(2,1)S(1)}, bf16[320,800]{1,0:T(8,128)(2,1)}, u32[]{:S(2)}) copy-start(bf16[320,800]{1,0:T(8,128)(2,1)} %copy-done.8) | copy-start | bytes 1536004
  123.4 29.4 %collective-permute-start.11 = (bf16[320,800]{1,0:T(8,128)(2,1)S(1)}, bf16[320,800]{1,0:T(8,128)(2,1)S(1)}, u32[]{:S(2)}, u32[]{:S(2)}) collective-permute-start(bf16[320,800]{1,0:T(8,128)(2,1)S(1)} %add_convert_fusion.1), channel_id=1, source_target_pairs={{0,480},{32,0},{64,32},{96,64},{128,96},{160,128},{192,160},{224,1... | collective-permute-start | bytes 1536008 | tf_op jit(solution)/shard_map/ppermute | solution.py:22
  135.2 17.6 %collective-permute-start.9 = (bf16[96,384]{1,0:T(8,128)(2,1)S(1)}, bf16[96,384]{1,0:T(8,128)(2,1)S(1)}, u32[]{:S(2)}, u32[]{:S(2)}) collective-permute-start(bf16[96,384]{1,0:T(8,128)(2,1)S(1)} %slice_bitcast_fusion), channel_id=1, source_target_pairs={{0,6},{1,3},{2,4},{3,1},{4,2},{5,7},{6,0},{7,5},{8,14},{9,11},{10,... | collective-permute-start | bytes 221192 | tf_op jit(solution)/shard_map/ppermute | solution.py:185
  152.8 9.7 %copy-start.18 = (f32[320,90]{0,1:T(8,128)S(1)}, f32[320,90]{0,1:T(8,128)}, u32[]{:S(2)}) copy-start(f32[320,90]{0,1:T(8,128)} %param.5) | copy-start | bytes 345604
  152.8 9.7 %collective-permute-start.14 = (bf16[96,384]{1,0:T(8,128)(2,1)S(1)}, bf16[96,384]{1,0:T(8,128)(2,1)S(1)}, u32[]{:S(2)}, u32[]{:S(2)}) collective-permute-start(bf16[96,384]{1,0:T(8,128)(2,1)S(1)} %fusion), channel_id=1, source_target_pairs={{0,0},{1,1},{2,2},{3,3},{4,4},{5,5},{6,6},{7,7},{8,200},{9,201},{1... | collective-permute-start | bytes 221192 | tf_op jit(solution)/shard_map/ppermute | solution.py:237
  154.9 7.6 %collective-permute-start.15 = (bf16[96,384]{1,0:T(8,128)(2,1)S(1)}, bf16[96,384]{1,0:T(8,128)(2,1)S(1)}, u32[]{:S(2)}, u32[]{:S(2)}) collective-permute-start(bf16[96,384]{1,0:T(8,128)(2,1)S(1)} %fusion), channel_id=1, source_target_pairs={{7,199},{10,490},{14,142},{21,213},{28,156},{39,231},{42,10},{46,1... | collective-permute-start | bytes 221192 | tf_op jit(solution)/shard_map/ppermute | solution.py:237

commit v4 on v3

--- a/solution.py
+++ b/solution.py
@@ -12,9 +12,9 @@
 COL = ("x", "zh", "core")
 ALL = ("row",) + COL
 TILES = ((0, 0), (0, -1), (6, 4), (-1, -4), (4, 0), (4, -1), (6, 0), (6, -1), (4, -4))
-LATE = tuple(k for k, t in enumerate(TILES) if 6 in t)
+LATE = tuple(range(1, len(TILES)))
 HIDES = 10**10
-EARLY = tuple(k for k, t in enumerate(TILES) if 6 not in t)
+EARLY = (0,)
 
 
 def passed_along(x, axis, by):
@@ -52,15 +52,12 @@
     )(*args)
 
 
-def early_gram(g0, gm1, gm4, g4, out):
-    held = {0: g0, -1: gm1, -4: gm4, 4: g4}
-    for n, k in enumerate(EARLY):
-        a, b = TILES[k]
-        out[n] = dot(held[b][...], held[a][...], ((1,), (1,))).astype(out.dtype)
-
-
-def late_gram(g0, gm1, g4, g6, early, keep, give, flat):
-    held = {0: g0, -1: gm1, 4: g4, 6: g6}
+def early_gram(g0, out):
+    out[0] = dot(g0[...], g0[...], ((1,), (1,))).astype(out.dtype)
+
+
+def late_gram(g0, gm1, gm4, g4, g6, early, keep, give, flat):
+    held = {0: g0, -1: gm1, -4: gm4, 4: g4, 6: g6}
     core = lax.axis_index("core")
     rows = early.shape[1]
     count, full, _ = keep.shape
@@ -103,7 +100,7 @@
             out[n] = total.astype(out.dtype)
 
 
-def assemble(mine, other, g0, gm1, gm4, g4, g6, tiles, out6, outm1, flat):
+def assemble(mine, other, g0, gm1, g4, tiles, out6, flat):
     nx, nzh = mine.shape[:2]
     rows = tiles.shape[1]
     shard = flat.shape[0] // (2 * nx * nzh)
@@ -126,9 +123,7 @@
 
     for k in range(len(TILES)):
         tiles[k] = flat[k * rows : (k + 1) * rows].astype(tiles.dtype)
-    held = {0: g0, -1: gm1, -4: gm4, 4: g4, 6: g6}
-    out6[...] = summed_terms(tiles, held, 6).astype(out6.dtype)
-    outm1[...] = summed_terms(tiles, held, -1).astype(outm1.dtype)
+    out6[...] = summed_terms(tiles, {0: g0, -1: gm1, 4: g4}, 6).astype(out6.dtype)
 
 
 def summed_terms(tiles, held, o):
@@ -192,42 +187,43 @@
     gm1 = passed_along(g0, "row", 1)
     gm4 = passed_along(g0, "row", 4)
     g4 = passed_along(g0, "row", -4)
-    g6 = passed_along(g0, "row", -6)
+    g6 = passed_along(gm1, "row", -7)
 
     g0 = gradient.astype(bf16)
     gm1 = passed_along(g0, "row", 1)
     gm4 = passed_along(g0, "row", 4)
     g4 = passed_along(g0, "row", -4)
-    g6 = passed_along(g0, "row", -6)
-    blocks = (g0, gm1, gm4, g4, g6)
+    g6 = passed_along(gm1, "row", -7)
+    g0, gm1, gm4, g4, g6 = blocks = lax.optimization_barrier((g0, gm1, gm4, g4, g6))
     chunks = (nx * nzh, full, lanes)
-    (early,) = call(early_gram, [((len(EARLY), rows, rows), bf16)], (g0, gm1, gm4, g4), flops=HIDES)
+    (early,) = call(early_gram, [((len(EARLY), rows, rows), bf16)], (g0,), flops=HIDES)
     keep, give = call(
         late_gram,
         [(chunks, bf16)] * 2,
-        (g0, gm1, g4, g6, early),
+        (*blocks, early),
         [pltpu.VMEM((len(TILES) * rows + 8, lanes), f32)],
         flops=HIDES,
     )
     came = passed_along(give, "core", 1)
 
     shape = g0.shape
-    tiles, out6, outm1 = call(
+    tiles, out6 = call(
         assemble,
-        [((len(TILES), rows, rows), bf16), (shape, bf16), (shape, f32)],
-        (*pieces, *blocks),
+        [((len(TILES), rows, rows), bf16), (shape, bf16)],
+        (*pieces, g0, gm1, g4),
         [pltpu.VMEM((len(TILES) * rows, rows), f32)],
-        flops=7 * product,
+        flops=3 * product,
     )
     came, tiles, out6 = lax.optimization_barrier((came, tiles, out6))
+    out4, outm4, outm1 = call(
+        functools.partial(products, (4, -4, -1)),
+        [(shape, bf16), (shape, bf16), (shape, f32)],
+        (tiles, *blocks),
+        flops=9 * product,
+    )
+    came4, camem4 = passed_along(out4, "row", 4), passed_along(outm4, "row", -4)
     chained = (outm1 + passed_along(out6, "row", 7).astype(f32)).astype(bf16)
     camem1 = passed_along(chained, "row", -1)
-    out4, outm4 = call(
-        functools.partial(products, (4, -4)), [(shape, bf16)] * 2, (tiles, *blocks), flops=5 * product
-    )
-    came4, camem4 = passed_along(out4, "row", 4), passed_along(outm4, "row", -4)
-    (out0,) = call(functools.partial(products, (0,)), [(shape, f32)], (tiles, *blocks), flops=4 * product)
-
     sent = (keep.astype(f32) + came.astype(f32)).astype(bf16).reshape(nx, nzh, full, lanes)
     got = lax.all_to_all(sent, "x", 0, 0, tiled=True)
     mine, sent = call(x_sum, [((2, full, lanes), bf16)] * 2, (got,))
@@ -238,6 +234,7 @@
     one, two = one[:shard, :rows], two[:shard, :rows]
     share = jnp.where(place_in_shard < cut, one, two).astype(f32).T
     statistic = 0.9 * previous + 0.1 / INTER * share
+    (out0,) = call(functools.partial(products, (0,)), [(shape, f32)], (tiles, *blocks), flops=4 * product)
     applied = out0 + came4.astype(f32) + camem4.astype(f32) + camem1.astype(f32)
     return (statistic, applied)
 

time: 164 us -> 162 us (0.988)
  the two profiles are of different devices: /device:TPU:10 before, /device:TPU:162 now
where the time goes in v4:
time: 162 us; the launch traced here: 161 us
  starting transfers between devices  74.5 us (46%)
  waiting for transfers between devices  57.2 us (35%)
  Pallas kernels  13.3 us (8%)
  other arithmetic  7.98 us (5%)
  local copies, waits for them, and re-layouts  7.43 us (5%)
    ppermute x10, starting transfers between devices, passed_along(): return lax.ppermute(x, axis, [(i, (i + by) % count) for i in range(count)])  29.3 us
    pallas_call x6, Pallas kernels, call(): pl.pallas_call(kernel, out_shape=[jax.ShapeDtypeStruct(s, d) for s, d in...  13.3 us
    ppermute x2, waiting for transfers between devices, traded(): return lax.ppermute(x, ('zh', 'core'), turns[turn])  13.1 us
    all_to_all x1, waiting for transfers between devices, local(): lax.all_to_all(jnp.broadcast_to(piece[None], (nx,) + piece.shape), 'x', 0...  12.4 us
    ppermute x10, waiting for transfers between devices, passed_along(): return lax.ppermute(x, axis, [(i, (i + by) % count) for i in range(count)])  12.4 us
    ppermute x2, waiting for transfers between devices, local(): lax.ppermute(total, ALL, [(b, a) for a, b in pairs(pick, 0)])  11.6 us
    ppermute x2, starting transfers between devices, local(): lax.ppermute(total, ALL, [(b, a) for a, b in pairs(pick, 0)])  9.22 us
    ppermute x2, starting transfers between devices, traded(): return lax.ppermute(x, ('zh', 'core'), turns[turn])  7.68 us
  transfers between devices with their start and end apart: 19, of which 10 were waited for; matrix products, arithmetic and copies ran while one was open for 5% of the time, Pallas kernels for 8%

profile of v4, /device:TPU:162, one launch (start us, length us, event | category | flops | bytes accessed | tf_op | source)
XLA Modules:
  0.0 161.4 jit_solution(13644653859383831741)
XLA Ops:
  0.6 3.8 %collective-permute-start.1 = (bf16[90,320]{1,0:T(8,128)(2,1)}, bf16[90,320]{1,0:T(8,128)(2,1)S(1)}, u32[]{:S(2)}, u32[]{:S(2)}) collective-permute-start(bf16[90,320]{1,0:T(8,128)(2,1)} %bitcast.13), channel_id=1, source_target_pairs={{199,7},{490,10},{142,14},{213,21},{156,28},{231,39},{10,42},{174,... | collective-permute-start | bytes 172808 | tf_op jit(solution)/shard_map/ppermute | solution.py:169
  4.5 5.9 %collective-permute-start = (bf16[90,320]{1,0:T(8,128)(2,1)}, bf16[90,320]{1,0:T(8,128)(2,1)S(1)}, u32[]{:S(2)}, u32[]{:S(2)}) collective-permute-start(bf16[90,320]{1,0:T(8,128)(2,1)} %bitcast.14), channel_id=1, source_target_pairs={{0,0},{1,1},{2,2},{3,3},{4,4},{5,5},{6,6},{7,7},{200,8},{201,9},{2... | collective-permute-start | bytes 172808 | tf_op jit(solution)/shard_map/ppermute | solution.py:168
  10.4 1.2 dynamic_slice.3
  11.6 0.6 iota_compare_fusion
  12.3 0.0 collective-permute-done.1
  12.3 0.4 collective-permute-done
  12.7 1.3 convert_element_type.53.g0
  14.0 5.3 %collective-permute-start.2 = (bf16[320,800]{1,0:T(8,128)(2,1)S(1)}, bf16[320,800]{1,0:T(8,128)(2,1)S(1)}, u32[]{:S(2)}, u32[]{:S(2)}) collective-permute-start(bf16[320,800]{1,0:T(8,128)(2,1)S(1)} %convert_element_type.53.g0), channel_id=1, source_target_pairs={{0,32},{32,64},{64,96},{96,128},{128,160},{160,192},{192,224},{224... | collective-permute-start | bytes 1536008 | tf_op jit(solution)/shard_map/ppermute | solution.py:22
  19.4 0.1 broadcast_select_fusion
  19.5 0.7 broadcast_in_dim.4
  20.2 7.2 %all-to-all-start = ((bf16[4,96,384]{2,1,0:T(8,128)(2,1)}), bf16[4,96,384]{2,1,0:T(8,128)(2,1)S(1)}, u32[]{:S(2)}, u32[]{:S(2)}) async-start(bf16[4,96,384]{2,1,0:T(8,128)(2,1)} %broadcast_in_dim.4), calls=%async_computation | async-start | bytes 589824 | tf_op jit(solution)/shard_map/all_to_all | solution.py:182
  27.4 5.0 %collective-permute-start.4 = (bf16[320,800]{1,0:T(8,128)(2,1)S(1)}, bf16[320,800]{1,0:T(8,128)(2,1)S(1)}, u32[]{:S(2)}, u32[]{:S(2)}) collective-permute-start(bf16[320,800]{1,0:T(8,128)(2,1)S(1)} %convert_element_type.53.g0), channel_id=1, source_target_pairs={{0,384},{32,416},{64,448},{96,480},{128,0},{160,32},{192,64},{224,... | collective-permute-start | bytes 1536008 | tf_op jit(solution)/shard_map/ppermute | solution.py:22
  32.4 1.9 %collective-permute-start.3 = (bf16[320,800]{1,0:T(8,128)(2,1)S(1)}, bf16[320,800]{1,0:T(8,128)(2,1)S(1)}, u32[]{:S(2)}, u32[]{:S(2)}) collective-permute-start(bf16[320,800]{1,0:T(8,128)(2,1)S(1)} %convert_element_type.53.g0), channel_id=1, source_target_pairs={{0,128},{32,160},{64,192},{96,224},{128,256},{160,288},{192,320},{... | collective-permute-start | bytes 1536008 | tf_op jit(solution)/shard_map/ppermute | solution.py:22
  34.3 5.4 %collective-permute-done.2.gm1 = bf16[320,800]{1,0:T(8,128)(2,1)S(1)} collective-permute-done((bf16[320,800]{1,0:T(8,128)(2,1)S(1)}, bf16[320,800]{1,0:T(8,128)(2,1)S(1)}, u32[]{:S(2)}, u32[]{:S(2)}) %collective-permute-start.2) | collective-permute-done | bytes 512032 | tf_op jit(solution)/shard_map/ppermute | solution.py:22
  39.7 1.9 %collective-permute-start.5 = (bf16[320,800]{1,0:T(8,128)(2,1)S(1)}, bf16[320,800]{1,0:T(8,128)(2,1)}, u32[]{:S(2)}, u32[]{:S(2)}) collective-permute-start(bf16[320,800]{1,0:T(8,128)(2,1)S(1)} %collective-permute-done.2.gm1), channel_id=1, source_target_pairs={{0,288},{32,320},{64,352},{96,384},{128,416},{160,448},{192,480},{... | collective-permute-start | bytes 1536008 | tf_op jit(solution)/shard_map/ppermute | solution.py:22
  41.7 7.3 %all-to-all-done = bf16[4,96,384]{2,1,0:T(8,128)(2,1)S(1)} async-done(((bf16[4,96,384]{2,1,0:T(8,128)(2,1)}), bf16[4,96,384]{2,1,0:T(8,128)(2,1)S(1)}, u32[]{:S(2)}, u32[]{:S(2)}) %all-to-all-start) | async-done | bytes 294944 | tf_op jit(solution)/shard_map/all_to_all | solution.py:182
  48.9 1.2 broadcast_in_dim.5
  50.1 6.3 %all-to-all-start.1 = ((bf16[4,4,96,384]{3,2,1,0:T(8,128)(2,1)}), bf16[4,4,96,384]{3,2,1,0:T(8,128)(2,1)S(1)}, u32[]{:S(2)}, u32[]{:S(2)}) async-start(bf16[4,4,96,384]{3,2,1,0:T(8,128)(2,1)} %broadcast_in_dim.5), calls=%async_computation.1 | async-start | bytes 2359296 | tf_op jit(solution)/shard_map/all_to_all | solution.py:183
  56.4 0.0 collective-permute-done.4.g4
  56.4 2.1 %collective-permute-done.3.gm4 = bf16[320,800]{1,0:T(8,128)(2,1)S(1)} collective-permute-done((bf16[320,800]{1,0:T(8,128)(2,1)S(1)}, bf16[320,800]{1,0:T(8,128)(2,1)S(1)}, u32[]{:S(2)}, u32[]{:S(2)}) %collective-permute-start.3) | collective-permute-done | bytes 512032 | tf_op jit(solution)/shard_map/ppermute | solution.py:22
  58.6 0.0 collective-permute-done.5.g6
  58.6 0.5 shard_map.59.early
  59.1 0.0 copy-start.6
  59.1 0.7 copy-done.6
  59.8 12.4 %all-to-all-done.1.mine = bf16[4,4,96,384]{3,2,1,0:T(8,128)(2,1)S(1)} async-done(((bf16[4,4,96,384]{3,2,1,0:T(8,128)(2,1)}), bf16[4,4,96,384]{3,2,1,0:T(8,128)(2,1)S(1)}, u32[]{:S(2)}, u32[]{:S(2)}) %all-to-all-start.1) | async-done | bytes 1179680 | tf_op jit(solution)/shard_map/all_to_all | solution.py:183
  72.2 2.4 %collective-permute-start.7 = (bf16[4,4,96,384]{3,2,1,0:T(8,128)(2,1)S(1)}, bf16[4,4,96,384]{3,2,1,0:T(8,128)(2,1)S(1)}, u32[]{:S(2)}, u32[]{:S(2)}) collective-permute-start(bf16[4,4,96,384]{3,2,1,0:T(8,128)(2,1)S(1)} %all-to-all-done.1.mine), channel_id=1, source_target_pairs={{0,1},{1,0},{2,3},{3,2},{4,5},{5,4},{6,7},{7,6},{8,9},{9,8},{10,11... | collective-permute-start | bytes 3538952 | tf_op jit(solution)/shard_map/ppermute | solution.py:22
  74.6 0.0 copy-start.7
  74.6 0.9 copy-done.7
  75.6 4.3 %shard_map.60 = (bf16[16,96,384]{2,1,0:T(8,128)(2,1)S(1)}, bf16[16,96,384]{2,1,0:T(8,128)(2,1)S(1)}) custom-call(bf16[320,800]{1,0:T(8,128)(2,1)S(1)} %convert_element_type.53.g0, bf16[320,800]{1,0:T(8,128)(2,1)S(1)} %collective-permute-done.2.gm1, bf16[320,800]{1,0:T(8,128)(2,1)S(1)} %collective-permute-done.3.gm4, ...), custom_call_target="tpu_custom_call" | custom-call | flops 10000000000 | bytes 2764800 | tf_op jit(solution)/shard_map/pallas_call | solution.py:44
  79.8 1.9 %collective-permute-start.6 = (bf16[16,96,384]{2,1,0:T(8,128)(2,1)S(1)}, bf16[16,96,384]{2,1,0:T(8,128)(2,1)S(1)}, u32[]{:S(2)}, u32[]{:S(2)}) collective-permute-start(bf16[16,96,384]{2,1,0:T(8,128)(2,1)S(1)} %get-tuple-element.33), channel_id=1, source_target_pairs={{0,1},{1,0},{2,3},{3,2},{4,5},{5,4},{6,7},{7,6},{8,9},{9,8},{10,11... | collective-permute-start | bytes 3538952 | tf_op jit(solution)/shard_map/ppermute | solution.py:22
  81.7 0.0 collective-permute-done.7.other
  81.8 1.7 %shard_map.61 = (bf16[9,320,320]{2,1,0:T(8,128)(2,1)S(1)}, bf16[320,800]{1,0:T(8,128)(2,1)S(1)}) custom-call(bf16[4,4,96,384]{3,2,1,0:T(8,128)(2,1)S(1)} %all-to-all-done.1.mine, bf16[4,4,96,384]{3,2,1,0:T(8,128)(2,1)S(1)} %collective-permute-done.7.other, bf16[320,800]{1,0:T(8,128)(2,1)S(1)} %convert_element_type.53.g0, ...), custom_call_target="tpu_custom_call" | custom-call | flops 491520000 | bytes 3895296 | tf_op jit(solution)/shard_map/pallas_call | solution.py:44
  83.5 0.0 copy-start
  83.5 1.1 collective-permute-done.6
  84.6 1.3 add_convert_fusion
  85.9 5.0 %all-to-all-start.2 = ((bf16[4,4,96,384]{3,2,1,0:T(8,128)(2,1)}), bf16[4,4,96,384]{3,2,1,0:T(8,128)(2,1)S(1)}, u32[]{:S(2)}, u32[]{:S(2)}) async-start(bf16[4,4,96,384]{3,2,1,0:T(8,128)(2,1)} %bitcast.12), calls=%async_computation.2 | async-start | bytes 2359296 | tf_op jit(solution)/shard_map/all_to_all | solution.py:228
  90.8 1.9 %collective-permute-start.10 = (bf16[320,800]{1,0:T(8,128)(2,1)}, bf16[320,800]{1,0:T(8,128)(2,1)}, u32[]{:S(2)}, u32[]{:S(2)}) collective-permute-start(bf16[320,800]{1,0:T(8,128)(2,1)} %copy-done.5), channel_id=1, source_target_pairs={{0,224},{32,256},{64,288},{96,320},{128,352},{160,384},{192,416},{... | collective-permute-start | bytes 1536008 | tf_op jit(solution)/shard_map/ppermute | solution.py:22
  92.8 1.6 %copy-done.1 = bf16[9,320,320]{2,1,0:T(8,128)(2,1)S(1)} copy-done((bf16[9,320,320]{2,1,0:T(8,128)(2,1)S(1)}, bf16[9,320,320]{2,1,0:T(8,128)(2,1)}, u32[]{:S(2)}) %copy-start.1) | copy-done | bytes 1843224
  94.4 4.2 %shard_map.63 = (bf16[320,800]{1,0:T(8,128)(2,1)}, bf16[320,800]{1,0:T(8,128)(2,1)}, f32[320,800]{1,0:T(8,128)S(1)}) custom-call(bf16[9,320,320]{2,1,0:T(8,128)(2,1)S(1)} %copy-done.1, bf16[320,800]{1,0:T(8,128)(2,1)S(1)} %convert_element_type.53.g0, bf16[320,800]{1,0:T(8,128)(2,1)S(1)} %collective-permute-done.2.gm1, ...), custom_call_target="tpu_custom_call" | custom-call | flops 1474560000 | bytes 4403200 | tf_op jit(solution)/shard_map/pallas_call | solution.py:44
  98.5 0.0 copy-start.3
  98.5 1.0 copy-done.3
  99.5 3.6 %collective-permute-start.12 = (bf16[320,800]{1,0:T(8,128)(2,1)}, bf16[320,800]{1,0:T(8,128)(2,1)}, u32[]{:S(2)}, u32[]{:S(2)}) collective-permute-start(bf16[320,800]{1,0:T(8,128)(2,1)} %get-tuple-element.44), channel_id=1, source_target_pairs={{0,128},{32,160},{64,192},{96,224},{128,256},{160,288},{192,320},{... | collective-permute-start | bytes 1536008 | tf_op jit(solution)/shard_map/ppermute | solution.py:22
  103.2 3.4 %collective-permute-start.13 = (bf16[320,800]{1,0:T(8,128)(2,1)}, bf16[320,800]{1,0:T(8,128)(2,1)}, u32[]{:S(2)}, u32[]{:S(2)}) collective-permute-start(bf16[320,800]{1,0:T(8,128)(2,1)} %get-tuple-element.45), channel_id=1, source_target_pairs={{0,384},{32,416},{64,448},{96,480},{128,0},{160,32},{192,64},{224,... | collective-permute-start | bytes 1536008 | tf_op jit(solution)/shard_map/ppermute | solution.py:22
  106.6 0.0 all-to-all-done.2.came
  106.6 0.0 copy-start.4
  106.6 0.2 shard_map.62
  106.8 3.9 %collective-permute-start.8 = (bf16[2,96,384]{2,1,0:T(8,128)(2,1)S(1)}, bf16[2,96,384]{2,1,0:T(8,128)(2,1)S(1)}, u32[]{:S(2)}, u32[]{:S(2)}) collective-permute-start(bf16[2,96,384]{2,1,0:T(8,128)(2,1)S(1)} %get-tuple-element.40), channel_id=1, source_target_pairs={{0,2},{1,7},{2,0},{3,5},{4,6},{5,3},{6,4},{7,1},{8,10},{9,15},{10,... | collective-permute-start | bytes 442376 | tf_op jit(solution)/shard_map/ppermute | solution.py:180
  110.8 3.8 %collective-permute-done.10 = bf16[320,800]{1,0:T(8,128)(2,1)} collective-permute-done((bf16[320,800]{1,0:T(8,128)(2,1)}, bf16[320,800]{1,0:T(8,128)(2,1)}, u32[]{:S(2)}, u32[]{:S(2)}) %collective-permute-start.10) | collective-permute-done | bytes 512032 | tf_op jit(solution)/shard_map/ppermute | solution.py:22
  114.5 1.3 add_convert_fusion.1
  115.9 1.9 %collective-permute-start.11 = (bf16[320,800]{1,0:T(8,128)(2,1)S(1)}, bf16[320,800]{1,0:T(8,128)(2,1)S(1)}, u32[]{:S(2)}, u32[]{:S(2)}) collective-permute-start(bf16[320,800]{1,0:T(8,128)(2,1)S(1)} %add_convert_fusion.1), channel_id=1, source_target_pairs={{0,480},{32,0},{64,32},{96,64},{128,96},{160,128},{192,160},{224,1... | collective-permute-start | bytes 1536008 | tf_op jit(solution)/shard_map/ppermute | solution.py:22
  117.8 1.8 %collective-permute-done.8 = bf16[2,96,384]{2,1,0:T(8,128)(2,1)S(1)} collective-permute-done((bf16[2,96,384]{2,1,0:T(8,128)(2,1)S(1)}, bf16[2,96,384]{2,1,0:T(8,128)(2,1)S(1)}, u32[]{:S(2)}, u32[]{:S(2)}) %collective-permute-start.8) | collective-permute-done | bytes 147488 | tf_op jit(solution)/shard_map/ppermute | solution.py:180
  119.7 3.7 %collective-permute-start.9 = (bf16[96,384]{1,0:T(8,128)(2,1)S(1)}, bf16[96,384]{1,0:T(8,128)(2,1)S(1)}, u32[]{:S(2)}, u32[]{:S(2)}) collective-permute-start(bf16[96,384]{1,0:T(8,128)(2,1)S(1)} %slice_bitcast_fusion), channel_id=1, source_target_pairs={{0,6},{1,3},{2,4},{3,1},{4,2},{5,7},{6,0},{7,5},{8,14},{9,11},{10,... | collective-permute-start | bytes 221192 | tf_op jit(solution)/shard_map/ppermute | solution.py:180
  123.4 2.5 %shard_map.64 = f32[320,800]{1,0:T(8,128)S(1)} custom-call(bf16[9,320,320]{2,1,0:T(8,128)(2,1)S(1)} %copy-done.2, bf16[320,800]{1,0:T(8,128)(2,1)S(1)} %convert_element_type.53.g0, bf16[320,800]{1,0:T(8,128)(2,1)S(1)} %collective-permute-done.2.gm1, bf16[320,800]{1,0:T(8,128)(2,1)S(1)} %collective-permute-done.3.gm4, ...), custom_call_target="tpu_custom_call" | custom-call | flops 655360000 | bytes 4403200 | tf_op jit(solution)/shard_map/pallas_call | solution.py:44
  126.0 11.3 %collective-permute-done.9 = bf16[96,384]{1,0:T(8,128)(2,1)S(1)} collective-permute-done((bf16[96,384]{1,0:T(8,128)(2,1)S(1)}, bf16[96,384]{1,0:T(8,128)(2,1)S(1)}, u32[]{:S(2)}, u32[]{:S(2)}) %collective-permute-start.9) | collective-permute-done | bytes 73760 | tf_op jit(solution)/shard_map/ppermute | solution.py:180
  137.3 0.0 copy-start.8
  137.3 0.0 collective-permute-done.12
  137.3 0.0 collective-permute-done.13
  137.3 0.0 collective-permute-done.11
  137.3 4.5 %collective-permute-start.15 = (bf16[96,384]{1,0:T(8,128)(2,1)S(1)}, bf16[96,384]{1,0:T(8,128)(2,1)S(1)}, u32[]{:S(2)}, u32[]{:S(2)}) collective-permute-start(bf16[96,384]{1,0:T(8,128)(2,1)S(1)} %fusion), channel_id=1, source_target_pairs={{7,199},{10,490},{14,142},{21,213},{28,156},{39,231},{42,10},{46,1... | collective-permute-start | bytes 221192 | tf_op jit(solution)/shard_map/ppermute | solution.py:233
  141.9 4.7 %collective-permute-start.14 = (bf16[96,384]{1,0:T(8,128)(2,1)S(1)}, bf16[96,384]{1,0:T(8,128)(2,1)S(1)}, u32[]{:S(2)}, u32[]{:S(2)}) collective-permute-start(bf16[96,384]{1,0:T(8,128)(2,1)S(1)} %fusion), channel_id=1, source_target_pairs={{0,0},{1,1},{2,2},{3,3},{4,4},{5,5},{6,6},{7,7},{8,200},{9,201},{1... | collective-permute-start | bytes 221192 | tf_op jit(solution)/shard_map/ppermute | solution.py:233
  146.6 2.5 %convert_add_fusion = f32[320,800]{1,0:T(8,128)} fusion(bf16[320,800]{1,0:T(8,128)(2,1)S(1)} %collective-permute-done.11, bf16[320,800]{1,0:T(8,128)(2,1)} %collective-permute-done.13, f32[320,800]{1,0:T(8,128)S(1)} %shard_map.64, bf16[320,800]{1,0:T(8,128)(2,1)} %collective-permute-done.12), kind=kLoop, calls=%fused_computation.1 | loop fusion | flops 1536000 | bytes 3584000 | tf_op jit(solution)/shard_map/add | solution.py:238
  149.0 0.0 collective-permute-done.15
  149.0 11.6 %collective-permute-done.14 = bf16[96,384]{1,0:T(8,128)(2,1)S(1)} collective-permute-done((bf16[96,384]{1,0:T(8,128)(2,1)S(1)}, bf16[96,384]{1,0:T(8,128)(2,1)S(1)}, u32[]{:S(2)}, u32[]{:S(2)}) %collective-permute-start.14) | collective-permute-done | bytes 73760 | tf_op jit(solution)/shard_map/ppermute | solution.py:233
  160.6 0.8 bitcast_add_fusion
  (12 shorter events, 0.1 us)
Async XLA Ops:
  0.6 11.7 %collective-permute-start.1 = (bf16[90,320]{1,0:T(8,128)(2,1)}, bf16[90,320]{1,0:T(8,128)(2,1)S(1)}, u32[]{:S(2)}, u32[]{:S(2)}) collective-permute-start(bf16[90,320]{1,0:T(8,128)(2,1)} %bitcast.13), channel_id=1, source_target_pairs={{199,7},{490,10},{142,14},{213,21},{156,28},{231,39},{10,42},{174,... | collective-permute-start | bytes 172808 | tf_op jit(solution)/shard_map/ppermute | solution.py:169
  4.5 8.3 %collective-permute-start = (bf16[90,320]{1,0:T(8,128)(2,1)}, bf16[90,320]{1,0:T(8,128)(2,1)S(1)}, u32[]{:S(2)}, u32[]{:S(2)}) collective-permute-start(bf16[90,320]{1,0:T(8,128)(2,1)} %bitcast.14), channel_id=1, source_target_pairs={{0,0},{1,1},{2,2},{3,3},{4,4},{5,5},{6,6},{7,7},{200,8},{201,9},{2... | collective-permute-start | bytes 172808 | tf_op jit(solution)/shard_map/ppermute | solution.py:168
  14.0 25.7 %collective-permute-start.2 = (bf16[320,800]{1,0:T(8,128)(2,1)S(1)}, bf16[320,800]{1,0:T(8,128)(2,1)S(1)}, u32[]{:S(2)}, u32[]{:S(2)}) collective-permute-start(bf16[320,800]{1,0:T(8,128)(2,1)S(1)} %convert_element_type.53.g0), channel_id=1, source_target_pairs={{0,32},{32,64},{64,96},{96,128},{128,160},{160,192},{192,224},{224... | collective-permute-start | bytes 1536008 | tf_op jit(solution)/shard_map/ppermute | solution.py:22
  20.2 28.7 %all-to-all-start = ((bf16[4,96,384]{2,1,0:T(8,128)(2,1)}), bf16[4,96,384]{2,1,0:T(8,128)(2,1)S(1)}, u32[]{:S(2)}, u32[]{:S(2)}) async-start(bf16[4,96,384]{2,1,0:T(8,128)(2,1)} %broadcast_in_dim.4), calls=%async_computation | async-start | bytes 589824 | tf_op jit(solution)/shard_map/all_to_all | solution.py:182
  27.4 29.0 %collective-permute-start.4 = (bf16[320,800]{1,0:T(8,128)(2,1)S(1)}, bf16[320,800]{1,0:T(8,128)(2,1)S(1)}, u32[]{:S(2)}, u32[]{:S(2)}) collective-permute-start(bf16[320,800]{1,0:T(8,128)(2,1)S(1)} %convert_element_type.53.g0), channel_id=1, source_target_pairs={{0,384},{32,416},{64,448},{96,480},{128,0},{160,32},{192,64},{224,... | collective-permute-start | bytes 1536008 | tf_op jit(solution)/shard_map/ppermute | solution.py:22
  32.4 26.1 %collective-permute-start.3 = (bf16[320,800]{1,0:T(8,128)(2,1)S(1)}, bf16[320,800]{1,0:T(8,128)(2,1)S(1)}, u32[]{:S(2)}, u32[]{:S(2)}) collective-permute-start(bf16[320,800]{1,0:T(8,128)(2,1)S(1)} %convert_element_type.53.g0), channel_id=1, source_target_pairs={{0,128},{32,160},{64,192},{96,224},{128,256},{160,288},{192,320},{... | collective-permute-start | bytes 1536008 | tf_op jit(solution)/shard_map/ppermute | solution.py:22
  39.7 18.8 %collective-permute-start.5 = (bf16[320,800]{1,0:T(8,128)(2,1)S(1)}, bf16[320,800]{1,0:T(8,128)(2,1)}, u32[]{:S(2)}, u32[]{:S(2)}) collective-permute-start(bf16[320,800]{1,0:T(8,128)(2,1)S(1)} %collective-permute-done.2.gm1), channel_id=1, source_target_pairs={{0,288},{32,320},{64,352},{96,384},{128,416},{160,448},{192,480},{... | collective-permute-start | bytes 1536008 | tf_op jit(solution)/shard_map/ppermute | solution.py:22
  50.1 22.1 %all-to-all-start.1 = ((bf16[4,4,96,384]{3,2,1,0:T(8,128)(2,1)}), bf16[4,4,96,384]{3,2,1,0:T(8,128)(2,1)S(1)}, u32[]{:S(2)}, u32[]{:S(2)}) async-start(bf16[4,4,96,384]{3,2,1,0:T(8,128)(2,1)} %broadcast_in_dim.5), calls=%async_computation.1 | async-start | bytes 2359296 | tf_op jit(solution)/shard_map/all_to_all | solution.py:183
  59.1 0.7 copy-start.6
  72.2 9.6 %collective-permute-start.7 = (bf16[4,4,96,384]{3,2,1,0:T(8,128)(2,1)S(1)}, bf16[4,4,96,384]{3,2,1,0:T(8,128)(2,1)S(1)}, u32[]{:S(2)}, u32[]{:S(2)}) collective-permute-start(bf16[4,4,96,384]{3,2,1,0:T(8,128)(2,1)S(1)} %all-to-all-done.1.mine), channel_id=1, source_target_pairs={{0,1},{1,0},{2,3},{3,2},{4,5},{5,4},{6,7},{7,6},{8,9},{9,8},{10,11... | collective-permute-start | bytes 3538952 | tf_op jit(solution)/shard_map/ppermute | solution.py:22
  74.6 0.9 copy-start.7
  79.8 4.7 %collective-permute-start.6 = (bf16[16,96,384]{2,1,0:T(8,128)(2,1)S(1)}, bf16[16,96,384]{2,1,0:T(8,128)(2,1)S(1)}, u32[]{:S(2)}, u32[]{:S(2)}) collective-permute-start(bf16[16,96,384]{2,1,0:T(8,128)(2,1)S(1)} %get-tuple-element.33), channel_id=1, source_target_pairs={{0,1},{1,0},{2,3},{3,2},{4,5},{5,4},{6,7},{7,6},{8,9},{9,8},{10,11... | collective-permute-start | bytes 3538952 | tf_op jit(solution)/shard_map/ppermute | solution.py:22
  83.5 2.4 %copy-start = (bf16[9,320,320]{2,1,0:T(8,128)(2,1)}, bf16[9,320,320]{2,1,0:T(8,128)(2,1)S(1)}, u32[]{:S(2)}) copy-start(bf16[9,320,320]{2,1,0:T(8,128)(2,1)S(1)} %get-tuple-element.41.tiles) | copy-start | bytes 5529604
  83.5 2.4 %copy-start.5 = (bf16[320,800]{1,0:T(8,128)(2,1)}, bf16[320,800]{1,0:T(8,128)(2,1)S(1)}, u32[]{:S(2)}) copy-start(bf16[320,800]{1,0:T(8,128)(2,1)S(1)} %get-tuple-element.43) | copy-start | bytes 1536004
  85.9 20.7 %all-to-all-start.2 = ((bf16[4,4,96,384]{3,2,1,0:T(8,128)(2,1)}), bf16[4,4,96,384]{3,2,1,0:T(8,128)(2,1)S(1)}, u32[]{:S(2)}, u32[]{:S(2)}) async-start(bf16[4,4,96,384]{3,2,1,0:T(8,128)(2,1)} %bitcast.12), calls=%async_computation.2 | async-start | bytes 2359296 | tf_op jit(solution)/shard_map/all_to_all | solution.py:228
  90.8 23.7 %collective-permute-start.10 = (bf16[320,800]{1,0:T(8,128)(2,1)}, bf16[320,800]{1,0:T(8,128)(2,1)}, u32[]{:S(2)}, u32[]{:S(2)}) collective-permute-start(bf16[320,800]{1,0:T(8,128)(2,1)} %copy-done.5), channel_id=1, source_target_pairs={{0,224},{32,256},{64,288},{96,320},{128,352},{160,384},{192,416},{... | collective-permute-start | bytes 1536008 | tf_op jit(solution)/shard_map/ppermute | solution.py:22
  92.8 1.6 %copy-start.1 = (bf16[9,320,320]{2,1,0:T(8,128)(2,1)S(1)}, bf16[9,320,320]{2,1,0:T(8,128)(2,1)}, u32[]{:S(2)}) copy-start(bf16[9,320,320]{2,1,0:T(8,128)(2,1)} %copy-done) | copy-start | bytes 5529604
  98.5 1.0 copy-start.3
  99.5 37.7 %collective-permute-start.12 = (bf16[320,800]{1,0:T(8,128)(2,1)}, bf16[320,800]{1,0:T(8,128)(2,1)}, u32[]{:S(2)}, u32[]{:S(2)}) collective-permute-start(bf16[320,800]{1,0:T(8,128)(2,1)} %get-tuple-element.44), channel_id=1, source_target_pairs={{0,128},{32,160},{64,192},{96,224},{128,256},{160,288},{192,320},{... | collective-permute-start | bytes 1536008 | tf_op jit(solution)/shard_map/ppermute | solution.py:22
  103.2 34.1 %collective-permute-start.13 = (bf16[320,800]{1,0:T(8,128)(2,1)}, bf16[320,800]{1,0:T(8,128)(2,1)}, u32[]{:S(2)}, u32[]{:S(2)}) collective-permute-start(bf16[320,800]{1,0:T(8,128)(2,1)} %get-tuple-element.45), channel_id=1, source_target_pairs={{0,384},{32,416},{64,448},{96,480},{128,0},{160,32},{192,64},{224,... | collective-permute-start | bytes 1536008 | tf_op jit(solution)/shard_map/ppermute | solution.py:22
  106.6 7.9 %copy-start.4 = (f32[320,800]{1,0:T(8,128)S(1)}, f32[320,800]{1,0:T(8,128)}, u32[]{:S(2)}) copy-start(f32[320,800]{1,0:T(8,128)} %copy-done.3) | copy-start | bytes 3072004
  106.8 12.8 %collective-permute-start.8 = (bf16[2,96,384]{2,1,0:T(8,128)(2,1)S(1)}, bf16[2,96,384]{2,1,0:T(8,128)(2,1)S(1)}, u32[]{:S(2)}, u32[]{:S(2)}) collective-permute-start(bf16[2,96,384]{2,1,0:T(8,128)(2,1)S(1)} %get-tuple-element.40), channel_id=1, source_target_pairs={{0,2},{1,7},{2,0},{3,5},{4,6},{5,3},{6,4},{7,1},{8,10},{9,15},{10,... | collective-permute-start | bytes 442376 | tf_op jit(solution)/shard_map/ppermute | solution.py:180
  114.5 8.9 %copy-start.2 = (bf16[9,320,320]{2,1,0:T(8,128)(2,1)S(1)}, bf16[9,320,320]{2,1,0:T(8,128)(2,1)}, u32[]{:S(2)}) copy-start(bf16[9,320,320]{2,1,0:T(8,128)(2,1)} %copy-done) | copy-start | bytes 5529604
  115.9 21.4 %collective-permute-start.11 = (bf16[320,800]{1,0:T(8,128)(2,1)S(1)}, bf16[320,800]{1,0:T(8,128)(2,1)S(1)}, u32[]{:S(2)}, u32[]{:S(2)}) collective-permute-start(bf16[320,800]{1,0:T(8,128)(2,1)S(1)} %add_convert_fusion.1), channel_id=1, source_target_pairs={{0,480},{32,0},{64,32},{96,64},{128,96},{160,128},{192,160},{224,1... | collective-permute-start | bytes 1536008 | tf_op jit(solution)/shard_map/ppermute | solution.py:22
  119.7 17.6 %collective-permute-start.9 = (bf16[96,384]{1,0:T(8,128)(2,1)S(1)}, bf16[96,384]{1,0:T(8,128)(2,1)S(1)}, u32[]{:S(2)}, u32[]{:S(2)}) collective-permute-start(bf16[96,384]{1,0:T(8,128)(2,1)S(1)} %slice_bitcast_fusion), channel_id=1, source_target_pairs={{0,6},{1,3},{2,4},{3,1},{4,2},{5,7},{6,0},{7,5},{8,14},{9,11},{10,... | collective-permute-start | bytes 221192 | tf_op jit(solution)/shard_map/ppermute | solution.py:180
  137.3 23.3 %copy-start.8 = (f32[320,90]{0,1:T(8,128)S(1)}, f32[320,90]{0,1:T(8,128)}, u32[]{:S(2)}) copy-start(f32[320,90]{0,1:T(8,128)} %param.5) | copy-start | bytes 345604
  137.3 11.7 %collective-permute-start.15 = (bf16[96,384]{1,0:T(8,128)(2,1)S(1)}, bf16[96,384]{1,0:T(8,128)(2,1)S(1)}, u32[]{:S(2)}, u32[]{:S(2)}) collective-permute-start(bf16[96,384]{1,0:T(8,128)(2,1)S(1)} %fusion), channel_id=1, source_target_pairs={{7,199},{10,490},{14,142},{21,213},{28,156},{39,231},{42,10},{46,1... | collective-permute-start | bytes 221192 | tf_op jit(solution)/shard_map/ppermute | solution.py:233
  141.9 18.7 %collective-permute-start.14 = (bf16[96,384]{1,0:T(8,128)(2,1)S(1)}, bf16[96,384]{1,0:T(8,128)(2,1)S(1)}, u32[]{:S(2)}, u32[]{:S(2)}) collective-permute-start(bf16[96,384]{1,0:T(8,128)(2,1)S(1)} %fusion), channel_id=1, source_target_pairs={{0,0},{1,1},{2,2},{3,3},{4,4},{5,5},{6,6},{7,7},{8,200},{9,201},{1... | collective-permute-start | bytes 221192 | tf_op jit(solution)/shard_map/ppermute | solution.py:233

commit v5 on v4

--- a/solution.py
+++ b/solution.py
@@ -12,9 +12,7 @@
 COL = ("x", "zh", "core")
 ALL = ("row",) + COL
 TILES = ((0, 0), (0, -1), (6, 4), (-1, -4), (4, 0), (4, -1), (6, 0), (6, -1), (4, -4))
-LATE = tuple(range(1, len(TILES)))
 HIDES = 10**10
-EARLY = (0,)
 
 
 def passed_along(x, axis, by):
@@ -52,22 +50,14 @@
     )(*args)
 
 
-def early_gram(g0, out):
-    out[0] = dot(g0[...], g0[...], ((1,), (1,))).astype(out.dtype)
-
-
-def late_gram(g0, gm1, gm4, g4, g6, early, keep, give, flat):
+def gram(g0, gm1, gm4, g4, g6, keep, give, flat):
     held = {0: g0, -1: gm1, -4: gm4, 4: g4, 6: g6}
     core = lax.axis_index("core")
-    rows = early.shape[1]
+    rows = g0.shape[0]
     count, full, _ = keep.shape
     shard = len(TILES) * rows // (2 * count)
     for k, (a, b) in enumerate(TILES):
-        if k in LATE:
-            tile = dot(held[b][...], held[a][...], ((1,), (1,)))
-        else:
-            tile = early[EARLY.index(k)].astype(jnp.float32)
-        flat[k * rows : (k + 1) * rows, :rows] = tile
+        flat[k * rows : (k + 1) * rows, :rows] = dot(held[b][...], held[a][...], ((1,), (1,)))
 
     def put(outs):
         for q in range(count):
@@ -82,6 +72,11 @@
     @pl.when(core == 1)
     def _():
         put((give, keep))
+
+
+def core_sum(keep, came, out):
+    for q in range(out.shape[0]):
+        out[q] = (keep[q].astype(jnp.float32) + came[q].astype(jnp.float32)).astype(out.dtype)
 
 
 def partner(zh, core, turn):
@@ -181,7 +176,6 @@
 
     piece = lax.all_to_all(jnp.broadcast_to(piece[None], (nzh,) + piece.shape), "zh", 0, 0, tiled=True)
     piece = lax.all_to_all(jnp.broadcast_to(piece[None], (nx,) + piece.shape), "x", 0, 0, tiled=True)
-    pieces = (piece, passed_along(piece, "core", 1))
 
     g0 = gradient.astype(bf16)
     gm1 = passed_along(g0, "row", 1)
@@ -196,15 +190,16 @@
     g6 = passed_along(gm1, "row", -7)
     g0, gm1, gm4, g4, g6 = blocks = lax.optimization_barrier((g0, gm1, gm4, g4, g6))
     chunks = (nx * nzh, full, lanes)
-    (early,) = call(early_gram, [((len(EARLY), rows, rows), bf16)], (g0,), flops=HIDES)
     keep, give = call(
-        late_gram,
+        gram,
         [(chunks, bf16)] * 2,
-        (*blocks, early),
+        blocks,
         [pltpu.VMEM((len(TILES) * rows + 8, lanes), f32)],
         flops=HIDES,
     )
+    give, piece = lax.optimization_barrier((give, piece))
     came = passed_along(give, "core", 1)
+    pieces = (piece, passed_along(piece, "core", 1))
 
     shape = g0.shape
     tiles, out6 = call(
@@ -214,7 +209,6 @@
         [pltpu.VMEM((len(TILES) * rows, rows), f32)],
         flops=3 * product,
     )
-    came, tiles, out6 = lax.optimization_barrier((came, tiles, out6))
     out4, outm4, outm1 = call(
         functools.partial(products, (4, -4, -1)),
         [(shape, bf16), (shape, bf16), (shape, f32)],
@@ -224,15 +218,28 @@
     came4, camem4 = passed_along(out4, "row", 4), passed_along(outm4, "row", -4)
     chained = (outm1 + passed_along(out6, "row", 7).astype(f32)).astype(bf16)
     camem1 = passed_along(chained, "row", -1)
-    sent = (keep.astype(f32) + came.astype(f32)).astype(bf16).reshape(nx, nzh, full, lanes)
+    (sent,) = call(core_sum, [(chunks, bf16)], (keep, came), flops=HIDES)
+    sent = sent.reshape(nx, nzh, full, lanes)
     got = lax.all_to_all(sent, "x", 0, 0, tiled=True)
     mine, sent = call(x_sum, [((2, full, lanes), bf16)] * 2, (got,))
     mine = (mine.astype(f32) + traded(sent, 0).astype(f32)).astype(bf16)
-    total = (mine[0].astype(f32) + traded(mine[1], 1).astype(f32)).astype(bf16)
-    total, camem1, came4, camem4 = lax.optimization_barrier((total, camem1, came4, camem4))
-    one, two = (lax.ppermute(total, ALL, [(b, a) for a, b in pairs(pick, 0)]) for pick in (2, 3))
-    one, two = one[:shard, :rows], two[:shard, :rows]
-    share = jnp.where(place_in_shard < cut, one, two).astype(f32).T
+    mine, came4, camem4 = lax.optimization_barrier((mine, came4, camem4))
+    halves = []
+    for pick in (2, 3):
+        parts = []
+        for n in (0, 1):
+            route = []
+            for i in range(n_row):
+                for r in routes:
+                    x_zh, c = divmod(r[0], ncore)
+                    x, zh = divmod(x_zh, nzh)
+                    source = (x * nzh + (partner(zh, c, 1) if n else zh)) * ncore + c
+                    if pick == 2 or r[2] != r[3]:
+                        route.append((i * n_col + source, (i + r[pick]) % n_row * n_col + r[0]))
+            parts.append(lax.ppermute(mine[n], ALL, route)[:shard, :rows].astype(f32))
+        halves.append(parts[0] + parts[1])
+    one, two = halves
+    share = jnp.where(place_in_shard < cut, one, two).T
     statistic = 0.9 * previous + 0.1 / INTER * share
     (out0,) = call(functools.partial(products, (0,)), [(shape, f32)], (tiles, *blocks), flops=4 * product)
     applied = out0 + came4.astype(f32) + camem4.astype(f32) + camem1.astype(f32)

time: 162 us -> 163 us (level)
  the two profiles are of different devices: /device:TPU:162 before, /device:TPU:74 now
where the time goes in v5:
time: 163 us; the launch traced here: 162 us
  starting transfers between devices  97.7 us (60%)
  waiting for transfers between devices  32.7 us (20%)
  Pallas kernels  15.8 us (10%)
  local copies, waits for them, and re-layouts  8.55 us (5%)
  other arithmetic  6.57 us (4%)
    ppermute x10, starting transfers between devices, passed_along(): return lax.ppermute(x, axis, [(i, (i + by) % count) for i in range(count)])  42.4 us
    ppermute x4, starting transfers between devices, local(): parts.append(lax.ppermute(mine[n], ALL, route)[:shard, :rows].astype(f32))  18.8 us
    pallas_call x6, Pallas kernels, call(): pl.pallas_call(kernel, out_shape=[jax.ShapeDtypeStruct(s, d) for s, d in...  15.8 us
    ppermute x1, starting transfers between devices, traded(): return lax.ppermute(x, ('zh', 'core'), turns[turn])  10.8 us
    all_to_all x1, starting transfers between devices, local(): lax.all_to_all(jnp.broadcast_to(piece[None], (nzh,) + piece.shape), 'zh',...  10.1 us
    ppermute x1, waiting for transfers between devices, traded(): return lax.ppermute(x, ('zh', 'core'), turns[turn])  9.39 us
    all_to_all x1, starting transfers between devices, local(): lax.all_to_all(jnp.broadcast_to(piece[None], (nx,) + piece.shape), 'x', 0...  7.93 us
    ppermute x4, waiting for transfers between devices, local(): parts.append(lax.ppermute(mine[n], ALL, route)[:shard, :rows].astype(f32))  5.71 us
  transfers between devices with their start and end apart: 20, of which 8 were waited for; matrix products, arithmetic and copies ran while one was open for 5% of the time, Pallas kernels for 10%

profile of v5, /device:TPU:74, one launch (start us, length us, event | category | flops | bytes accessed | tf_op | source)
XLA Modules:
  0.0 162.3 jit_solution(6027792678185799236)
XLA Ops:
  0.6 1.9 %collective-permute-start = (bf16[90,320]{1,0:T(8,128)(2,1)}, bf16[90,320]{1,0:T(8,128)(2,1)S(1)}, u32[]{:S(2)}, u32[]{:S(2)}) collective-permute-start(bf16[90,320]{1,0:T(8,128)(2,1)} %bitcast.10), channel_id=1, source_target_pairs={{0,0},{1,1},{2,2},{3,3},{4,4},{5,5},{6,6},{7,7},{200,8},{201,9},{2... | collective-permute-start | bytes 172808 | tf_op jit(solution)/shard_map/ppermute | solution.py:163
  2.6 0.7 collective-permute-start.1
  3.2 1.2 dynamic_slice.3
  4.5 0.6 iota_compare_fusion
  5.1 5.2 %collective-permute-done = bf16[90,320]{1,0:T(8,128)(2,1)S(1)} collective-permute-done((bf16[90,320]{1,0:T(8,128)(2,1)}, bf16[90,320]{1,0:T(8,128)(2,1)S(1)}, u32[]{:S(2)}, u32[]{:S(2)}) %collective-permute-start) | collective-permute-done | bytes 57632 | tf_op jit(solution)/shard_map/ppermute | solution.py:163
  10.4 0.0 collective-permute-done.1
  10.4 1.3 convert_element_type.41.g0
  11.7 4.6 %collective-permute-start.2 = (bf16[320,800]{1,0:T(8,128)(2,1)S(1)}, bf16[320,800]{1,0:T(8,128)(2,1)S(1)}, u32[]{:S(2)}, u32[]{:S(2)}) collective-permute-start(bf16[320,800]{1,0:T(8,128)(2,1)S(1)} %convert_element_type.41.g0), channel_id=1, source_target_pairs={{0,32},{32,64},{64,96},{96,128},{128,160},{160,192},{192,224},{224... | collective-permute-start | bytes 1536008 | tf_op jit(solution)/shard_map/ppermute | solution.py:20
  16.3 0.1 broadcast_select_fusion
  16.4 0.7 broadcast_in_dim.4
  17.2 10.1 %all-to-all-start = ((bf16[4,96,384]{2,1,0:T(8,128)(2,1)}), bf16[4,96,384]{2,1,0:T(8,128)(2,1)S(1)}, u32[]{:S(2)}, u32[]{:S(2)}) async-start(bf16[4,96,384]{2,1,0:T(8,128)(2,1)} %broadcast_in_dim.4), calls=%async_computation | async-start | bytes 589824 | tf_op jit(solution)/shard_map/all_to_all | solution.py:177
  27.3 3.2 %collective-permute-start.3 = (bf16[320,800]{1,0:T(8,128)(2,1)S(1)}, bf16[320,800]{1,0:T(8,128)(2,1)S(1)}, u32[]{:S(2)}, u32[]{:S(2)}) collective-permute-start(bf16[320,800]{1,0:T(8,128)(2,1)S(1)} %convert_element_type.41.g0), channel_id=1, source_target_pairs={{0,128},{32,160},{64,192},{96,224},{128,256},{160,288},{192,320},{... | collective-permute-start | bytes 1536008 | tf_op jit(solution)/shard_map/ppermute | solution.py:20
  30.5 2.7 %collective-permute-start.4 = (bf16[320,800]{1,0:T(8,128)(2,1)S(1)}, bf16[320,800]{1,0:T(8,128)(2,1)S(1)}, u32[]{:S(2)}, u32[]{:S(2)}) collective-permute-start(bf16[320,800]{1,0:T(8,128)(2,1)S(1)} %convert_element_type.41.g0), channel_id=1, source_target_pairs={{0,384},{32,416},{64,448},{96,480},{128,0},{160,32},{192,64},{224,... | collective-permute-start | bytes 1536008 | tf_op jit(solution)/shard_map/ppermute | solution.py:20
  33.2 2.1 %collective-permute-done.2.gm1 = bf16[320,800]{1,0:T(8,128)(2,1)S(1)} collective-permute-done((bf16[320,800]{1,0:T(8,128)(2,1)S(1)}, bf16[320,800]{1,0:T(8,128)(2,1)S(1)}, u32[]{:S(2)}, u32[]{:S(2)}) %collective-permute-start.2) | collective-permute-done | bytes 512032 | tf_op jit(solution)/shard_map/ppermute | solution.py:20
  35.3 7.6 %collective-permute-start.5 = (bf16[320,800]{1,0:T(8,128)(2,1)S(1)}, bf16[320,800]{1,0:T(8,128)(2,1)}, u32[]{:S(2)}, u32[]{:S(2)}) collective-permute-start(bf16[320,800]{1,0:T(8,128)(2,1)S(1)} %collective-permute-done.2.gm1), channel_id=1, source_target_pairs={{0,288},{32,320},{64,352},{96,384},{128,416},{160,448},{192,480},{... | collective-permute-start | bytes 1536008 | tf_op jit(solution)/shard_map/ppermute | solution.py:20
  42.9 3.7 %all-to-all-done = bf16[4,96,384]{2,1,0:T(8,128)(2,1)S(1)} async-done(((bf16[4,96,384]{2,1,0:T(8,128)(2,1)}), bf16[4,96,384]{2,1,0:T(8,128)(2,1)S(1)}, u32[]{:S(2)}, u32[]{:S(2)}) %all-to-all-start) | async-done | bytes 294944 | tf_op jit(solution)/shard_map/all_to_all | solution.py:177
  46.6 1.1 broadcast_in_dim.5
  47.8 7.9 %all-to-all-start.1 = ((bf16[4,4,96,384]{3,2,1,0:T(8,128)(2,1)}), bf16[4,4,96,384]{3,2,1,0:T(8,128)(2,1)S(1)}, u32[]{:S(2)}, u32[]{:S(2)}) async-start(bf16[4,4,96,384]{3,2,1,0:T(8,128)(2,1)} %broadcast_in_dim.5), calls=%async_computation.1 | async-start | bytes 2359296 | tf_op jit(solution)/shard_map/all_to_all | solution.py:178
  55.7 0.0 collective-permute-done.3.gm4
  55.7 1.7 %collective-permute-done.4.g4 = bf16[320,800]{1,0:T(8,128)(2,1)S(1)} collective-permute-done((bf16[320,800]{1,0:T(8,128)(2,1)S(1)}, bf16[320,800]{1,0:T(8,128)(2,1)S(1)}, u32[]{:S(2)}, u32[]{:S(2)}) %collective-permute-start.4) | collective-permute-done | bytes 512032 | tf_op jit(solution)/shard_map/ppermute | solution.py:20
  57.4 0.0 collective-permute-done.5.g6
  57.4 4.8 %shard_map.59 = (bf16[16,96,384]{2,1,0:T(8,128)(2,1)S(1)}, bf16[16,96,384]{2,1,0:T(8,128)(2,1)S(1)}) custom-call(bf16[320,800]{1,0:T(8,128)(2,1)S(1)} %convert_element_type.41.g0, bf16[320,800]{1,0:T(8,128)(2,1)S(1)} %collective-permute-done.2.gm1, bf16[320,800]{1,0:T(8,128)(2,1)S(1)} %collective-permute-done.3.gm4, ...), custom_call_target="tpu_custom_call" | custom-call | flops 10000000000 | bytes 2560000 | tf_op jit(solution)/shard_map/pallas_call | solution.py:42
  62.2 0.0 copy-done.6
  62.3 1.0 copy-done.9
  63.3 1.0 copy-done.10
  64.3 4.2 %all-to-all-done.1.mine = bf16[4,4,96,384]{3,2,1,0:T(8,128)(2,1)S(1)} async-done(((bf16[4,4,96,384]{3,2,1,0:T(8,128)(2,1)}), bf16[4,4,96,384]{3,2,1,0:T(8,128)(2,1)S(1)}, u32[]{:S(2)}, u32[]{:S(2)}) %all-to-all-start.1) | async-done | bytes 1179680 | tf_op jit(solution)/shard_map/all_to_all | solution.py:178
  68.5 1.9 %collective-permute-start.6 = (bf16[16,96,384]{2,1,0:T(8,128)(2,1)}, bf16[16,96,384]{2,1,0:T(8,128)(2,1)S(1)}, u32[]{:S(2)}, u32[]{:S(2)}) collective-permute-start(bf16[16,96,384]{2,1,0:T(8,128)(2,1)} %copy-done.9), channel_id=1, source_target_pairs={{0,1},{1,0},{2,3},{3,2},{4,5},{5,4},{6,7},{7,6},{8,9},{9,8},{10,11... | collective-permute-start | bytes 3538952 | tf_op jit(solution)/shard_map/ppermute | solution.py:20
  70.4 2.4 %collective-permute-start.8 = (bf16[4,4,96,384]{3,2,1,0:T(8,128)(2,1)S(1)}, bf16[4,4,96,384]{3,2,1,0:T(8,128)(2,1)}, u32[]{:S(2)}, u32[]{:S(2)}) collective-permute-start(bf16[4,4,96,384]{3,2,1,0:T(8,128)(2,1)S(1)} %all-to-all-done.1.mine), channel_id=1, source_target_pairs={{0,1},{1,0},{2,3},{3,2},{4,5},{5,4},{6,7},{7,6},{8,9},{9,8},{10,11... | collective-permute-start | bytes 3538952 | tf_op jit(solution)/shard_map/ppermute | solution.py:20
  72.8 0.6 collective-permute-done.6.came
  73.4 1.3 copy-done.11
  74.7 0.3 shard_map.60
  75.0 0.0 copy-start.5
  75.0 1.0 copy-done.5
  76.0 5.0 %all-to-all-start.2 = ((bf16[4,4,96,384]{3,2,1,0:T(8,128)(2,1)}), bf16[4,4,96,384]{3,2,1,0:T(8,128)(2,1)S(1)}, u32[]{:S(2)}, u32[]{:S(2)}) async-start(bf16[4,4,96,384]{3,2,1,0:T(8,128)(2,1)} %bitcast.9), calls=%async_computation.2 | async-start | bytes 2359296 | tf_op jit(solution)/shard_map/all_to_all | solution.py:223
  81.0 0.0 collective-permute-done.8.other
  81.0 1.1 copy-done.1
  82.0 3.8 %shard_map.62 = (bf16[9,320,320]{2,1,0:T(8,128)(2,1)S(1)}, bf16[320,800]{1,0:T(8,128)(2,1)}) custom-call(bf16[4,4,96,384]{3,2,1,0:T(8,128)(2,1)S(1)} %all-to-all-done.1.mine, bf16[4,4,96,384]{3,2,1,0:T(8,128)(2,1)} %collective-permute-done.8.other, bf16[320,800]{1,0:T(8,128)(2,1)S(1)} %convert_element_type.41.g0, ...), custom_call_target="tpu_custom_call" | custom-call | flops 491520000 | bytes 3895296 | tf_op jit(solution)/shard_map/pallas_call | solution.py:42
  85.9 12.3 %collective-permute-start.15 = (bf16[320,800]{1,0:T(8,128)(2,1)}, bf16[320,800]{1,0:T(8,128)(2,1)}, u32[]{:S(2)}, u32[]{:S(2)}) collective-permute-start(bf16[320,800]{1,0:T(8,128)(2,1)} %get-tuple-element.45), channel_id=1, source_target_pairs={{0,224},{32,256},{64,288},{96,320},{128,352},{160,384},{192,416},{... | collective-permute-start | bytes 1536008 | tf_op jit(solution)/shard_map/ppermute | solution.py:20
  98.2 4.2 %shard_map.63 = (bf16[320,800]{1,0:T(8,128)(2,1)}, bf16[320,800]{1,0:T(8,128)(2,1)}, f32[320,800]{1,0:T(8,128)S(1)}) custom-call(bf16[9,320,320]{2,1,0:T(8,128)(2,1)S(1)} %get-tuple-element.38.tiles, bf16[320,800]{1,0:T(8,128)(2,1)S(1)} %convert_element_type.41.g0, bf16[320,800]{1,0:T(8,128)(2,1)S(1)} %collective-permute-done.2.gm1, ...), custom_call_target="tpu_custom_call" | custom-call | flops 1474560000 | bytes 4403200 | tf_op jit(solution)/shard_map/pallas_call | solution.py:42
  102.3 1.9 %collective-permute-start.9 = (bf16[320,800]{1,0:T(8,128)(2,1)}, bf16[320,800]{1,0:T(8,128)(2,1)}, u32[]{:S(2)}, u32[]{:S(2)}) collective-permute-start(bf16[320,800]{1,0:T(8,128)(2,1)} %get-tuple-element.39), channel_id=1, source_target_pairs={{0,128},{32,160},{64,192},{96,224},{128,256},{160,288},{192,320},{... | collective-permute-start | bytes 1536008 | tf_op jit(solution)/shard_map/ppermute | solution.py:20
  104.3 3.9 %collective-permute-start.10 = (bf16[320,800]{1,0:T(8,128)(2,1)}, bf16[320,800]{1,0:T(8,128)(2,1)}, u32[]{:S(2)}, u32[]{:S(2)}) collective-permute-start(bf16[320,800]{1,0:T(8,128)(2,1)} %get-tuple-element.40), channel_id=1, source_target_pairs={{0,384},{32,416},{64,448},{96,480},{128,0},{160,32},{192,64},{224,... | collective-permute-start | bytes 1536008 | tf_op jit(solution)/shard_map/ppermute | solution.py:20
  108.2 0.0 all-to-all-done.2.came
  108.2 0.2 shard_map.61
  108.4 10.8 %collective-permute-start.7 = (bf16[2,96,384]{2,1,0:T(8,128)(2,1)S(1)}, bf16[2,96,384]{2,1,0:T(8,128)(2,1)S(1)}, u32[]{:S(2)}, u32[]{:S(2)}) collective-permute-start(bf16[2,96,384]{2,1,0:T(8,128)(2,1)S(1)} %get-tuple-element.36), channel_id=1, source_target_pairs={{0,2},{1,7},{2,0},{3,5},{4,6},{5,3},{6,4},{7,1},{8,10},{9,15},{10,... | collective-permute-start | bytes 442376 | tf_op jit(solution)/shard_map/ppermute | solution.py:175
  119.2 0.0 collective-permute-done.15
  119.3 0.0 copy-start.2
  119.3 1.3 add_convert_fusion
  120.5 1.9 %collective-permute-start.16 = (bf16[320,800]{1,0:T(8,128)(2,1)S(1)}, bf16[320,800]{1,0:T(8,128)(2,1)S(1)}, u32[]{:S(2)}, u32[]{:S(2)}) collective-permute-start(bf16[320,800]{1,0:T(8,128)(2,1)S(1)} %add_convert_fusion), channel_id=1, source_target_pairs={{0,480},{32,0},{64,32},{96,64},{128,96},{160,128},{192,160},{224,1... | collective-permute-start | bytes 1536008 | tf_op jit(solution)/shard_map/ppermute | solution.py:20
  122.5 2.5 %shard_map.64 = f32[320,800]{1,0:T(8,128)S(1)} custom-call(bf16[9,320,320]{2,1,0:T(8,128)(2,1)S(1)} %copy-done.4, bf16[320,800]{1,0:T(8,128)(2,1)S(1)} %convert_element_type.41.g0, bf16[320,800]{1,0:T(8,128)(2,1)S(1)} %collective-permute-done.2.gm1, bf16[320,800]{1,0:T(8,128)(2,1)S(1)} %copy-done.8, bf16[320,800]{1,0:T(8,128)(2,1)S(1)} %copy-done.2, ...), custom_call_target="tpu_custom_call" | custom-call | flops 655360000 | bytes 4403200 | tf_op jit(solution)/shard_map/pallas_call | solution.py:42
  125.0 9.4 %collective-permute-done.7 = bf16[2,96,384]{2,1,0:T(8,128)(2,1)S(1)} collective-permute-done((bf16[2,96,384]{2,1,0:T(8,128)(2,1)S(1)}, bf16[2,96,384]{2,1,0:T(8,128)(2,1)S(1)}, u32[]{:S(2)}, u32[]{:S(2)}) %collective-permute-start.7) | collective-permute-done | bytes 147488 | tf_op jit(solution)/shard_map/ppermute | solution.py:175
  134.5 0.0 collective-permute-done.9
  134.5 0.0 collective-permute-done.10
  134.5 14.2 %collective-permute-start.14 = (bf16[96,384]{1,0:T(8,128)(2,1)S(1)}, bf16[96,384]{1,0:T(8,128)(2,1)S(1)}, u32[]{:S(2)}, u32[]{:S(2)}) collective-permute-start(bf16[96,384]{1,0:T(8,128)(2,1)S(1)} %get-tuple-element.47), channel_id=1, source_target_pairs={{5,199},{12,490},{8,142},{23,213},{26,156},{37,231},{44,10},{40,17... | collective-permute-start | bytes 221192 | tf_op jit(solution)/shard_map/ppermute | solution.py:239
  148.7 1.9 %collective-permute-start.12 = (bf16[96,384]{1,0:T(8,128)(2,1)S(1)}, bf16[96,384]{1,0:T(8,128)(2,1)S(1)}, u32[]{:S(2)}, u32[]{:S(2)}) collective-permute-start(bf16[96,384]{1,0:T(8,128)(2,1)S(1)} %get-tuple-element.47), channel_id=1, source_target_pairs={{6,0},{3,1},{4,2},{1,3},{2,4},{7,5},{0,6},{5,7},{14,200},{11,201},... | collective-permute-start | bytes 221192 | tf_op jit(solution)/shard_map/ppermute | solution.py:239
  150.6 0.0 copy-start.12
  150.6 0.8 collective-permute-start.13
  151.4 1.9 %collective-permute-start.11 = (bf16[96,384]{1,0:T(8,128)(2,1)S(1)}, bf16[96,384]{1,0:T(8,128)(2,1)S(1)}, u32[]{:S(2)}, u32[]{:S(2)}) collective-permute-start(bf16[96,384]{1,0:T(8,128)(2,1)S(1)} %get-tuple-element.46), channel_id=1, source_target_pairs={{0,0},{1,1},{2,2},{3,3},{4,4},{5,5},{6,6},{7,7},{8,200},{9,201},{1... | collective-permute-start | bytes 221192 | tf_op jit(solution)/shard_map/ppermute | solution.py:239
  153.4 0.0 collective-permute-done.16
  153.4 2.5 %convert_add_fusion = f32[320,800]{1,0:T(8,128)} fusion(bf16[320,800]{1,0:T(8,128)(2,1)S(1)} %collective-permute-done.16, bf16[320,800]{1,0:T(8,128)(2,1)} %collective-permute-done.10, f32[320,800]{1,0:T(8,128)S(1)} %shard_map.64, bf16[320,800]{1,0:T(8,128)(2,1)} %collective-permute-done.9), kind=kLoop, calls=%fused_computation | loop fusion | flops 1536000 | bytes 3584000 | tf_op jit(solution)/shard_map/add | solution.py:245
  155.8 0.0 collective-permute-done.14
  155.8 0.0 collective-permute-done.13
  155.9 5.7 %collective-permute-done.12 = bf16[96,384]{1,0:T(8,128)(2,1)S(1)} collective-permute-done((bf16[96,384]{1,0:T(8,128)(2,1)S(1)}, bf16[96,384]{1,0:T(8,128)(2,1)S(1)}, u32[]{:S(2)}, u32[]{:S(2)}) %collective-permute-start.12) | collective-permute-done | bytes 73760 | tf_op jit(solution)/shard_map/ppermute | solution.py:239
  161.6 0.0 collective-permute-done.11
  161.6 0.8 bitcast_add_fusion
  (20 shorter events, 0.1 us)
Async XLA Ops:
  0.6 9.8 %collective-permute-start = (bf16[90,320]{1,0:T(8,128)(2,1)}, bf16[90,320]{1,0:T(8,128)(2,1)S(1)}, u32[]{:S(2)}, u32[]{:S(2)}) collective-permute-start(bf16[90,320]{1,0:T(8,128)(2,1)} %bitcast.10), channel_id=1, source_target_pairs={{0,0},{1,1},{2,2},{3,3},{4,4},{5,5},{6,6},{7,7},{200,8},{201,9},{2... | collective-permute-start | bytes 172808 | tf_op jit(solution)/shard_map/ppermute | solution.py:163
  2.6 7.8 %collective-permute-start.1 = (bf16[90,320]{1,0:T(8,128)(2,1)}, bf16[90,320]{1,0:T(8,128)(2,1)S(1)}, u32[]{:S(2)}, u32[]{:S(2)}) collective-permute-start(bf16[90,320]{1,0:T(8,128)(2,1)} %bitcast.11), channel_id=1, source_target_pairs={{199,7},{490,10},{142,14},{213,21},{156,28},{231,39},{10,42},{174,... | collective-permute-start | bytes 172808 | tf_op jit(solution)/shard_map/ppermute | solution.py:164
  11.7 23.6 %collective-permute-start.2 = (bf16[320,800]{1,0:T(8,128)(2,1)S(1)}, bf16[320,800]{1,0:T(8,128)(2,1)S(1)}, u32[]{:S(2)}, u32[]{:S(2)}) collective-permute-start(bf16[320,800]{1,0:T(8,128)(2,1)S(1)} %convert_element_type.41.g0), channel_id=1, source_target_pairs={{0,32},{32,64},{64,96},{96,128},{128,160},{160,192},{192,224},{224... | collective-permute-start | bytes 1536008 | tf_op jit(solution)/shard_map/ppermute | solution.py:20
  17.2 29.4 %all-to-all-start = ((bf16[4,96,384]{2,1,0:T(8,128)(2,1)}), bf16[4,96,384]{2,1,0:T(8,128)(2,1)S(1)}, u32[]{:S(2)}, u32[]{:S(2)}) async-start(bf16[4,96,384]{2,1,0:T(8,128)(2,1)} %broadcast_in_dim.4), calls=%async_computation | async-start | bytes 589824 | tf_op jit(solution)/shard_map/all_to_all | solution.py:177
  27.3 28.4 %collective-permute-start.3 = (bf16[320,800]{1,0:T(8,128)(2,1)S(1)}, bf16[320,800]{1,0:T(8,128)(2,1)S(1)}, u32[]{:S(2)}, u32[]{:S(2)}) collective-permute-start(bf16[320,800]{1,0:T(8,128)(2,1)S(1)} %convert_element_type.41.g0), channel_id=1, source_target_pairs={{0,128},{32,160},{64,192},{96,224},{128,256},{160,288},{192,320},{... | collective-permute-start | bytes 1536008 | tf_op jit(solution)/shard_map/ppermute | solution.py:20
  30.5 26.9 %collective-permute-start.4 = (bf16[320,800]{1,0:T(8,128)(2,1)S(1)}, bf16[320,800]{1,0:T(8,128)(2,1)S(1)}, u32[]{:S(2)}, u32[]{:S(2)}) collective-permute-start(bf16[320,800]{1,0:T(8,128)(2,1)S(1)} %convert_element_type.41.g0), channel_id=1, source_target_pairs={{0,384},{32,416},{64,448},{96,480},{128,0},{160,32},{192,64},{224,... | collective-permute-start | bytes 1536008 | tf_op jit(solution)/shard_map/ppermute | solution.py:20
  35.3 22.1 %collective-permute-start.5 = (bf16[320,800]{1,0:T(8,128)(2,1)S(1)}, bf16[320,800]{1,0:T(8,128)(2,1)}, u32[]{:S(2)}, u32[]{:S(2)}) collective-permute-start(bf16[320,800]{1,0:T(8,128)(2,1)S(1)} %collective-permute-done.2.gm1), channel_id=1, source_target_pairs={{0,288},{32,320},{64,352},{96,384},{128,416},{160,448},{192,480},{... | collective-permute-start | bytes 1536008 | tf_op jit(solution)/shard_map/ppermute | solution.py:20
  47.8 20.7 %all-to-all-start.1 = ((bf16[4,4,96,384]{3,2,1,0:T(8,128)(2,1)}), bf16[4,4,96,384]{3,2,1,0:T(8,128)(2,1)S(1)}, u32[]{:S(2)}, u32[]{:S(2)}) async-start(bf16[4,4,96,384]{3,2,1,0:T(8,128)(2,1)} %broadcast_in_dim.5), calls=%async_computation.1 | async-start | bytes 2359296 | tf_op jit(solution)/shard_map/all_to_all | solution.py:178
  55.7 6.5 %copy-start.6 = (bf16[320,800]{1,0:T(8,128)(2,1)}, bf16[320,800]{1,0:T(8,128)(2,1)S(1)}, u32[]{:S(2)}) copy-start(bf16[320,800]{1,0:T(8,128)(2,1)S(1)} %collective-permute-done.3.gm4) | copy-start | bytes 1536004
  57.4 4.8 %copy-start = (bf16[320,800]{1,0:T(8,128)(2,1)}, bf16[320,800]{1,0:T(8,128)(2,1)S(1)}, u32[]{:S(2)}) copy-start(bf16[320,800]{1,0:T(8,128)(2,1)S(1)} %collective-permute-done.4.g4) | copy-start | bytes 1536004
  62.2 1.0 copy-start.9
  63.3 1.0 copy-start.10
  68.5 4.9 %collective-permute-start.6 = (bf16[16,96,384]{2,1,0:T(8,128)(2,1)}, bf16[16,96,384]{2,1,0:T(8,128)(2,1)S(1)}, u32[]{:S(2)}, u32[]{:S(2)}) collective-permute-start(bf16[16,96,384]{2,1,0:T(8,128)(2,1)} %copy-done.9), channel_id=1, source_target_pairs={{0,1},{1,0},{2,3},{3,2},{4,5},{5,4},{6,7},{7,6},{8,9},{9,8},{10,11... | collective-permute-start | bytes 3538952 | tf_op jit(solution)/shard_map/ppermute | solution.py:20
  70.4 10.6 %collective-permute-start.8 = (bf16[4,4,96,384]{3,2,1,0:T(8,128)(2,1)S(1)}, bf16[4,4,96,384]{3,2,1,0:T(8,128)(2,1)}, u32[]{:S(2)}, u32[]{:S(2)}) collective-permute-start(bf16[4,4,96,384]{3,2,1,0:T(8,128)(2,1)S(1)} %all-to-all-done.1.mine), channel_id=1, source_target_pairs={{0,1},{1,0},{2,3},{3,2},{4,5},{5,4},{6,7},{7,6},{8,9},{9,8},{10,11... | collective-permute-start | bytes 3538952 | tf_op jit(solution)/shard_map/ppermute | solution.py:20
  73.4 1.3 copy-start.11
  75.0 1.0 copy-start.5
  76.0 32.2 %all-to-all-start.2 = ((bf16[4,4,96,384]{3,2,1,0:T(8,128)(2,1)}), bf16[4,4,96,384]{3,2,1,0:T(8,128)(2,1)S(1)}, u32[]{:S(2)}, u32[]{:S(2)}) async-start(bf16[4,4,96,384]{3,2,1,0:T(8,128)(2,1)} %bitcast.9), calls=%async_computation.2 | async-start | bytes 2359296 | tf_op jit(solution)/shard_map/all_to_all | solution.py:223
  81.0 1.1 copy-start.1
  82.0 16.1 %copy-start.7 = (bf16[320,800]{1,0:T(8,128)(2,1)S(1)}, bf16[320,800]{1,0:T(8,128)(2,1)}, u32[]{:S(2)}) copy-start(bf16[320,800]{1,0:T(8,128)(2,1)} %copy-done.6) | copy-start | bytes 1536004
  85.9 16.4 %copy-start.3 = (bf16[9,320,320]{2,1,0:T(8,128)(2,1)}, bf16[9,320,320]{2,1,0:T(8,128)(2,1)S(1)}, u32[]{:S(2)}) copy-start(bf16[9,320,320]{2,1,0:T(8,128)(2,1)S(1)} %get-tuple-element.38.tiles) | copy-start | bytes 5529604
  85.9 33.4 %collective-permute-start.15 = (bf16[320,800]{1,0:T(8,128)(2,1)}, bf16[320,800]{1,0:T(8,128)(2,1)}, u32[]{:S(2)}, u32[]{:S(2)}) collective-permute-start(bf16[320,800]{1,0:T(8,128)(2,1)} %get-tuple-element.45), channel_id=1, source_target_pairs={{0,224},{32,256},{64,288},{96,320},{128,352},{160,384},{192,416},{... | collective-permute-start | bytes 1536008 | tf_op jit(solution)/shard_map/ppermute | solution.py:20
  102.3 32.1 %collective-permute-start.9 = (bf16[320,800]{1,0:T(8,128)(2,1)}, bf16[320,800]{1,0:T(8,128)(2,1)}, u32[]{:S(2)}, u32[]{:S(2)}) collective-permute-start(bf16[320,800]{1,0:T(8,128)(2,1)} %get-tuple-element.39), channel_id=1, source_target_pairs={{0,128},{32,160},{64,192},{96,224},{128,256},{160,288},{192,320},{... | collective-permute-start | bytes 1536008 | tf_op jit(solution)/shard_map/ppermute | solution.py:20
  104.3 30.2 %collective-permute-start.10 = (bf16[320,800]{1,0:T(8,128)(2,1)}, bf16[320,800]{1,0:T(8,128)(2,1)}, u32[]{:S(2)}, u32[]{:S(2)}) collective-permute-start(bf16[320,800]{1,0:T(8,128)(2,1)} %get-tuple-element.40), channel_id=1, source_target_pairs={{0,384},{32,416},{64,448},{96,480},{128,0},{160,32},{192,64},{224,... | collective-permute-start | bytes 1536008 | tf_op jit(solution)/shard_map/ppermute | solution.py:20
  108.2 14.3 %copy-start.4 = (bf16[9,320,320]{2,1,0:T(8,128)(2,1)S(1)}, bf16[9,320,320]{2,1,0:T(8,128)(2,1)}, u32[]{:S(2)}) copy-start(bf16[9,320,320]{2,1,0:T(8,128)(2,1)} %copy-done.3) | copy-start | bytes 5529604
  108.4 26.0 %collective-permute-start.7 = (bf16[2,96,384]{2,1,0:T(8,128)(2,1)S(1)}, bf16[2,96,384]{2,1,0:T(8,128)(2,1)S(1)}, u32[]{:S(2)}, u32[]{:S(2)}) collective-permute-start(bf16[2,96,384]{2,1,0:T(8,128)(2,1)S(1)} %get-tuple-element.36), channel_id=1, source_target_pairs={{0,2},{1,7},{2,0},{3,5},{4,6},{5,3},{6,4},{7,1},{8,10},{9,15},{10,... | collective-permute-start | bytes 442376 | tf_op jit(solution)/shard_map/ppermute | solution.py:175
  119.3 3.2 %copy-start.2 = (bf16[320,800]{1,0:T(8,128)(2,1)S(1)}, bf16[320,800]{1,0:T(8,128)(2,1)}, u32[]{:S(2)}) copy-start(bf16[320,800]{1,0:T(8,128)(2,1)} %copy-done) | copy-start | bytes 1536004
  119.3 3.2 %copy-start.8 = (bf16[320,800]{1,0:T(8,128)(2,1)S(1)}, bf16[320,800]{1,0:T(8,128)(2,1)}, u32[]{:S(2)}) copy-start(bf16[320,800]{1,0:T(8,128)(2,1)} %copy-done.6) | copy-start | bytes 1536004
  120.5 32.8 %collective-permute-start.16 = (bf16[320,800]{1,0:T(8,128)(2,1)S(1)}, bf16[320,800]{1,0:T(8,128)(2,1)S(1)}, u32[]{:S(2)}, u32[]{:S(2)}) collective-permute-start(bf16[320,800]{1,0:T(8,128)(2,1)S(1)} %add_convert_fusion), channel_id=1, source_target_pairs={{0,480},{32,0},{64,32},{96,64},{128,96},{160,128},{192,160},{224,1... | collective-permute-start | bytes 1536008 | tf_op jit(solution)/shard_map/ppermute | solution.py:20
  134.5 21.3 %collective-permute-start.14 = (bf16[96,384]{1,0:T(8,128)(2,1)S(1)}, bf16[96,384]{1,0:T(8,128)(2,1)S(1)}, u32[]{:S(2)}, u32[]{:S(2)}) collective-permute-start(bf16[96,384]{1,0:T(8,128)(2,1)S(1)} %get-tuple-element.47), channel_id=1, source_target_pairs={{5,199},{12,490},{8,142},{23,213},{26,156},{37,231},{44,10},{40,17... | collective-permute-start | bytes 221192 | tf_op jit(solution)/shard_map/ppermute | solution.py:239
  148.7 12.9 %collective-permute-start.12 = (bf16[96,384]{1,0:T(8,128)(2,1)S(1)}, bf16[96,384]{1,0:T(8,128)(2,1)S(1)}, u32[]{:S(2)}, u32[]{:S(2)}) collective-permute-start(bf16[96,384]{1,0:T(8,128)(2,1)S(1)} %get-tuple-element.47), channel_id=1, source_target_pairs={{6,0},{3,1},{4,2},{1,3},{2,4},{7,5},{0,6},{5,7},{14,200},{11,201},... | collective-permute-start | bytes 221192 | tf_op jit(solution)/shard_map/ppermute | solution.py:239
  150.6 10.9 %copy-start.12 = (f32[320,90]{0,1:T(8,128)S(1)}, f32[320,90]{0,1:T(8,128)}, u32[]{:S(2)}) copy-start(f32[320,90]{0,1:T(8,128)} %param.5) | copy-start | bytes 345604
  150.6 5.2 %collective-permute-start.13 = (bf16[96,384]{1,0:T(8,128)(2,1)S(1)}, bf16[96,384]{1,0:T(8,128)(2,1)S(1)}, u32[]{:S(2)}, u32[]{:S(2)}) collective-permute-start(bf16[96,384]{1,0:T(8,128)(2,1)S(1)} %get-tuple-element.46), channel_id=1, source_target_pairs={{7,199},{10,490},{14,142},{21,213},{28,156},{39,231},{42,10},{46,1... | collective-permute-start | bytes 221192 | tf_op jit(solution)/shard_map/ppermute | solution.py:239
  151.4 10.1 %collective-permute-start.11 = (bf16[96,384]{1,0:T(8,128)(2,1)S(1)}, bf16[96,384]{1,0:T(8,128)(2,1)S(1)}, u32[]{:S(2)}, u32[]{:S(2)}) collective-permute-start(bf16[96,384]{1,0:T(8,128)(2,1)S(1)} %get-tuple-element.46), channel_id=1, source_target_pairs={{0,0},{1,1},{2,2},{3,3},{4,4},{5,5},{6,6},{7,7},{8,200},{9,201},{1... | collective-permute-start | bytes 221192 | tf_op jit(solution)/shard_map/ppermute | solution.py:239
